TPU v7x, 32 devices: a whole 2x2x4 slice. The times are simulated.
32 devices in a mesh: tile: 16 (over z, x, core), row: 2 (over y).
Axes of the slice: x: 2, y: 2, z: 4, core: 2. Of those that a mesh axis runs over, the one named last changes fastest.
Arguments:
- swath_blocks: bfloat16 [16, 2, 768, 2048], P('tile', 'row'), may hold values from -6 to 6
- footprint: int32 [16, 2, 768, 1], P('tile', 'row'), may hold values from 0 to 31; in each aligned block of 768 rows (0 to 767, 768 to 1535, ..., all dimensions but the last counted through in order) at most 36 rows name the same one
- cell_row: int32 [16, 2, 768], P('tile', 'row'), may hold values from 0 to 127
- tile_pick: int32 [16, 2, 768], P('tile', 'row'), may hold values from 0 to 3
- sensor: int32 [16, 2, 768], P('tile', 'row'), may hold values from 0 to 1
- bandpass_offset: float32 [2, 8, 8], replicated, may hold values from -0.4 to 0.4
- weight_tiles: bfloat16 [4, 256, 256], replicated, may hold values from -0.375 to 0.375
- lookup_table: float32 [8, 33], replicated, may hold values from 0.5 to 2
- lookup_bin: int32 [16, 256, 256], P('tile', 'row'), may hold values from 0 to 31
- lookup_frac: float32 [16, 256, 256], P('tile', 'row'), may hold values from 0 to 1
- brdf_params: float32 [8, 3], replicated, may hold values from 0.05 to 1
- vol_kernel: float32 [16, 256, 256], P('tile', 'row'), may hold values from 0.1 to 2
- geo_kernel: float32 [16, 256, 256], P('tile', 'row'), may hold values from 0.1 to 2
- clear_mask: int32 [16, 256, 256], P('tile', 'row'), may hold values 0 or 1
Outputs:
- nbar: bfloat16 [16, 256, 2048], P('tile', 'row')
Inputs may be any that keep to these rules, and one draw needn't show every extreme that they name: `footprint`: at most 36 of the blocks of one device name one destination, and in every draw some destination is named by exactly 36 of them.
All inputs are finite; a program needn't handle non-finite values. No bound on the sum of `clear_mask` on one device may be relied on, other than what follows from the above.
Results may differ from a plain program's by a relative error of at most 0.0057.
Values may be sent and summed in bfloat16 or wider, within the bound.
No kernel may reach another device: no remote copies, remote signals or barrier semaphores. Data moves between devices by JAX's collectives and lax.ppermute only.
A program may use at most 64 MiB of HBM per device.

v0:
```python
import jax
import jax.numpy as jnp
from jax import lax
from jax.sharding import PartitionSpec as P

nadir_volume = 0.3
nadir_geometric = 0.6


def with_halo(block, sides, width):
    for axis, dim in sides:
        count = lax.axis_size(axis)
        forward = [(i, i + 1) for i in range(count - 1)]
        backward = [(target, source) for source, target in forward]
        low = lax.ppermute(
            lax.slice_in_dim(block, block.shape[dim] - width, None, axis=dim), axis, forward
        )
        high = lax.ppermute(lax.slice_in_dim(block, 0, width, axis=dim), axis, backward)
        block = jnp.concatenate([low, block, high], axis=dim)
    return block


def resample_rows(rows_in, tag_codes, mixing, stacked_weights, band_count, tile_count):
    slot_count = rows_in.shape[0]
    row_width = rows_in.shape[1]
    pixels = row_width // band_count
    group_size = slot_count // 8

    def resample_group(operands):
        payload, codes_here = operands
        sensor_g = codes_here % 2
        tile_g = codes_here // 2 % tile_count
        chosen_mix = jnp.where(sensor_g[:, None, None] == 1, mixing[1][None], mixing[0][None])
        banded = jnp.einsum(
            "ons,osi->oni",
            chosen_mix,
            payload.reshape(group_size, band_count, pixels).astype(jnp.float32),
            precision=lax.Precision.HIGHEST,
        ).astype(jnp.bfloat16)
        chosen = tile_g[:, None] == jnp.arange(tile_count, dtype=jnp.int32)[None, :]
        spread = jnp.where(
            chosen[:, None, :, None], banded[:, :, None, :], jnp.zeros((), jnp.bfloat16)
        )
        result = jnp.dot(
            spread.reshape(group_size * band_count, tile_count * pixels),
            stacked_weights,
            preferred_element_type=jnp.float32,
        )
        return result.astype(jnp.bfloat16).reshape(group_size, row_width)

    grouped = lax.map(
        resample_group,
        (rows_in.reshape(8, group_size, row_width), tag_codes.reshape(8, group_size)),
    )
    return grouped.reshape(slot_count, row_width)


def on_device(
    swath_blocks,
    footprint,
    cell_row,
    tile_pick,
    sensor,
    bandpass_offset,
    weight_tiles,
    lookup_table,
    lookup_bin,
    lookup_frac,
    brdf_params,
    vol_kernel,
    geo_kernel,
    clear_mask,
):
    tile_devices = lax.axis_size("tile")
    row_devices = lax.axis_size("row")
    destinations = tile_devices * row_devices
    block_count = swath_blocks.shape[2]
    row_width = swath_blocks.shape[3]
    band_count = bandpass_offset.shape[1]
    pixels = row_width // band_count
    tile_count = weight_tiles.shape[0]
    grid_rows = lookup_bin.shape[1]
    bin_count = lookup_table.shape[1] - 1
    capacity = max(2, 3 * block_count // (2 * destinations))
    mixing = jnp.eye(band_count, dtype=jnp.float32)[None, :, :] + bandpass_offset
    stacked_weights = weight_tiles.reshape(tile_count * pixels, pixels)
    blocks = swath_blocks.reshape(block_count, row_width)
    target = footprint.reshape(block_count)
    tag_codes = (
        cell_row.reshape(block_count) * tile_count + tile_pick.reshape(block_count)
    ) * 2 + sensor.reshape(block_count)
    order_index = jnp.arange(block_count, dtype=jnp.int32)
    same_dest = target[:, None] == target[None, :]
    earlier = order_index[:, None] > order_index[None, :]
    slot_rank = jnp.sum(jnp.logical_and(same_dest, earlier).astype(jnp.int32), axis=1)
    position = target * capacity + slot_rank
    buffer = jnp.zeros((destinations * capacity, row_width), jnp.bfloat16).at[position].set(blocks)
    buffer = buffer.reshape(tile_devices, row_devices, capacity, row_width)
    tag_buffer = jnp.full((destinations * capacity,), -1, jnp.int32).at[position].set(tag_codes)
    tag_buffer = tag_buffer.reshape(tile_devices, row_devices, capacity)
    received, arrived_tags = (
        lax.all_to_all(
            lax.all_to_all(buffer, "tile", split_axis=0, concat_axis=0, tiled=True),
            "row",
            split_axis=1,
            concat_axis=1,
            tiled=True,
        ),
        lax.all_to_all(
            lax.all_to_all(tag_buffer, "tile", split_axis=0, concat_axis=0, tiled=True),
            "row",
            split_axis=1,
            concat_axis=1,
            tiled=True,
        ),
    )
    received_rows = received.reshape(destinations * capacity, row_width)
    clipped = jnp.maximum(arrived_tags.reshape(destinations * capacity), 0)
    arrived_rows = resample_rows(
        received_rows, clipped, mixing, stacked_weights, band_count, tile_count
    )
    target_row = clipped // (2 * tile_count)
    accum_grid = (
        jnp.zeros((grid_rows, row_width), jnp.float32)
        .at[target_row]
        .add(arrived_rows.astype(jnp.float32))
    )
    padded = with_halo(accum_grid, (("row", 0),), 1)
    smoothed = 0.25 * padded[:-2] + 0.5 * padded[1:-1] + 0.25 * padded[2:]
    smoothed = smoothed.reshape(grid_rows, band_count, pixels)
    bin_index = lookup_bin[0]
    fraction = lookup_frac[0][:, None, :]
    onehot = (
        bin_index[:, :, None] == jnp.arange(bin_count, dtype=jnp.int32)[None, None, :]
    ).astype(jnp.float32)
    lower_value = jnp.einsum(
        "rpn,bn->rbp", onehot, lookup_table[:, :-1], precision=lax.Precision.HIGHEST
    )
    upper_value = jnp.einsum(
        "rpn,bn->rbp", onehot, lookup_table[:, 1:], precision=lax.Precision.HIGHEST
    )
    table_value = lower_value * (1.0 - fraction) + upper_value * fraction
    isotropic = brdf_params[:, 0][None, :, None]
    volume = brdf_params[:, 1][None, :, None]
    geometric = brdf_params[:, 2][None, :, None]
    numerator = isotropic + volume * nadir_volume + geometric * nadir_geometric
    denominator = (
        isotropic + volume * vol_kernel[0][:, None, :] + geometric * geo_kernel[0][:, None, :]
    )
    cfactor = numerator / denominator
    result = smoothed * table_value * cfactor * clear_mask[0][:, None, :].astype(jnp.float32)
    return result.reshape(1, grid_rows, row_width).astype(jnp.bfloat16)


def solution(mesh):
    in_specs = (
        P("tile", "row", None, None),
        P("tile", "row", None, None),
        P("tile", "row", None),
        P("tile", "row", None),
        P("tile", "row", None),
        P(),
        P(),
        P(),
        P("tile", "row", None),
        P("tile", "row", None),
        P(),
        P("tile", "row", None),
        P("tile", "row", None),
        P("tile", "row", None),
    )
    out_specs = P("tile", "row", None)
    return jax.shard_map(
        on_device, mesh=mesh, in_specs=in_specs, out_specs=out_specs, check_vma=False
    )
```

profile of v0, /device:TPU:10, one launch (start us, length us, event | category | flops | bytes accessed | tf_op | source)
XLA Modules:
  0.0 350.6 jit_solution(6626633104236595492)
XLA Ops:
  0.0 0.8 reduce
  2.7 3.4 scatter_custom_fusion
  6.8 6.2 %all-to-all-start = ((s32[16,2,36]{2,1,0:T(2,128)}), s32[16,2,36]{2,1,0:T(2,128)S(1)}, u32[]{:S(2)}, u32[]{:S(2)}) async-start(s32[16,2,36]{2,1,0:T(2,128)} %reshape.289), calls=%async_computation | async-start | bytes 32768 | tf_op jit(solution)/shard_map/all_to_all | solution.py:110
  13.0 9.7 %scatter_custom_fusion.1 = bf16[1152,2048]{1,0:T(8,128)(2,1)} fusion(s32[768]{0:T(1024)S(1)} %fusion.38, bf16[1,1,768,2048]{3,2,1,0:T(8,128)(2,1)S(1)} %copy-done, bf16[]{:T(256)} %constant.120.clone.1), kind=kCustom, calls=%fused_computation.33 | custom fusion | bytes 7864322 | tf_op jit(solution)/shard_map/scatter | solution.py:97
  22.7 7.2 %reshape.291 = bf16[16,2,36,2048]{3,2,1,0:T(8,128)(2,1)} reshape(bf16[1152,2048]{1,0:T(8,128)(2,1)} %scatter_custom_fusion.1) | data formatting | bytes 9437184 | tf_op jit(solution)/shard_map/reshape | solution.py:98
  29.9 9.6 %copy.31 = bf16[16,2,36,2048]{3,1,2,0:T(2,128)(2,1)} copy(bf16[16,2,36,2048]{3,2,1,0:T(8,128)(2,1)} %reshape.291) | data formatting | bytes 9437184 | tf_op jit(solution)/shard_map/reshape | solution.py:98
  39.6 6.0 %all-to-all-start.2 = ((bf16[16,2,36,2048]{3,1,2,0:T(2,128)(2,1)}), bf16[16,2,36,2048]{3,1,2,0:T(2,128)(2,1)}, u32[]{:S(2)}, u32[]{:S(2)}) async-start(bf16[16,2,36,2048]{3,1,2,0:T(2,128)(2,1)} %copy.31), calls=%async_computation.2 | async-start | bytes 9437184 | tf_op jit(solution)/shard_map/all_to_all | solution.py:103
  46.3 102.9 %all-to-all-done.2 = bf16[16,2,36,2048]{3,1,2,0:T(2,128)(2,1)} async-done(((bf16[16,2,36,2048]{3,1,2,0:T(2,128)(2,1)}), bf16[16,2,36,2048]{3,1,2,0:T(2,128)(2,1)}, u32[]{:S(2)}, u32[]{:S(2)}) %all-to-all-start.2) | async-done | bytes 4718624 | tf_op jit(solution)/shard_map/all_to_all | solution.py:103
  149.1 3.2 all-to-all-start.1
  152.4 7.0 %copy.32 = bf16[16,2,36,2048]{3,0,2,1:T(8,128)(2,1)} copy(bf16[16,2,36,2048]{3,1,2,0:T(2,128)(2,1)} %all-to-all-done.2) | data formatting | bytes 9437184 | tf_op jit(solution)/shard_map/all_to_all | solution.py:103
  159.4 6.0 %all-to-all-start.3 = ((bf16[16,2,36,2048]{3,0,2,1:T(8,128)(2,1)}), bf16[16,2,36,2048]{3,0,2,1:T(8,128)(2,1)}, u32[]{:S(2)}, u32[]{:S(2)}) async-start(bf16[16,2,36,2048]{3,0,2,1:T(8,128)(2,1)} %copy.32), calls=%async_computation.3 | async-start | bytes 9437184 | tf_op jit(solution)/shard_map/all_to_all | solution.py:102
  168.0 3.0 fusion.19
  172.6 46.5 %all-to-all-done.3 = bf16[16,2,36,2048]{3,0,2,1:T(8,128)(2,1)} async-done(((bf16[16,2,36,2048]{3,0,2,1:T(8,128)(2,1)}), bf16[16,2,36,2048]{3,0,2,1:T(8,128)(2,1)}, u32[]{:S(2)}, u32[]{:S(2)}) %all-to-all-start.3) | async-done | bytes 4718624 | tf_op jit(solution)/shard_map/all_to_all | solution.py:102
  219.1 7.3 %copy.33 = bf16[16,2,36,2048]{3,2,1,0:T(8,128)(2,1)} copy(bf16[16,2,36,2048]{3,0,2,1:T(8,128)(2,1)} %all-to-all-done.3) | data formatting | bytes 9437184 | tf_op jit(solution)/shard_map/all_to_all | solution.py:102
  226.4 7.2 %reshape_reshape.3 = bf16[8,144,2048]{2,1,0:T(8,128)(2,1)} reshape(bf16[16,2,36,2048]{3,2,1,0:T(8,128)(2,1)} %copy.33) | data formatting | bytes 9437184 | tf_op jit(solution)/shard_map/reshape;reshape | solution.py:53
  233.6 77.6 %while.13 = (s32[]{:T(128)}, bf16[8,144,2048]{2,1,0:T(8,128)(2,1)}, s32[8,144]{1,0:T(8,128)S(1)}, f32[2,8,8]{2,1,0:T(8,128)S(1)}, bf16[8,144,2048]{2,1,0:T(8,128)(2,1)}, /*index=5*/bf16[1024,256]{1,0:T(8,128)(2,1)}, s32[]{:T(128)}) while((s32[]{:T(128)}, bf16[8,144,2048]{2,1,0:T(8,128)(2,1)}, s32[8,144]{1,0:T(8,128)S(1)}, ...), condition=%wide.region_4.5_spmd, body=%wide.region_3.4_spmd.sunk | while | flops 634076032 | bytes 19143568 | solution.py:51
  233.6 1.1 constant_dynamic-slice_fusion.5
  235.7 1.4 select_bitcast_fusion.2
  237.7 1.6 convolution_convert_fusion.5
  239.3 2.1 broadcast_in_dim.140
  241.4 1.9 constant_dynamic-update-slice_fusion.2
  243.3 1.1 constant_dynamic-slice_fusion.5
  245.4 1.4 select_bitcast_fusion.2
  247.4 1.6 convolution_convert_fusion.5
  249.0 2.1 broadcast_in_dim.140
  251.1 2.0 constant_dynamic-update-slice_fusion.2
  253.0 1.1 constant_dynamic-slice_fusion.5
  255.1 1.4 select_bitcast_fusion.2
  257.1 1.6 convolution_convert_fusion.5
  258.7 2.1 broadcast_in_dim.140
  260.8 1.9 constant_dynamic-update-slice_fusion.2
  262.7 1.1 constant_dynamic-slice_fusion.5
  264.8 1.4 select_bitcast_fusion.2
  266.8 1.6 convolution_convert_fusion.5
  268.4 2.1 broadcast_in_dim.140
  270.5 1.9 constant_dynamic-update-slice_fusion.2
  272.4 1.1 constant_dynamic-slice_fusion.5
  274.5 1.4 select_bitcast_fusion.2
  276.5 1.6 convolution_convert_fusion.5
  278.1 2.1 broadcast_in_dim.140
  280.2 1.9 constant_dynamic-update-slice_fusion.2
  282.1 1.1 constant_dynamic-slice_fusion.5
  284.2 1.4 select_bitcast_fusion.2
  286.2 1.6 convolution_convert_fusion.5
  287.8 2.1 broadcast_in_dim.140
  289.9 2.0 constant_dynamic-update-slice_fusion.2
  291.9 1.1 constant_dynamic-slice_fusion.5
  294.0 1.4 select_bitcast_fusion.2
  295.9 1.6 convolution_convert_fusion.5
  297.5 2.1 broadcast_in_dim.140
  299.6 1.9 constant_dynamic-update-slice_fusion.2
  301.6 1.1 constant_dynamic-slice_fusion.5
  303.7 1.4 select_bitcast_fusion.2
  305.6 1.6 convolution_convert_fusion.5
  307.2 2.1 broadcast_in_dim.140
  309.3 1.9 constant_dynamic-update-slice_fusion.2
  311.2 22.2 %scatter_custom_fusion.2 = f32[128,2048]{1,0:T(8,128)} fusion(s32[1152]{0:T(1024)S(1)} %fusion.30, bf16[1152,2048]{1,0:T(8,128)(2,1)} %bitcast.89, f32[]{:T(128)} %constant.109.clone.1), kind=kCustom, calls=%fused_computation.28 | custom fusion | flops 4718592 | bytes 5767172 | tf_op jit(solution)/shard_map/scatter-add | solution.py:126
  333.4 0.9 fusion.39
  334.3 2.2 collective-permute-start
  336.5 1.6 collective-permute-start.1
  338.9 3.2 collective-permute-done.1
  342.0 2.4 fusion.25
  344.8 3.7 %fusion.23 = bf16[128,8,256]{2,1,0:T(8,128)(2,1)} fusion(f32[128,8,256]{2,1,0:T(8,128)S(1)} %bitcast.91, f32[128,256,8]{1,2,0:T(8,128)} %fusion.19, s32[128,256]{1,0:T(8,128)S(1)} %bitcast.94, f32[128,256]{1,0:T(8,128)S(1)} %copy-done.5, f32[128,256]{1,0:T(8,128)} %bitcast.99, f32[8]{0:T(128)} %get-tuple-element.132, f32[128,256]{1,0:T(8,128)} %bitcast.100, ...), kind=kOutput, calls=%fused_computation.48 | convolution fusion | flops 104595456 | bytes 3277984 | tf_op jit(solution)/shard_map/rpn,bn->rbp/dot_general | solution.py:136
  348.5 2.1 convert_element_type.64
  (123 shorter events, 20.5 us)
Async XLA Ops:
  0.0 13.0 %copy-start = (bf16[1,1,768,2048]{3,2,1,0:T(8,128)(2,1)S(1)}, bf16[1,1,768,2048]{3,2,1,0:T(8,128)(2,1)}, u32[]{:S(2)}) copy-start(bf16[1,1,768,2048]{3,2,1,0:T(8,128)(2,1)} %param.16) | copy-start | bytes 9437188
  6.8 32.8 %all-to-all-start = ((s32[16,2,36]{2,1,0:T(2,128)}), s32[16,2,36]{2,1,0:T(2,128)S(1)}, u32[]{:S(2)}, u32[]{:S(2)}) async-start(s32[16,2,36]{2,1,0:T(2,128)} %reshape.289), calls=%async_computation | async-start | bytes 32768 | tf_op jit(solution)/shard_map/all_to_all | solution.py:110
  39.6 109.6 %all-to-all-start.2 = ((bf16[16,2,36,2048]{3,1,2,0:T(2,128)(2,1)}), bf16[16,2,36,2048]{3,1,2,0:T(2,128)(2,1)}, u32[]{:S(2)}, u32[]{:S(2)}) async-start(bf16[16,2,36,2048]{3,1,2,0:T(2,128)(2,1)} %copy.31), calls=%async_computation.2 | async-start | bytes 9437184 | tf_op jit(solution)/shard_map/all_to_all | solution.py:103
  149.1 10.3 %all-to-all-start.1 = ((s32[2,1,576]{2,1,0:T(1,128)}), s32[2,1,576]{2,1,0:T(1,128)S(1)}, u32[]{:S(2)}, u32[]{:S(2)}) async-start(s32[2,1,576]{2,1,0:T(1,128)} %reshape.331), calls=%async_computation.1 | async-start | bytes 10240 | tf_op jit(solution)/shard_map/all_to_all | solution.py:109
  159.4 6.0 %copy-start.6 = (f32[8,3]{0,1:T(4,128)S(1)}, f32[8,3]{0,1:T(4,128)}, u32[]{:S(2)}) copy-start(f32[8,3]{0,1:T(4,128)} %param.26) | copy-start | bytes 292
  159.4 7.3 %copy-start.1 = (f32[1,128,256]{2,1,0:T(8,128)S(1)}, f32[1,128,256]{2,1,0:T(8,128)}, u32[]{:S(2)}) copy-start(f32[1,128,256]{2,1,0:T(8,128)} %param.25) | copy-start | bytes 393220
  159.4 7.9 %copy-start.3 = (s32[1,128,256]{2,1,0:T(8,128)S(1)}, s32[1,128,256]{2,1,0:T(8,128)}, u32[]{:S(2)}) copy-start(s32[1,128,256]{2,1,0:T(8,128)} %param.29) | copy-start | bytes 393220
  159.4 8.6 %copy-start.2 = (s32[1,128,256]{2,1,0:T(8,128)S(1)}, s32[1,128,256]{2,1,0:T(8,128)}, u32[]{:S(2)}) copy-start(s32[1,128,256]{2,1,0:T(8,128)} %param.24) | copy-start | bytes 393220
  159.4 59.7 %all-to-all-start.3 = ((bf16[16,2,36,2048]{3,0,2,1:T(8,128)(2,1)}), bf16[16,2,36,2048]{3,0,2,1:T(8,128)(2,1)}, u32[]{:S(2)}, u32[]{:S(2)}) async-start(bf16[16,2,36,2048]{3,0,2,1:T(8,128)(2,1)} %copy.32), calls=%async_computation.3 | async-start | bytes 9437184 | tf_op jit(solution)/shard_map/all_to_all | solution.py:102
  234.9 2.8 copy-start.7
  244.6 2.8 copy-start.7
  254.3 2.8 copy-start.7
  264.0 2.8 copy-start.7
  273.7 2.8 copy-start.7
  283.4 2.8 copy-start.7
  293.1 2.8 copy-start.7
  302.8 2.8 copy-start.7
  311.2 33.5 %copy-start.4 = (f32[128,256]{1,0:T(8,128)S(1)}, f32[128,256]{1,0:T(8,128)}, u32[]{:S(2)}) copy-start(f32[128,256]{1,0:T(8,128)} %broadcast_subtract_fusion) | copy-start | bytes 393220
  311.2 33.5 %copy-start.5 = (f32[128,256]{1,0:T(8,128)S(1)}, f32[128,256]{1,0:T(8,128)}, u32[]{:S(2)}) copy-start(f32[128,256]{1,0:T(8,128)} %convert_bitcast_fusion) | copy-start | bytes 393220
  334.3 4.6 %collective-permute-start = (f32[1,2048]{1,0:T(1,128)S(1)}, f32[1,2048]{1,0:T(1,128)S(1)}, u32[]{:S(2)}, u32[]{:S(2)}) collective-permute-start(f32[1,2048]{1,0:T(1,128)S(1)} %get-tuple-element.127), channel_id=1, source_target_pairs={{0,1},{2,3},{4,5},{6,7},{8,9},{10,11},{12,13},{14,15},{16,17},{18,... | collective-permute-start | bytes 24584 | tf_op jit(solution)/shard_map/ppermute | solution.py:15
  336.5 5.5 %collective-permute-start.1 = (f32[1,2048]{1,0:T(1,128)S(1)}, f32[1,2048]{1,0:T(1,128)S(1)}, u32[]{:S(2)}, u32[]{:S(2)}) collective-permute-start(f32[1,2048]{1,0:T(1,128)S(1)} %get-tuple-element.128), channel_id=1, source_target_pairs={{1,0},{3,2},{5,4},{7,6},{9,8},{11,10},{13,12},{15,14},{17,16},{19,... | collective-permute-start | bytes 24584 | tf_op jit(solution)/shard_map/ppermute | solution.py:18
where the time goes:
time: 353 us; the launch traced here: 351 us
  waiting for transfers between devices  153 us (43%)
  local copies, waits for them, and re-layouts  104 us (29%)
  other arithmetic  42.6 us (12%)
  starting transfers between devices  25.2 us (7%)
  matrix products  25.1 us (7%)
    all_to_all x1, waiting for transfers between devices, on_device(): lax.all_to_all(buffer, 'tile', split_axis=0, concat_axis=0, tiled=True)  103 us
    all_to_all x1, waiting for transfers between devices, on_device(): lax.all_to_all(lax.all_to_all(buffer, 'tile', split_axis=0, concat_axis=0...  46.5 us
    scatter-add x1, other arithmetic, on_device(): accum_grid = jnp.zeros((grid_rows, row_width), jnp.float32).at[target_row...  22.2 us
    reshape x2, local copies, waits for them, and re-layouts, on_device(): buffer = buffer.reshape(tile_devices, row_devices, capacity, row_width)  16.8 us
    broadcast_in_dim x8, local copies, waits for them, and re-layouts, resample_rows(): lax.map(resample_group, (rows_in.reshape(8, group_size, row_width), tag_c...  16.8 us
    dynamic_update_slice x8, local copies, waits for them, and re-layouts, resample_rows(): lax.map(resample_group, (rows_in.reshape(8, group_size, row_width), tag_c...  15.5 us
    dot_general x8, matrix products, resample_group(): jnp.dot(spread.reshape(group_size * band_count, tile_count * pixels), sta...  12.7 us
    while x8, other arithmetic  11.1 us
  transfers between devices with their start and end apart: 6, of which 3 were waited for; matrix products, arithmetic and copies ran while one was open for 12% of the time, Pallas kernels for 0%

commit v1 on v0

v1 whole, which is shorter than its diff:
```python
import functools

import jax
import jax.numpy as jnp
from jax import lax
from jax.experimental import pallas as pl
from jax.experimental.pallas import tpu as pltpu
from jax.sharding import PartitionSpec as P

nadir_volume = 0.3
nadir_geometric = 0.6

GROUP = 32
CHUNKS = ((0, 3), (3, 6), (6, 8))
VMEM_LIMIT = 40 * 1024 * 1024


def params():
    return pltpu.CompilerParams(vmem_limit_bytes=VMEM_LIMIT)


def dot(a, b):
    return jnp.dot(a, b, preferred_element_type=jnp.float32)


def resample_kernel(bands, pixels, x_ref, sensor_ref, pick_ref, mix_ref, weights_ref, out_ref):
    tiles = weights_ref.shape[0]
    groups = x_ref.shape[0] // GROUP

    def one_group(g, carry):
        rows = pl.ds(pl.multiple_of(g * GROUP, GROUP), GROUP)
        block = x_ref[rows, :]
        stacked = jnp.concatenate(
            [block[:, c * pixels : (c + 1) * pixels] for c in range(bands)], axis=0
        )
        second = sensor_ref[g] == 1
        high = jnp.where(second, mix_ref[1, 0], mix_ref[0, 0])
        low = jnp.where(second, mix_ref[1, 1], mix_ref[0, 1])
        banded = (
            dot(high.astype(jnp.bfloat16), stacked) + dot(low.astype(jnp.bfloat16), stacked)
        )
        pick = jnp.concatenate([pick_ref[rows, :]] * bands, axis=0)
        total = jnp.zeros((bands * GROUP, pixels), jnp.float32)
        for t in range(tiles):
            masked = jnp.where(pick == t, banded, 0.0).astype(jnp.bfloat16)
            total = total + dot(masked, weights_ref[t])
        result = total.astype(jnp.bfloat16)
        for b in range(bands):
            out_ref[rows, b * pixels : (b + 1) * pixels] = result[b * GROUP : (b + 1) * GROUP]
        return carry

    lax.fori_loop(0, groups, one_group, 0)


def pack_kernel(position_ref, rows_ref, own_ref, other_ref):
    peers, slots, columns = own_ref.shape
    blocks = rows_ref.shape[0]
    position = position_ref[...]
    for half, ref in ((0, own_ref), (1, other_ref)):
        for k in range(peers):
            first = (half * peers + k) * slots
            ids = lax.broadcasted_iota(jnp.int32, (slots, blocks), 0) + first
            onehot = (ids == position).astype(jnp.float32).astype(jnp.bfloat16)
            ref[k] = dot(onehot, rows_ref[...]).astype(jnp.bfloat16)


def merge_kernel(count, cells, *refs):
    tags, rows = refs[:count], refs[count : 2 * count]
    own_ref, send_ref = refs[2 * count :]
    depth = send_ref.shape[0] + 1
    for d in range(depth):
        total = None
        for tag_ref, row_ref in zip(tags, rows):
            slots = row_ref.shape[0]
            ids = lax.broadcasted_iota(jnp.int32, (cells, slots), 0) + d * cells
            onehot = (ids == tag_ref[...]).astype(jnp.float32).astype(jnp.bfloat16)
            part = dot(onehot, row_ref[...])
            total = part if total is None else total + part
        if d == 0:
            own_ref[...] = total
        else:
            send_ref[d - 1] = total.astype(jnp.bfloat16)


def factor_kernel(bands, pixels, bin_ref, frac_ref, vol_ref, geo_ref, mask_ref, table_ref, brdf_ref, out_ref):
    rows = 8

    def some_rows(i, carry):
        here = pl.ds(pl.multiple_of(i * rows, rows), rows)
        for p in range(0, pixels, 128):
            at = (here, slice(p, p + 128))
            index, fraction = bin_ref[at], frac_ref[at]
            vol, geo = vol_ref[at], geo_ref[at]
            mask = mask_ref[at].astype(jnp.float32)
            for b in range(bands):
                line = jnp.broadcast_to(table_ref[b : b + 1, :], (rows, 128))
                lower = jnp.take_along_axis(line, index, axis=1)
                upper = jnp.take_along_axis(line, index + 1, axis=1)
                table_value = lower * (1.0 - fraction) + upper * fraction
                w0, w1, w2 = brdf_ref[b, 0], brdf_ref[b, 1], brdf_ref[b, 2]
                numerator = w0 + w1 * nadir_volume + w2 * nadir_geometric
                cfactor = numerator / (w0 + w1 * vol + w2 * geo)
                first = b * pixels + p
                out_ref[here, first : first + 128] = table_value * cfactor * mask
        return carry

    lax.fori_loop(0, out_ref.shape[0] // rows, some_rows, 0)


def finish_kernel(count, *refs):
    own_ref, parts = refs[0], refs[1 : 1 + count]
    low_ref, high_ref, factor_ref, out_ref = refs[1 + count :]
    grid = own_ref[...]
    for part in parts:
        grid = grid + part[...].astype(jnp.float32)
    before = jnp.concatenate([low_ref[...], grid[:-1]], axis=0)
    after = jnp.concatenate([grid[1:], high_ref[...]], axis=0)
    smoothed = 0.25 * before + 0.5 * grid + 0.25 * after
    out_ref[...] = (smoothed * factor_ref[...]).astype(jnp.bfloat16)


def on_device(
    swath_blocks,
    footprint,
    cell_row,
    tile_pick,
    sensor,
    bandpass_offset,
    weight_tiles,
    lookup_table,
    lookup_bin,
    lookup_frac,
    brdf_params,
    vol_kernel,
    geo_kernel,
    clear_mask,
):
    tiles, rows = lax.axis_size("tile"), lax.axis_size("row")
    devices = tiles * rows
    blocks, width = swath_blocks.shape[2], swath_blocks.shape[3]
    bands = bandpass_offset.shape[1]
    pixels = width // bands
    cells = lookup_bin.shape[1]
    capacity = max(2, 3 * blocks // (2 * devices))
    depth = tiles // 4
    peers = 2 * rows
    slots = depth * capacity
    bits = dict(z=4 * rows, x=2 * rows, core=rows, y=1)

    def exchange(array, flip):
        pairs = [(i, i ^ flip) for i in range(devices)]
        return lax.ppermute(array, ("tile", "row"), pairs)

    def chip_flip(k):
        return (k // rows) * bits["x"] + k % rows

    me = lax.axis_index("tile") * rows + lax.axis_index("row")
    relative = footprint.reshape(blocks) ^ me
    rel_z = relative // bits["z"]
    rel_x = relative // bits["x"] % 2
    rel_core = relative // bits["core"] % 2
    rel_y = relative % rows
    group = (rel_core * 2 + rel_x) * rows + rel_y
    key = rel_z * cells + cell_row.reshape(blocks)
    order = jnp.arange(blocks, dtype=jnp.int32)
    ahead = jnp.logical_and(group[:, None] == group[None, :], order[:, None] < order[None, :])
    position = group * slots + jnp.sum(ahead.astype(jnp.int32), axis=0)
    slot_ids = jnp.arange(2 * peers * slots, dtype=jnp.int32)
    tags = (
        jnp.sum(jnp.where(slot_ids[None, :] == position[:, None], key[:, None] + 1, 0), axis=0) - 1
    ).reshape(2, peers, slots)

    mixing = jnp.eye(bands, dtype=jnp.float32)[None] + bandpass_offset
    spread = (
        mixing[:, :, None, :, None] * jnp.eye(GROUP, dtype=jnp.float32)[None, None, :, None, :]
    ).reshape(2, bands * GROUP, bands * GROUP)
    high = lax.reduce_precision(spread, 8, 7)
    mix = jnp.stack([high, spread - high], axis=1)
    sensor_lanes = jnp.tile(sensor.reshape(blocks // GROUP, 1, GROUP), (1, 1, bands))

    resampled = pl.pallas_call(
        functools.partial(resample_kernel, bands, pixels),
        out_shape=jax.ShapeDtypeStruct((blocks, width), jnp.bfloat16),
        compiler_params=params(),
        name="resample",
    )(
        swath_blocks.reshape(blocks, width),
        sensor_lanes,
        tile_pick.reshape(blocks, 1),
        mix,
        weight_tiles,
    )

    other_tags = exchange(tags[1], bits["core"])
    tag_lists = []
    for k in range(peers):
        both = jnp.concatenate([tags[0, k], other_tags[k]])[None, :]
        tag_lists.append(both if k == 0 else exchange(both, chip_flip(k)))

    table = jnp.pad(lookup_table, ((0, 0), (0, 128 - lookup_table.shape[1])))
    vmem = pl.BlockSpec(memory_space=pltpu.VMEM)
    factor = pl.pallas_call(
        functools.partial(factor_kernel, bands, pixels),
        out_shape=jax.ShapeDtypeStruct((cells, width), jnp.float32),
        in_specs=[vmem] * 6 + [pl.BlockSpec(memory_space=pltpu.SMEM)],
        out_specs=vmem,
        compiler_params=params(),
        name="factor",
    )(lookup_bin[0], lookup_frac[0], vol_kernel[0], geo_kernel[0], clear_mask[0], table, brdf_params)

    results = []
    for begin, end in CHUNKS:
        first, last = begin * pixels, end * pixels
        columns = last - first
        own, other = pl.pallas_call(
            pack_kernel,
            out_shape=[jax.ShapeDtypeStruct((peers, slots, columns), jnp.bfloat16)] * 2,
            compiler_params=params(),
            name="pack",
        )(position.reshape(1, blocks), resampled[:, first:last])
        arrived = exchange(other, bits["core"])
        row_lists = []
        for k in range(peers):
            both = jnp.concatenate([own[k], arrived[k]], axis=0)
            row_lists.append(both if k == 0 else exchange(both, chip_flip(k)))
        mine, sends = pl.pallas_call(
            functools.partial(merge_kernel, peers, cells),
            out_shape=[
                jax.ShapeDtypeStruct((cells, columns), jnp.float32),
                jax.ShapeDtypeStruct((depth - 1, cells, columns), jnp.bfloat16),
            ],
            compiler_params=params(),
            name="merge",
        )(*tag_lists, *row_lists)
        parts = [exchange(sends[k - 1], k * bits["z"]) for k in range(1, depth)]
        first_row, last_row = mine[:1], mine[-1:]
        for part in parts:
            first_row = first_row + part[:1].astype(jnp.float32)
            last_row = last_row + part[-1:].astype(jnp.float32)
        up = [(i, i + 1) for i in range(rows - 1)]
        down = [(i + 1, i) for i in range(rows - 1)]
        low = lax.ppermute(last_row, "row", up)
        high_row = lax.ppermute(first_row, "row", down)
        result = pl.pallas_call(
            functools.partial(finish_kernel, depth - 1),
            out_shape=jax.ShapeDtypeStruct((cells, columns), jnp.bfloat16),
            compiler_params=params(),
            name="finish",
        )(mine, *parts, low, high_row, factor[:, first:last])
        results.append(result)
    return jnp.concatenate(results, axis=1).reshape(1, cells, width)


def solution(mesh):
    in_specs = (
        P("tile", "row", None, None),
        P("tile", "row", None, None),
        P("tile", "row", None),
        P("tile", "row", None),
        P("tile", "row", None),
        P(),
        P(),
        P(),
        P("tile", "row", None),
        P("tile", "row", None),
        P(),
        P("tile", "row", None),
        P("tile", "row", None),
        P("tile", "row", None),
    )
    out_specs = P("tile", "row", None)
    return jax.shard_map(
        on_device, mesh=mesh, in_specs=in_specs, out_specs=out_specs, check_vma=False
    )
```

time: 353 us -> 151 us (0.43)
  the two profiles are of different devices: /device:TPU:10 before, /device:TPU:0 now
where the time goes in v1:
time: 151 us
  starting transfers between devices  53 us (35%)
  waiting for transfers between devices  47 us (31%)
  Pallas kernels  27 us (18%)
  local copies, waits for them, and re-layouts  13.1 us (9%)
  other arithmetic  9.96 us (7%)
    ppermute x25, waiting for transfers between devices, exchange(): return lax.ppermute(array, ('tile', 'row'), pairs)  43.3 us
    ppermute x25, starting transfers between devices, exchange(): return lax.ppermute(array, ('tile', 'row'), pairs)  37.4 us
    pallas_call x1, Pallas kernels, on_device(): pl.pallas_call(functools.partial(resample_kernel, bands, pixels), out_sha...  13.7 us
    ppermute x3, starting transfers between devices, on_device(): low = lax.ppermute(last_row, 'row', up)  11.6 us
    pallas_call x3, Pallas kernels, on_device(): pl.pallas_call(pack_kernel, out_shape=[jax.ShapeDtypeStruct((peers, slots...  5.15 us
    mul x4, local copies, waits for them, and re-layouts, on_device(): mixing[:, :, None, :, None]  5.03 us
    pallas_call x3, Pallas kernels, on_device(): pl.pallas_call(functools.partial(merge_kernel, peers, cells), out_shape=[...  4.79 us
    squeeze x6, local copies, waits for them, and re-layouts, on_device(): both = jnp.concatenate([own[k], arrived[k]], axis=0)  4.29 us
  transfers between devices with their start and end apart: 31, of which 12 were waited for; matrix products, arithmetic and copies ran while one was open for 13% of the time, Pallas kernels for 18%

profile of v1, /device:TPU:0, one launch (start us, length us, event | category | flops | bytes accessed | tf_op | source)
XLA Modules:
  0.0 150.6 jit_solution(12804779041204049452)
XLA Ops:
  0.0 0.7 xor_reduce_fusion
  0.7 0.7 reduce.1
  2.3 0.7 slice.223
  3.4 0.7 reshape_add_fusion.position_ref
  4.2 0.7 reduce.2
  4.9 0.7 tile.12.sensor_ref
  5.7 0.9 copy.18.pick_ref
  6.5 0.7 broadcast_add_fusion
  7.4 1.4 mul.121
  8.8 1.1 mul.122
  9.9 2.4 %mul.123 = f32[256,256]{1,0:T(8,128)} reshape(f32[8,32,8,32]{3,2,1,0:T(8,128)} %mul.122) | data formatting | bytes 524288 | tf_op jit(solution)/shard_map/mul | solution.py:175
  12.3 1.2 multiply_reduce-precision_fusion
  13.6 13.7 %resample.1 = bf16[768,2048]{1,0:T(8,128)(2,1)S(1)} custom-call(bf16[768,2048]{1,0:T(8,128)(2,1)S(1)} %bitcast.103, s32[24,1,256]{2,1,0:T(1,128)S(1)} %copy-done.7, s32[768,1]{1,0:T(8,128)S(1)} %copy.18.pick_ref, f32[2,2,256,256]{3,2,1,0:T(8,128)S(1)} %pad_maximum_fusion.mix_ref, bf16[4,256,256]{2,1,0:T(8,128)(2,1)S(1)} %copy-done.1), custom_call_target="tpu_custom_call" | custom-call | tf_op jit(solution)/shard_map/resample/pallas_call | solution.py:181
  27.4 1.1 pack.5
  28.9 2.5 %pack.4 = (bf16[4,144,768]{2,1,0:T(8,128)(2,1)S(1)}, bf16[4,144,768]{2,1,0:T(8,128)(2,1)}) custom-call(s32[1,768]{1,0:T(1,128)S(1)} %reshape_add_fusion.position_ref, bf16[768,768]{1,0:T(8,128)(2,1)S(1)} %get-tuple-element.30.rows_ref), custom_call_target="tpu_custom_call" | custom-call | tf_op jit(solution)/shard_map/pack/pallas_call | solution.py:215
  31.9 0.8 slice_bitcast_fusion.26
  32.8 0.8 slice_bitcast_fusion.8
  33.6 1.5 %pack.3 = (bf16[4,144,768]{2,1,0:T(8,128)(2,1)S(1)}, bf16[4,144,768]{2,1,0:T(8,128)(2,1)S(1)}) custom-call(s32[1,768]{1,0:T(1,128)S(1)} %reshape_add_fusion.position_ref, bf16[768,768]{1,0:T(8,128)(2,1)S(1)} %get-tuple-element.29.rows_ref), custom_call_target="tpu_custom_call" | custom-call | tf_op jit(solution)/shard_map/pack/pallas_call | solution.py:215
  35.3 0.8 copy.19.brdf_ref
  36.1 2.7 %factor.1 = f32[128,2048]{1,0:T(8,128)S(1)} custom-call(s32[128,256]{1,0:T(8,128)S(1)} %bitcast.104, f32[128,256]{1,0:T(8,128)S(1)} %bitcast.105, f32[128,256]{1,0:T(8,128)S(1)} %bitcast.106, f32[128,256]{1,0:T(8,128)S(1)} %bitcast.107, s32[128,256]{1,0:T(8,128)S(1)} %bitcast.108, f32[8,128]{1,0:T(8,128)S(1)} %pad.4.table_ref, f32[8,3]{1,0:T(8,128)S(1)} %copy.19.brdf_ref), custom_call_target="tpu_custom_call" | custom-call | tf_op jit(solution)/shard_map/factor/pallas_call | solution.py:202
  38.9 2.5 %collective-permute-start.1 = (s32[1,288]{1,0:T(1,128)S(1)}, s32[1,288]{1,0:T(1,128)S(1)}, u32[]{:S(2)}, u32[]{:S(2)}) collective-permute-start(s32[1,288]{1,0:T(1,128)S(1)} %broadcast_in_dim.37), channel_id=1, source_target_pairs={{0,1},{1,0},{2,3},{3,2},{4,5},{5,4},{6,7},{7,6},{8,9},{9,8},{10,11... | collective-permute-start | bytes 3464 | tf_op jit(solution)/shard_map/ppermute | solution.py:152
  41.5 1.2 slice_bitcast_fusion.22
  42.7 0.9 pad_maximum_fusion.10
  43.7 0.9 pad_maximum_fusion.11
  44.6 2.0 %collective-permute-start.24 = (bf16[288,512]{1,0:T(8,128)(2,1)S(1)}, bf16[288,512]{1,0:T(8,128)(2,1)S(1)}, u32[]{:S(2)}, u32[]{:S(2)}) collective-permute-start(bf16[288,512]{1,0:T(8,128)(2,1)S(1)} %pad_maximum_fusion.11), channel_id=1, source_target_pairs={{0,4},{1,5},{2,6},{3,7},{4,0},{5,1},{6,2},{7,3},{8,12},{9,13},{10,... | collective-permute-start | bytes 884744 | tf_op jit(solution)/shard_map/ppermute | solution.py:152
  46.7 1.0 pad_maximum_fusion.12
  47.7 1.6 %collective-permute-start.25 = (bf16[288,512]{1,0:T(8,128)(2,1)S(1)}, bf16[288,512]{1,0:T(8,128)(2,1)S(1)}, u32[]{:S(2)}, u32[]{:S(2)}) collective-permute-start(bf16[288,512]{1,0:T(8,128)(2,1)S(1)} %pad_maximum_fusion.12), channel_id=1, source_target_pairs={{0,5},{1,4},{2,7},{3,6},{4,1},{5,0},{6,3},{7,2},{8,13},{9,12},{10,... | collective-permute-start | bytes 884744 | tf_op jit(solution)/shard_map/ppermute | solution.py:152
  49.3 1.5 collective-permute-start.2
  50.9 9.3 %collective-permute-done.2.refs_2_ = s32[1,288]{1,0:T(1,128)S(1)} collective-permute-done((s32[1,288]{1,0:T(1,128)S(1)}, s32[1,288]{1,0:T(1,128)S(1)}, u32[]{:S(2)}, u32[]{:S(2)}) %collective-permute-start.2) | collective-permute-done | bytes 1184 | tf_op jit(solution)/shard_map/ppermute | solution.py:152
  60.2 2.7 %collective-permute-start.3 = (s32[1,288]{1,0:T(1,128)S(1)}, s32[1,288]{1,0:T(1,128)S(1)}, u32[]{:S(2)}, u32[]{:S(2)}) collective-permute-start(s32[1,288]{1,0:T(1,128)S(1)} %broadcast_in_dim.39), channel_id=1, source_target_pairs={{0,5},{1,4},{2,7},{3,6},{4,1},{5,0},{6,3},{7,2},{8,13},{9,12},{10,... | collective-permute-start | bytes 3464 | tf_op jit(solution)/shard_map/ppermute | solution.py:152
  62.9 1.8 %collective-permute-done.3.refs_3_ = s32[1,288]{1,0:T(1,128)S(1)} collective-permute-done((s32[1,288]{1,0:T(1,128)S(1)}, s32[1,288]{1,0:T(1,128)S(1)}, u32[]{:S(2)}, u32[]{:S(2)}) %collective-permute-start.3) | collective-permute-done | bytes 1184 | tf_op jit(solution)/shard_map/ppermute | solution.py:152
  64.7 1.3 merge.5
  66.0 1.9 %collective-permute-start.26 = (bf16[128,512]{1,0:T(8,128)(2,1)S(1)}, bf16[128,512]{1,0:T(8,128)(2,1)S(1)}, u32[]{:S(2)}, u32[]{:S(2)}) collective-permute-start(bf16[128,512]{1,0:T(8,128)(2,1)S(1)} %get-tuple-element.73), channel_id=1, source_target_pairs={{0,8},{1,9},{2,10},{3,11},{4,12},{5,13},{6,14},{7,15},{8,0},{9,1},... | collective-permute-start | bytes 393224 | tf_op jit(solution)/shard_map/ppermute | solution.py:152
  67.8 2.6 %collective-permute-start.27 = (bf16[128,512]{1,0:T(8,128)(2,1)S(1)}, bf16[128,512]{1,0:T(8,128)(2,1)S(1)}, u32[]{:S(2)}, u32[]{:S(2)}) collective-permute-start(bf16[128,512]{1,0:T(8,128)(2,1)S(1)} %get-tuple-element.72), channel_id=1, source_target_pairs={{0,16},{1,17},{2,18},{3,19},{4,20},{5,21},{6,22},{7,23},{8,24},{9,... | collective-permute-start | bytes 393224 | tf_op jit(solution)/shard_map/ppermute | solution.py:152
  70.4 1.3 slice_bitcast_fusion
  71.8 1.8 %collective-permute-start.14 = (bf16[288,768]{1,0:T(8,128)(2,1)S(1)}, bf16[288,768]{1,0:T(8,128)(2,1)S(1)}, u32[]{:S(2)}, u32[]{:S(2)}) collective-permute-start(bf16[288,768]{1,0:T(8,128)(2,1)S(1)} %pad_maximum_fusion.6), channel_id=1, source_target_pairs={{0,1},{1,0},{2,3},{3,2},{4,5},{5,4},{6,7},{7,6},{8,9},{9,8},{10,11... | collective-permute-start | bytes 1327112 | tf_op jit(solution)/shard_map/ppermute | solution.py:152
  73.8 1.6 %collective-permute-start.15 = (bf16[288,768]{1,0:T(8,128)(2,1)S(1)}, bf16[288,768]{1,0:T(8,128)(2,1)S(1)}, u32[]{:S(2)}, u32[]{:S(2)}) collective-permute-start(bf16[288,768]{1,0:T(8,128)(2,1)S(1)} %pad_maximum_fusion.7), channel_id=1, source_target_pairs={{0,4},{1,5},{2,6},{3,7},{4,0},{5,1},{6,2},{7,3},{8,12},{9,13},{10,... | collective-permute-start | bytes 1327112 | tf_op jit(solution)/shard_map/ppermute | solution.py:152
  75.5 1.5 collective-permute-start.16
  77.0 3.7 %collective-permute-done.27.refs_2_ = bf16[128,512]{1,0:T(8,128)(2,1)S(1)} collective-permute-done((bf16[128,512]{1,0:T(8,128)(2,1)S(1)}, bf16[128,512]{1,0:T(8,128)(2,1)S(1)}, u32[]{:S(2)}, u32[]{:S(2)}) %collective-permute-start.27) | collective-permute-done | bytes 131104 | tf_op jit(solution)/shard_map/ppermute | solution.py:152
  80.7 1.5 %collective-permute-start.5 = (bf16[288,768]{1,0:T(8,128)(2,1)S(1)}, bf16[288,768]{1,0:T(8,128)(2,1)S(1)}, u32[]{:S(2)}, u32[]{:S(2)}) collective-permute-start(bf16[288,768]{1,0:T(8,128)(2,1)S(1)} %pad_maximum_fusion.2), channel_id=1, source_target_pairs={{0,1},{1,0},{2,3},{3,2},{4,5},{5,4},{6,7},{7,6},{8,9},{9,8},{10,11... | collective-permute-start | bytes 1327112 | tf_op jit(solution)/shard_map/ppermute | solution.py:152
  82.3 1.5 collective-permute-start.6
  83.7 2.2 %collective-permute-done.14.refs_5_ = bf16[288,768]{1,0:T(8,128)(2,1)S(1)} collective-permute-done((bf16[288,768]{1,0:T(8,128)(2,1)S(1)}, bf16[288,768]{1,0:T(8,128)(2,1)S(1)}, u32[]{:S(2)}, u32[]{:S(2)}) %collective-permute-start.14) | collective-permute-done | bytes 442400 | tf_op jit(solution)/shard_map/ppermute | solution.py:152
  85.9 3.2 %collective-permute-start.7 = (bf16[288,768]{1,0:T(8,128)(2,1)S(1)}, bf16[288,768]{1,0:T(8,128)(2,1)S(1)}, u32[]{:S(2)}, u32[]{:S(2)}) collective-permute-start(bf16[288,768]{1,0:T(8,128)(2,1)S(1)} %pad_maximum_fusion.4), channel_id=1, source_target_pairs={{0,5},{1,4},{2,7},{3,6},{4,1},{5,0},{6,3},{7,2},{8,13},{9,12},{10,... | collective-permute-start | bytes 1327112 | tf_op jit(solution)/shard_map/ppermute | solution.py:152
  89.1 2.4 %collective-permute-start.29 = (f32[1,512]{1,0:T(1,128)S(1)}, f32[1,512]{1,0:T(1,128)S(1)}, u32[]{:S(2)}, u32[]{:S(2)}) collective-permute-start(f32[1,512]{1,0:T(1,128)S(1)} %get-tuple-element.56), channel_id=1, source_target_pairs={{0,1},{2,3},{4,5},{6,7},{8,9},{10,11},{12,13},{14,15},{16,17},{18,... | collective-permute-start | bytes 6152 | tf_op jit(solution)/shard_map/ppermute | solution.py:242
  91.5 4.6 %collective-permute-done.16.refs_7_ = bf16[288,768]{1,0:T(8,128)(2,1)S(1)} collective-permute-done((bf16[288,768]{1,0:T(8,128)(2,1)S(1)}, bf16[288,768]{1,0:T(8,128)(2,1)S(1)}, u32[]{:S(2)}, u32[]{:S(2)}) %collective-permute-start.16) | collective-permute-done | bytes 442400 | tf_op jit(solution)/shard_map/ppermute | solution.py:152
  96.2 1.5 collective-permute-start.30
  97.6 1.8 %merge.4 = (f32[128,768]{1,0:T(8,128)S(1)}, bf16[3,128,768]{2,1,0:T(8,128)(2,1)S(1)}) custom-call(s32[1,288]{1,0:T(1,128)S(1)} %broadcast_in_dim.36.refs_0_, s32[1,288]{1,0:T(1,128)S(1)} %collective-permute-done.1.refs_1_, s32[1,288]{1,0:T(1,128)S(1)} %collective-permute-done.2.refs_2_, s32[1,288]{1,0:T(1,128)S(1)} %collective-permute-done.3.refs_3_, ...), custom_call_target="tpu_custom_call" | custom-call | tf_op jit(solution)/shard_map/merge/pallas_call | solution.py:226
  99.5 3.4 %collective-permute-done.5.refs_5_ = bf16[288,768]{1,0:T(8,128)(2,1)S(1)} collective-permute-done((bf16[288,768]{1,0:T(8,128)(2,1)S(1)}, bf16[288,768]{1,0:T(8,128)(2,1)S(1)}, u32[]{:S(2)}, u32[]{:S(2)}) %collective-permute-start.5) | collective-permute-done | bytes 442400 | tf_op jit(solution)/shard_map/ppermute | solution.py:152
  102.9 0.9 collective-permute-start.17
  103.7 2.2 %collective-permute-done.6.refs_6_ = bf16[288,768]{1,0:T(8,128)(2,1)S(1)} collective-permute-done((bf16[288,768]{1,0:T(8,128)(2,1)S(1)}, bf16[288,768]{1,0:T(8,128)(2,1)S(1)}, u32[]{:S(2)}, u32[]{:S(2)}) %collective-permute-start.6) | collective-permute-done | bytes 442400 | tf_op jit(solution)/shard_map/ppermute | solution.py:152
  105.9 1.7 %collective-permute-start.18 = (bf16[128,768]{1,0:T(8,128)(2,1)S(1)}, bf16[128,768]{1,0:T(8,128)(2,1)S(1)}, u32[]{:S(2)}, u32[]{:S(2)}) collective-permute-start(bf16[128,768]{1,0:T(8,128)(2,1)S(1)} %get-tuple-element.61), channel_id=1, source_target_pairs={{0,16},{1,17},{2,18},{3,19},{4,20},{5,21},{6,22},{7,23},{8,24},{9,... | collective-permute-start | bytes 589832 | tf_op jit(solution)/shard_map/ppermute | solution.py:152
  107.6 6.1 %collective-permute-done.7.refs_7_ = bf16[288,768]{1,0:T(8,128)(2,1)S(1)} collective-permute-done((bf16[288,768]{1,0:T(8,128)(2,1)S(1)}, bf16[288,768]{1,0:T(8,128)(2,1)S(1)}, u32[]{:S(2)}, u32[]{:S(2)}) %collective-permute-start.7) | collective-permute-done | bytes 442400 | tf_op jit(solution)/shard_map/ppermute | solution.py:152
  113.8 3.5 %collective-permute-start.19 = (bf16[128,768]{1,0:T(8,128)(2,1)S(1)}, bf16[128,768]{1,0:T(8,128)(2,1)S(1)}, u32[]{:S(2)}, u32[]{:S(2)}) collective-permute-start(bf16[128,768]{1,0:T(8,128)(2,1)S(1)} %get-tuple-element.60), channel_id=1, source_target_pairs={{0,24},{1,25},{2,26},{3,27},{4,28},{5,29},{6,30},{7,31},{8,16},{9,... | collective-permute-start | bytes 589832 | tf_op jit(solution)/shard_map/ppermute | solution.py:152
  117.3 1.8 %merge.3 = (f32[128,768]{1,0:T(8,128)S(1)}, bf16[3,128,768]{2,1,0:T(8,128)(2,1)S(1)}) custom-call(s32[1,288]{1,0:T(1,128)S(1)} %broadcast_in_dim.36.refs_0_, s32[1,288]{1,0:T(1,128)S(1)} %collective-permute-done.1.refs_1_, s32[1,288]{1,0:T(1,128)S(1)} %collective-permute-done.2.refs_2_, s32[1,288]{1,0:T(1,128)S(1)} %collective-permute-done.3.refs_3_, ...), custom_call_target="tpu_custom_call" | custom-call | tf_op jit(solution)/shard_map/merge/pallas_call | solution.py:226
  119.2 0.8 collective-permute-start.9
  120.1 3.3 %collective-permute-done.19.refs_3_ = bf16[128,768]{1,0:T(8,128)(2,1)S(1)} collective-permute-done((bf16[128,768]{1,0:T(8,128)(2,1)S(1)}, bf16[128,768]{1,0:T(8,128)(2,1)S(1)}, u32[]{:S(2)}, u32[]{:S(2)}) %collective-permute-start.19) | collective-permute-done | bytes 196640 | tf_op jit(solution)/shard_map/ppermute | solution.py:152
  123.4 3.5 %collective-permute-start.10 = (bf16[128,768]{1,0:T(8,128)(2,1)S(1)}, bf16[128,768]{1,0:T(8,128)(2,1)S(1)}, u32[]{:S(2)}, u32[]{:S(2)}) collective-permute-start(bf16[128,768]{1,0:T(8,128)(2,1)S(1)} %get-tuple-element.57), channel_id=1, source_target_pairs={{0,24},{1,25},{2,26},{3,27},{4,28},{5,29},{6,30},{7,31},{8,16},{9,... | collective-permute-start | bytes 589832 | tf_op jit(solution)/shard_map/ppermute | solution.py:152
  127.4 4.7 %collective-permute-start.20 = (f32[1,768]{1,0:T(1,128)S(1)}, f32[1,768]{1,0:T(1,128)S(1)}, u32[]{:S(2)}, u32[]{:S(2)}) collective-permute-start(f32[1,768]{1,0:T(1,128)S(1)} %get-tuple-element.36), channel_id=1, source_target_pairs={{0,1},{2,3},{4,5},{6,7},{8,9},{10,11},{12,13},{14,15},{16,17},{18,... | collective-permute-start | bytes 9224 | tf_op jit(solution)/shard_map/ppermute | solution.py:242
  132.0 6.1 %collective-permute-done.9.refs_2_ = bf16[128,768]{1,0:T(8,128)(2,1)S(1)} collective-permute-done((bf16[128,768]{1,0:T(8,128)(2,1)S(1)}, bf16[128,768]{1,0:T(8,128)(2,1)S(1)}, u32[]{:S(2)}, u32[]{:S(2)}) %collective-permute-start.9) | collective-permute-done | bytes 196640 | tf_op jit(solution)/shard_map/ppermute | solution.py:152
  138.1 1.3 collective-permute-start.21
  139.5 4.5 %collective-permute-start.11 = (f32[1,768]{1,0:T(1,128)S(1)}, f32[1,768]{1,0:T(1,128)S(1)}, u32[]{:S(2)}, u32[]{:S(2)}) collective-permute-start(f32[1,768]{1,0:T(1,128)S(1)} %get-tuple-element.34), channel_id=1, source_target_pairs={{0,1},{2,3},{4,5},{6,7},{8,9},{10,11},{12,13},{14,15},{16,17},{18,... | collective-permute-start | bytes 9224 | tf_op jit(solution)/shard_map/ppermute | solution.py:242
  144.0 1.3 collective-permute-start.12
  145.9 3.7 %collective-permute-done.12.refs_5_ = f32[1,768]{1,0:T(1,128)S(1)} collective-permute-done((f32[1,768]{1,0:T(1,128)S(1)}, f32[1,768]{1,0:T(1,128)S(1)}, u32[]{:S(2)}, u32[]{:S(2)}) %collective-permute-start.12) | collective-permute-done | bytes 3104 | tf_op jit(solution)/shard_map/ppermute | solution.py:243
  149.8 0.8 maximum_bitcast_fusion
  (101 shorter events, 4.8 us)
Async XLA Ops:
  2.9 35.9 %collective-permute-start = (s32[4,144]{1,0:T(4,128)}, s32[4,144]{1,0:T(4,128)S(1)}, u32[]{:S(2)}, u32[]{:S(2)}) collective-permute-start(s32[4,144]{1,0:T(4,128)} %slice.223), channel_id=1, source_target_pairs={{0,2},{1,3},{2,0},{3,1},{4,6},{5,7},{6,4},{7,5},{8,10},{9,11},{10,... | collective-permute-start | bytes 6920 | tf_op jit(solution)/shard_map/ppermute | solution.py:152
  9.9 3.7 %copy-start = (bf16[1,1,768,2048]{3,2,1,0:T(8,128)(2,1)S(1)}, bf16[1,1,768,2048]{3,2,1,0:T(8,128)(2,1)}, u32[]{:S(2)}) copy-start(bf16[1,1,768,2048]{3,2,1,0:T(8,128)(2,1)} %param.14) | copy-start | bytes 9437188
  12.3 1.4 copy-start.1
  12.3 1.4 copy-start.7
  28.5 13.0 %collective-permute-start.22 = (bf16[4,144,512]{2,1,0:T(8,128)(2,1)S(1)}, bf16[4,144,512]{2,1,0:T(8,128)(2,1)}, u32[]{:S(2)}, u32[]{:S(2)}) collective-permute-start(bf16[4,144,512]{2,1,0:T(8,128)(2,1)S(1)} %get-tuple-element.26), channel_id=1, source_target_pairs={{0,2},{1,3},{2,0},{3,1},{4,6},{5,7},{6,4},{7,5},{8,10},{9,11},{10,... | collective-permute-start | bytes 1769480 | tf_op jit(solution)/shard_map/ppermute | solution.py:152
  31.4 39.1 %collective-permute-start.13 = (bf16[4,144,768]{2,1,0:T(8,128)(2,1)}, bf16[4,144,768]{2,1,0:T(8,128)(2,1)}, u32[]{:S(2)}, u32[]{:S(2)}) collective-permute-start(bf16[4,144,768]{2,1,0:T(8,128)(2,1)} %get-tuple-element.22), channel_id=1, source_target_pairs={{0,2},{1,3},{2,0},{3,1},{4,6},{5,7},{6,4},{7,5},{8,10},{9,11},{10,... | collective-permute-start | bytes 2654216 | tf_op jit(solution)/shard_map/ppermute | solution.py:152
  32.7 3.3 %copy-start.12 = (f32[8,33]{1,0:T(8,128)S(1)}, f32[8,33]{1,0:T(8,128)}, u32[]{:S(2)}) copy-start(f32[8,33]{1,0:T(8,128)} %param.21) | copy-start | bytes 3172
  32.7 3.3 %copy-start.2 = (s32[1,128,256]{2,1,0:T(8,128)S(1)}, s32[1,128,256]{2,1,0:T(8,128)}, u32[]{:S(2)}) copy-start(s32[1,128,256]{2,1,0:T(8,128)} %param.22) | copy-start | bytes 393220
  32.7 3.3 %copy-start.3 = (f32[1,128,256]{2,1,0:T(8,128)S(1)}, f32[1,128,256]{2,1,0:T(8,128)}, u32[]{:S(2)}) copy-start(f32[1,128,256]{2,1,0:T(8,128)} %param.23) | copy-start | bytes 393220
  32.7 3.3 %copy-start.4 = (f32[1,128,256]{2,1,0:T(8,128)S(1)}, f32[1,128,256]{2,1,0:T(8,128)}, u32[]{:S(2)}) copy-start(f32[1,128,256]{2,1,0:T(8,128)} %param.25) | copy-start | bytes 393220
  32.8 3.3 %copy-start.5 = (f32[1,128,256]{2,1,0:T(8,128)S(1)}, f32[1,128,256]{2,1,0:T(8,128)}, u32[]{:S(2)}) copy-start(f32[1,128,256]{2,1,0:T(8,128)} %param.26) | copy-start | bytes 393220
  32.8 3.3 %copy-start.6 = (s32[1,128,256]{2,1,0:T(8,128)S(1)}, s32[1,128,256]{2,1,0:T(8,128)}, u32[]{:S(2)}) copy-start(s32[1,128,256]{2,1,0:T(8,128)} %param.27) | copy-start | bytes 393220
  36.1 26.8 %copy-start.11 = (bf16[144,512]{1,0:T(8,128)(2,1)S(1)}, bf16[144,512]{1,0:T(8,128)(2,1)}, u32[]{:S(2)}) copy-start(bf16[144,512]{1,0:T(8,128)(2,1)} %get-tuple-element.66) | copy-start | bytes 442372
  38.9 10.4 %collective-permute-start.1 = (s32[1,288]{1,0:T(1,128)S(1)}, s32[1,288]{1,0:T(1,128)S(1)}, u32[]{:S(2)}, u32[]{:S(2)}) collective-permute-start(s32[1,288]{1,0:T(1,128)S(1)} %broadcast_in_dim.37), channel_id=1, source_target_pairs={{0,1},{1,0},{2,3},{3,2},{4,5},{5,4},{6,7},{7,6},{8,9},{9,8},{10,11... | collective-permute-start | bytes 3464 | tf_op jit(solution)/shard_map/ppermute | solution.py:152
  43.6 21.0 %collective-permute-start.23 = (bf16[288,512]{1,0:T(8,128)(2,1)S(1)}, bf16[288,512]{1,0:T(8,128)(2,1)S(1)}, u32[]{:S(2)}, u32[]{:S(2)}) collective-permute-start(bf16[288,512]{1,0:T(8,128)(2,1)S(1)} %pad_maximum_fusion.10), channel_id=1, source_target_pairs={{0,1},{1,0},{2,3},{3,2},{4,5},{5,4},{6,7},{7,6},{8,9},{9,8},{10,11... | collective-permute-start | bytes 884744 | tf_op jit(solution)/shard_map/ppermute | solution.py:152
  44.6 20.0 %collective-permute-start.24 = (bf16[288,512]{1,0:T(8,128)(2,1)S(1)}, bf16[288,512]{1,0:T(8,128)(2,1)S(1)}, u32[]{:S(2)}, u32[]{:S(2)}) collective-permute-start(bf16[288,512]{1,0:T(8,128)(2,1)S(1)} %pad_maximum_fusion.11), channel_id=1, source_target_pairs={{0,4},{1,5},{2,6},{3,7},{4,0},{5,1},{6,2},{7,3},{8,12},{9,13},{10,... | collective-permute-start | bytes 884744 | tf_op jit(solution)/shard_map/ppermute | solution.py:152
  46.7 25.1 %copy-start.10 = (bf16[144,768]{1,0:T(8,128)(2,1)S(1)}, bf16[144,768]{1,0:T(8,128)(2,1)}, u32[]{:S(2)}) copy-start(bf16[144,768]{1,0:T(8,128)(2,1)} %get-tuple-element.47) | copy-start | bytes 663556
  47.7 17.0 %collective-permute-start.25 = (bf16[288,512]{1,0:T(8,128)(2,1)S(1)}, bf16[288,512]{1,0:T(8,128)(2,1)S(1)}, u32[]{:S(2)}, u32[]{:S(2)}) collective-permute-start(bf16[288,512]{1,0:T(8,128)(2,1)S(1)} %pad_maximum_fusion.12), channel_id=1, source_target_pairs={{0,5},{1,4},{2,7},{3,6},{4,1},{5,0},{6,3},{7,2},{8,13},{9,12},{10,... | collective-permute-start | bytes 884744 | tf_op jit(solution)/shard_map/ppermute | solution.py:152
  49.3 10.9 %collective-permute-start.2 = (s32[1,288]{1,0:T(1,128)S(1)}, s32[1,288]{1,0:T(1,128)S(1)}, u32[]{:S(2)}, u32[]{:S(2)}) collective-permute-start(s32[1,288]{1,0:T(1,128)S(1)} %broadcast_in_dim.38), channel_id=1, source_target_pairs={{0,4},{1,5},{2,6},{3,7},{4,0},{5,1},{6,2},{7,3},{8,12},{9,13},{10,... | collective-permute-start | bytes 3464 | tf_op jit(solution)/shard_map/ppermute | solution.py:152
  60.2 4.5 %collective-permute-start.3 = (s32[1,288]{1,0:T(1,128)S(1)}, s32[1,288]{1,0:T(1,128)S(1)}, u32[]{:S(2)}, u32[]{:S(2)}) collective-permute-start(s32[1,288]{1,0:T(1,128)S(1)} %broadcast_in_dim.39), channel_id=1, source_target_pairs={{0,5},{1,4},{2,7},{3,6},{4,1},{5,0},{6,3},{7,2},{8,13},{9,12},{10,... | collective-permute-start | bytes 3464 | tf_op jit(solution)/shard_map/ppermute | solution.py:152
  62.9 10.8 %copy-start.9 = (bf16[144,768]{1,0:T(8,128)(2,1)S(1)}, bf16[144,768]{1,0:T(8,128)(2,1)}, u32[]{:S(2)}) copy-start(bf16[144,768]{1,0:T(8,128)(2,1)} %get-tuple-element.48) | copy-start | bytes 663556
  64.7 9.1 %collective-permute-start.4 = (bf16[4,144,768]{2,1,0:T(8,128)(2,1)S(1)}, bf16[4,144,768]{2,1,0:T(8,128)(2,1)S(1)}, u32[]{:S(2)}, u32[]{:S(2)}) collective-permute-start(bf16[4,144,768]{2,1,0:T(8,128)(2,1)S(1)} %get-tuple-element.18), channel_id=1, source_target_pairs={{0,2},{1,3},{2,0},{3,1},{4,6},{5,7},{6,4},{7,5},{8,10},{9,11},{10,... | collective-permute-start | bytes 2654216 | tf_op jit(solution)/shard_map/ppermute | solution.py:152
  65.9 7.7 %copy-start.8 = (bf16[144,768]{1,0:T(8,128)(2,1)S(1)}, bf16[144,768]{1,0:T(8,128)(2,1)}, u32[]{:S(2)}) copy-start(bf16[144,768]{1,0:T(8,128)(2,1)} %get-tuple-element.46) | copy-start | bytes 663556
  66.0 9.5 %collective-permute-start.26 = (bf16[128,512]{1,0:T(8,128)(2,1)S(1)}, bf16[128,512]{1,0:T(8,128)(2,1)S(1)}, u32[]{:S(2)}, u32[]{:S(2)}) collective-permute-start(bf16[128,512]{1,0:T(8,128)(2,1)S(1)} %get-tuple-element.73), channel_id=1, source_target_pairs={{0,8},{1,9},{2,10},{3,11},{4,12},{5,13},{6,14},{7,15},{8,0},{9,1},... | collective-permute-start | bytes 393224 | tf_op jit(solution)/shard_map/ppermute | solution.py:152
  67.8 12.9 %collective-permute-start.27 = (bf16[128,512]{1,0:T(8,128)(2,1)S(1)}, bf16[128,512]{1,0:T(8,128)(2,1)S(1)}, u32[]{:S(2)}, u32[]{:S(2)}) collective-permute-start(bf16[128,512]{1,0:T(8,128)(2,1)S(1)} %get-tuple-element.72), channel_id=1, source_target_pairs={{0,16},{1,17},{2,18},{3,19},{4,20},{5,21},{6,22},{7,23},{8,24},{9,... | collective-permute-start | bytes 393224 | tf_op jit(solution)/shard_map/ppermute | solution.py:152
  70.4 11.8 %collective-permute-start.28 = (bf16[128,512]{1,0:T(8,128)(2,1)S(1)}, bf16[128,512]{1,0:T(8,128)(2,1)S(1)}, u32[]{:S(2)}, u32[]{:S(2)}) collective-permute-start(bf16[128,512]{1,0:T(8,128)(2,1)S(1)} %get-tuple-element.71), channel_id=1, source_target_pairs={{0,24},{1,25},{2,26},{3,27},{4,28},{5,29},{6,30},{7,31},{8,16},{9,... | collective-permute-start | bytes 393224 | tf_op jit(solution)/shard_map/ppermute | solution.py:152
  71.8 14.1 %collective-permute-start.14 = (bf16[288,768]{1,0:T(8,128)(2,1)S(1)}, bf16[288,768]{1,0:T(8,128)(2,1)S(1)}, u32[]{:S(2)}, u32[]{:S(2)}) collective-permute-start(bf16[288,768]{1,0:T(8,128)(2,1)S(1)} %pad_maximum_fusion.6), channel_id=1, source_target_pairs={{0,1},{1,0},{2,3},{3,2},{4,5},{5,4},{6,7},{7,6},{8,9},{9,8},{10,11... | collective-permute-start | bytes 1327112 | tf_op jit(solution)/shard_map/ppermute | solution.py:152
  73.8 15.4 %collective-permute-start.15 = (bf16[288,768]{1,0:T(8,128)(2,1)S(1)}, bf16[288,768]{1,0:T(8,128)(2,1)S(1)}, u32[]{:S(2)}, u32[]{:S(2)}) collective-permute-start(bf16[288,768]{1,0:T(8,128)(2,1)S(1)} %pad_maximum_fusion.7), channel_id=1, source_target_pairs={{0,4},{1,5},{2,6},{3,7},{4,0},{5,1},{6,2},{7,3},{8,12},{9,13},{10,... | collective-permute-start | bytes 1327112 | tf_op jit(solution)/shard_map/ppermute | solution.py:152
  75.5 20.7 %collective-permute-start.16 = (bf16[288,768]{1,0:T(8,128)(2,1)S(1)}, bf16[288,768]{1,0:T(8,128)(2,1)S(1)}, u32[]{:S(2)}, u32[]{:S(2)}) collective-permute-start(bf16[288,768]{1,0:T(8,128)(2,1)S(1)} %pad_maximum_fusion.8), channel_id=1, source_target_pairs={{0,5},{1,4},{2,7},{3,6},{4,1},{5,0},{6,3},{7,2},{8,13},{9,12},{10,... | collective-permute-start | bytes 1327112 | tf_op jit(solution)/shard_map/ppermute | solution.py:152
  80.7 22.1 %collective-permute-start.5 = (bf16[288,768]{1,0:T(8,128)(2,1)S(1)}, bf16[288,768]{1,0:T(8,128)(2,1)S(1)}, u32[]{:S(2)}, u32[]{:S(2)}) collective-permute-start(bf16[288,768]{1,0:T(8,128)(2,1)S(1)} %pad_maximum_fusion.2), channel_id=1, source_target_pairs={{0,1},{1,0},{2,3},{3,2},{4,5},{5,4},{6,7},{7,6},{8,9},{9,8},{10,11... | collective-permute-start | bytes 1327112 | tf_op jit(solution)/shard_map/ppermute | solution.py:152
  82.3 23.7 %collective-permute-start.6 = (bf16[288,768]{1,0:T(8,128)(2,1)S(1)}, bf16[288,768]{1,0:T(8,128)(2,1)S(1)}, u32[]{:S(2)}, u32[]{:S(2)}) collective-permute-start(bf16[288,768]{1,0:T(8,128)(2,1)S(1)} %pad_maximum_fusion.3), channel_id=1, source_target_pairs={{0,4},{1,5},{2,6},{3,7},{4,0},{5,1},{6,2},{7,3},{8,12},{9,13},{10,... | collective-permute-start | bytes 1327112 | tf_op jit(solution)/shard_map/ppermute | solution.py:152
  85.9 27.8 %collective-permute-start.7 = (bf16[288,768]{1,0:T(8,128)(2,1)S(1)}, bf16[288,768]{1,0:T(8,128)(2,1)S(1)}, u32[]{:S(2)}, u32[]{:S(2)}) collective-permute-start(bf16[288,768]{1,0:T(8,128)(2,1)S(1)} %pad_maximum_fusion.4), channel_id=1, source_target_pairs={{0,5},{1,4},{2,7},{3,6},{4,1},{5,0},{6,3},{7,2},{8,13},{9,12},{10,... | collective-permute-start | bytes 1327112 | tf_op jit(solution)/shard_map/ppermute | solution.py:152
  89.1 54.9 %collective-permute-start.29 = (f32[1,512]{1,0:T(1,128)S(1)}, f32[1,512]{1,0:T(1,128)S(1)}, u32[]{:S(2)}, u32[]{:S(2)}) collective-permute-start(f32[1,512]{1,0:T(1,128)S(1)} %get-tuple-element.56), channel_id=1, source_target_pairs={{0,1},{2,3},{4,5},{6,7},{8,9},{10,11},{12,13},{14,15},{16,17},{18,... | collective-permute-start | bytes 6152 | tf_op jit(solution)/shard_map/ppermute | solution.py:242
  96.2 49.3 %collective-permute-start.30 = (f32[1,512]{1,0:T(1,128)S(1)}, f32[1,512]{1,0:T(1,128)S(1)}, u32[]{:S(2)}, u32[]{:S(2)}) collective-permute-start(f32[1,512]{1,0:T(1,128)S(1)} %get-tuple-element.55), channel_id=1, source_target_pairs={{1,0},{3,2},{5,4},{7,6},{9,8},{11,10},{13,12},{15,14},{17,16},{19,... | collective-permute-start | bytes 6152 | tf_op jit(solution)/shard_map/ppermute | solution.py:243
  102.9 16.3 %collective-permute-start.17 = (bf16[128,768]{1,0:T(8,128)(2,1)S(1)}, bf16[128,768]{1,0:T(8,128)(2,1)S(1)}, u32[]{:S(2)}, u32[]{:S(2)}) collective-permute-start(bf16[128,768]{1,0:T(8,128)(2,1)S(1)} %get-tuple-element.62), channel_id=1, source_target_pairs={{0,8},{1,9},{2,10},{3,11},{4,12},{5,13},{6,14},{7,15},{8,0},{9,1},... | collective-permute-start | bytes 589832 | tf_op jit(solution)/shard_map/ppermute | solution.py:152
  105.9 13.3 %collective-permute-start.18 = (bf16[128,768]{1,0:T(8,128)(2,1)S(1)}, bf16[128,768]{1,0:T(8,128)(2,1)S(1)}, u32[]{:S(2)}, u32[]{:S(2)}) collective-permute-start(bf16[128,768]{1,0:T(8,128)(2,1)S(1)} %get-tuple-element.61), channel_id=1, source_target_pairs={{0,16},{1,17},{2,18},{3,19},{4,20},{5,21},{6,22},{7,23},{8,24},{9,... | collective-permute-start | bytes 589832 | tf_op jit(solution)/shard_map/ppermute | solution.py:152
  113.8 9.6 %collective-permute-start.19 = (bf16[128,768]{1,0:T(8,128)(2,1)S(1)}, bf16[128,768]{1,0:T(8,128)(2,1)S(1)}, u32[]{:S(2)}, u32[]{:S(2)}) collective-permute-start(bf16[128,768]{1,0:T(8,128)(2,1)S(1)} %get-tuple-element.60), channel_id=1, source_target_pairs={{0,24},{1,25},{2,26},{3,27},{4,28},{5,29},{6,30},{7,31},{8,16},{9,... | collective-permute-start | bytes 589832 | tf_op jit(solution)/shard_map/ppermute | solution.py:152
  119.1 8.2 %collective-permute-start.8 = (bf16[128,768]{1,0:T(8,128)(2,1)S(1)}, bf16[128,768]{1,0:T(8,128)(2,1)S(1)}, u32[]{:S(2)}, u32[]{:S(2)}) collective-permute-start(bf16[128,768]{1,0:T(8,128)(2,1)S(1)} %get-tuple-element.59), channel_id=1, source_target_pairs={{0,8},{1,9},{2,10},{3,11},{4,12},{5,13},{6,14},{7,15},{8,0},{9,1},... | collective-permute-start | bytes 589832 | tf_op jit(solution)/shard_map/ppermute | solution.py:152
  119.2 18.9 %collective-permute-start.9 = (bf16[128,768]{1,0:T(8,128)(2,1)S(1)}, bf16[128,768]{1,0:T(8,128)(2,1)S(1)}, u32[]{:S(2)}, u32[]{:S(2)}) collective-permute-start(bf16[128,768]{1,0:T(8,128)(2,1)S(1)} %get-tuple-element.58), channel_id=1, source_target_pairs={{0,16},{1,17},{2,18},{3,19},{4,20},{5,21},{6,22},{7,23},{8,24},{9,... | collective-permute-start | bytes 589832 | tf_op jit(solution)/shard_map/ppermute | solution.py:152
  123.4 16.0 %collective-permute-start.10 = (bf16[128,768]{1,0:T(8,128)(2,1)S(1)}, bf16[128,768]{1,0:T(8,128)(2,1)S(1)}, u32[]{:S(2)}, u32[]{:S(2)}) collective-permute-start(bf16[128,768]{1,0:T(8,128)(2,1)S(1)} %get-tuple-element.57), channel_id=1, source_target_pairs={{0,24},{1,25},{2,26},{3,27},{4,28},{5,29},{6,30},{7,31},{8,16},{9,... | collective-permute-start | bytes 589832 | tf_op jit(solution)/shard_map/ppermute | solution.py:152
  127.4 18.2 %collective-permute-start.20 = (f32[1,768]{1,0:T(1,128)S(1)}, f32[1,768]{1,0:T(1,128)S(1)}, u32[]{:S(2)}, u32[]{:S(2)}) collective-permute-start(f32[1,768]{1,0:T(1,128)S(1)} %get-tuple-element.36), channel_id=1, source_target_pairs={{0,1},{2,3},{4,5},{6,7},{8,9},{10,11},{12,13},{14,15},{16,17},{18,... | collective-permute-start | bytes 9224 | tf_op jit(solution)/shard_map/ppermute | solution.py:242
  138.1 7.5 %collective-permute-start.21 = (f32[1,768]{1,0:T(1,128)S(1)}, f32[1,768]{1,0:T(1,128)S(1)}, u32[]{:S(2)}, u32[]{:S(2)}) collective-permute-start(f32[1,768]{1,0:T(1,128)S(1)} %get-tuple-element.35), channel_id=1, source_target_pairs={{1,0},{3,2},{5,4},{7,6},{9,8},{11,10},{13,12},{15,14},{17,16},{19,... | collective-permute-start | bytes 9224 | tf_op jit(solution)/shard_map/ppermute | solution.py:243
  139.5 6.4 %collective-permute-start.11 = (f32[1,768]{1,0:T(1,128)S(1)}, f32[1,768]{1,0:T(1,128)S(1)}, u32[]{:S(2)}, u32[]{:S(2)}) collective-permute-start(f32[1,768]{1,0:T(1,128)S(1)} %get-tuple-element.34), channel_id=1, source_target_pairs={{0,1},{2,3},{4,5},{6,7},{8,9},{10,11},{12,13},{14,15},{16,17},{18,... | collective-permute-start | bytes 9224 | tf_op jit(solution)/shard_map/ppermute | solution.py:242
  144.0 5.5 %collective-permute-start.12 = (f32[1,768]{1,0:T(1,128)S(1)}, f32[1,768]{1,0:T(1,128)S(1)}, u32[]{:S(2)}, u32[]{:S(2)}) collective-permute-start(f32[1,768]{1,0:T(1,128)S(1)} %get-tuple-element.33), channel_id=1, source_target_pairs={{1,0},{3,2},{5,4},{7,6},{9,8},{11,10},{13,12},{15,14},{17,16},{19,... | collective-permute-start | bytes 9224 | tf_op jit(solution)/shard_map/ppermute | solution.py:243

commit v2 on v1

v2 whole, which is shorter than its diff:
```python
import functools

import jax
import jax.numpy as jnp
from jax import lax
from jax.experimental import pallas as pl
from jax.experimental.pallas import tpu as pltpu
from jax.sharding import PartitionSpec as P

nadir_volume = 0.3
nadir_geometric = 0.6

GROUP = 32
TAG_ROWS = 16
CHUNKS = ((0, 2), (2, 4), (4, 6), (6, 8))
ORDER = ("s0", "s1", "j0", "s2", "j1", "m0", "h0", "s3", "j2", "h0", "m1", "h1", "g0", "j3", "h1", "m2", "h2", "g1", "h2", "m3", "h3", "g2", "h3", "x0", "g3", "f0")
UNROLL = 6
SPLIT = (2, 1, 1)
MIB = 1024 * 1024


def call(kernel, name, limit, out_shape, operands, after, scalars=0, **more):
    vmem = pl.BlockSpec(memory_space=pltpu.VMEM)
    smem = pl.BlockSpec(memory_space=pltpu.SMEM)
    specs = more.pop("in_specs", None)
    if specs is None:
        specs = [smem] * scalars + [vmem] * (len(operands) - scalars)
    body = kernel
    if after is not None:
        specs = [pl.BlockSpec(memory_space=pl.ANY), *specs]
        operands = (after, *operands)

        def body(unused, *refs):
            kernel(*refs)

    return pl.pallas_call(
        body,
        out_shape=out_shape,
        in_specs=specs,
        out_specs=jax.tree.map(lambda _: vmem, out_shape),
        compiler_params=pltpu.CompilerParams(vmem_limit_bytes=limit * MIB),
        name=name,
        **more,
    )(*operands)


def dot(a, b):
    return jnp.dot(a, b, preferred_element_type=jnp.float32)


def one_hot(mask):
    return mask.astype(jnp.float32).astype(jnp.bfloat16)


def spread_mixing(offset_ref, s, b, bands):
    lane = lax.broadcasted_iota(jnp.int32, (GROUP, bands * GROUP), 1)
    row = lax.broadcasted_iota(jnp.int32, (GROUP, bands * GROUP), 0)
    total = jnp.zeros((GROUP, bands * GROUP), jnp.float32)
    for c in range(bands):
        value = offset_ref[s, b, c] + (1.0 if b == c else 0.0)
        total = jnp.where(lane == row + c * GROUP, value, total)
    return total


def routes(me, footprint, depth, rows):
    shift = rows.bit_length() - 1
    relative = jnp.bitwise_xor(footprint, me)
    rel_y = relative & (rows - 1)
    rel_core = lax.shift_right_logical(relative, shift) & 1
    rel_x = lax.shift_right_logical(relative, shift + 1) & 1
    rel_z = lax.shift_right_logical(relative, shift + 2)
    chip = rel_x * rows + rel_y
    if rows == 2:
        core = lax.shift_right_logical(me, shift) & 1
        swap = jnp.logical_and(core == 1, jnp.logical_or(chip == 1, chip == 2))
        chip = jnp.where(swap, 3 - chip, chip)
    return rel_z, chip * 2 + rel_core


def resample(shape, chunk, offset_ref, x_ref, wait, code_cols, weights_ref, banded_ref, result_ref):
    bands, pixels = shape[:2]
    begin, end = chunk
    blocks = x_ref.shape[0]
    count = end - begin
    tiles = weights_ref.shape[0]
    high, low = [], []
    for s in range(2):
        exact = jnp.concatenate(
            [spread_mixing(offset_ref, s, b, bands) for b in range(begin, end)], axis=0
        )
        upper = exact.astype(jnp.bfloat16)
        high.append(upper)
        low.append((exact - upper.astype(jnp.float32)).astype(jnp.bfloat16))
    mixers = jnp.concatenate(high + low, axis=0)
    size = count * GROUP

    def one_group(g):
        here = pl.ds(pl.multiple_of(g * GROUP, GROUP), GROUP)
        stacked = jnp.concatenate(
            [x_ref[here, c * pixels : (c + 1) * pixels] for c in range(bands)], axis=0
        )
        mixed = dot(mixers, stacked)
        first = mixed[:size] + mixed[2 * size : 3 * size]
        second = mixed[size : 2 * size] + mixed[3 * size :]
        lanes = code_cols[here, :]
        choice = jnp.concatenate([lanes] * (pixels // 128), axis=1) > tiles - 0.5
        for b in range(count):
            part = slice(b * GROUP, (b + 1) * GROUP)
            banded_ref[b, here, :] = jnp.where(choice, second[part], first[part]).astype(
                jnp.bfloat16
            )

    step = UNROLL * GROUP
    for start in range(0, blocks, step):
        wait(start, step)
        for g in range(start // GROUP, (start + step) // GROUP):
            one_group(g)

    code = jnp.concatenate([code_cols[...]] * (pixels // 128), axis=1)
    pick = jnp.where(code > tiles - 0.5, code - tiles, code)
    for b in range(count):
        banded = banded_ref[b].astype(jnp.float32)
        total = None
        for t in range(tiles):
            part = dot(jnp.where(pick == t, banded, 0.0).astype(jnp.bfloat16), weights_ref[t])
            total = part if total is None else total + part
        result_ref[:, b * pixels : (b + 1) * pixels] = total.astype(jnp.bfloat16)


def pack(position, slots, layout, result_ref, out_refs, tags=None):
    blocks = result_ref.shape[0]
    for chips, ref in zip(layout, out_refs):
        height = ref.shape[0] // len(chips)
        for i, k in enumerate(chips):
            ids = lax.broadcasted_iota(jnp.int32, (slots, blocks), 0) + k * slots
            chosen = one_hot(ids == position)
            start = i * height
            ref[start : start + slots, :] = dot(chosen, result_ref[...]).astype(jnp.bfloat16)
            if tags is not None:
                start, stop = start + slots, start + height
                ref[start:stop, :] = jnp.zeros((TAG_ROWS, ref.shape[1]), jnp.bfloat16)
                ref[start:stop, :slots] = lax.dot_general(
                    tags, chosen, (((1,), (1,)), ((), ())), preferred_element_type=jnp.float32
                ).astype(jnp.bfloat16)


def lead_kernel(shape, chunk, *refs):
    bands, pixels, rows, depth, slots, peers, layout = shape
    count = len(layout)
    ins, outs, scratch = refs[:8], refs[8 : 10 + count], refs[10 + count :]
    me_ref = ins[0]
    position_ref, code_cols = outs[count:]
    offset, x, foot, cell, pick, sensor, weights, banded_ref, result_ref, sems = scratch
    blocks = x.shape[0]
    tiles = weights.shape[0]
    step = UNROLL * GROUP
    small = [
        pltpu.make_async_copy(src, dst, sems.at[i])
        for i, (src, dst) in enumerate(
            ((ins[3], foot), (ins[4], cell), (ins[5], pick), (ins[6], sensor), (ins[1], offset))
        )
    ]
    matrices = pltpu.make_async_copy(ins[7], weights, sems.at[5])
    pieces = {
        start: pltpu.make_async_copy(
            ins[2].at[pl.ds(start, step), :], x.at[pl.ds(start, step), :], sems.at[6 + i]
        )
        for i, start in enumerate(range(0, blocks, step))
    }
    for copy in (*small, *pieces.values(), matrices):
        copy.start()
    for copy in small:
        copy.wait()

    code = pick[...] + tiles * sensor[...]
    code_cols[...] = jnp.broadcast_to(code.astype(jnp.float32), (128, blocks)).T

    place, group = routes(me_ref[0], foot[...], depth, rows)
    member = lax.broadcasted_iota(jnp.int32, (2 * peers, blocks), 0) == group
    member = member.astype(jnp.float32)
    earlier = lax.broadcasted_iota(jnp.int32, (blocks, blocks), 0) < lax.broadcasted_iota(
        jnp.int32, (blocks, blocks), 1
    )
    before = dot(member.astype(jnp.bfloat16), one_hot(earlier))
    rank = jnp.sum(member * before, axis=0, keepdims=True).astype(jnp.int32)
    position = group * (slots // 2) + rank
    position_ref[...] = position
    line = lax.broadcasted_iota(jnp.int32, (TAG_ROWS, blocks), 0)
    tags = jnp.where(line == 0, cell[...] + 1, jnp.where(line == 1, place, 0))
    tags = tags.astype(jnp.float32).astype(jnp.bfloat16)

    def wait(start, size):
        pieces[start].wait()
        if start == 0:
            matrices.wait()

    resample(shape, chunk, offset, x, wait, code_cols, weights, banded_ref, result_ref)
    pack(position, slots, layout, result_ref, outs[:count], tags)


def follow_kernel(shape, chunk, *refs):
    slots, layout = shape[4], shape[6]
    count = len(layout)
    offset_ref, x_ref, position_ref, code_cols, weights_ref = refs[:5]
    outs, (banded_ref, result_ref) = refs[5 : 5 + count], refs[5 + count :]
    resample(
        shape,
        chunk,
        offset_ref,
        x_ref,
        lambda start, size: None,
        code_cols,
        weights_ref,
        banded_ref,
        result_ref,
    )
    pack(position_ref[...], slots, layout, result_ref, outs)


def join_kernel(own_ref, arrived_ref, out_ref):
    height = own_ref.shape[0]
    out_ref[:height, :] = own_ref[...]
    out_ref[height:, :] = arrived_ref[height:, :]


def put(refs, planes):
    start = 0
    for ref in refs:
        ref[...] = planes[start : start + ref.shape[0]]
        start += ref.shape[0]


def merge_kernel(lead, slots, cells, parts, *refs):
    count = max(part[0] for part in parts) + 1
    rows = refs[:count]
    if lead:
        keep_ref, *sends, keys_ref = refs[count:]
    else:
        keys_ref, keep_ref, *sends = refs[count:]
    depth, columns = keep_ref.shape[0], keep_ref.shape[2]
    half = slots // 2
    ids = lax.broadcasted_iota(jnp.int32, (depth * cells, half), 0)
    for h in (1, 0):
        total = None
        for i, (j, start) in enumerate(parts):
            if lead:
                tag = rows[j][start + slots : start + slots + TAG_ROWS, h * half : (h + 1) * half]
                tag = tag.astype(jnp.float32)
                cell, place = tag[0:1].astype(jnp.int32), tag[1:2].astype(jnp.int32)
                key = place * cells + cell - 1
                keys_ref[2 * i + h] = key
            else:
                key = keys_ref[2 * i + h]
            first = start + h * half
            part = dot(one_hot(ids == key), rows[j][first : first + half, :])
            total = part if total is None else total + part
        total = total.reshape(depth, cells, columns)
        if h == 0:
            keep_ref[...] = total
        else:
            put(sends, total.astype(jnp.bfloat16))


def halve_kernel(count, *refs):
    kept_ref, arrived, keep_ref, sends = (
        refs[0],
        refs[1 : 1 + count],
        refs[1 + count],
        refs[2 + count :],
    )
    away = []
    start = 0
    for ref in arrived:
        for i in range(ref.shape[0]):
            plane = kept_ref[start] + ref[i].astype(jnp.float32)
            if start % 2 == 0:
                keep_ref[start // 2] = plane
            else:
                away.append(plane.astype(jnp.bfloat16)[None])
            start += 1
    put(sends, jnp.concatenate(away, axis=0))


def factor_kernel(bands, pixels, bin_ref, frac_ref, vol_ref, geo_ref, mask_ref, table_ref, brdf_ref, out_ref):
    rows = 8

    def some_rows(i, carry):
        here = pl.ds(pl.multiple_of(i * rows, rows), rows)
        for p in range(0, pixels, 128):
            at = (here, slice(p, p + 128))
            index, fraction = bin_ref[at], frac_ref[at]
            vol, geo = vol_ref[at], geo_ref[at]
            mask = mask_ref[at].astype(jnp.float32)
            for b in range(bands):
                line = jnp.broadcast_to(table_ref[b : b + 1, :], (rows, 128))
                lower = jnp.take_along_axis(line, index, axis=1)
                upper = jnp.take_along_axis(line, index + 1, axis=1)
                table_value = lower * (1.0 - fraction) + upper * fraction
                w0, w1, w2 = brdf_ref[b, 0], brdf_ref[b, 1], brdf_ref[b, 2]
                numerator = w0 + w1 * nadir_volume + w2 * nadir_geometric
                cfactor = numerator / (w0 + w1 * vol + w2 * geo)
                first = b * pixels + p
                out_ref[here, first : first + 128] = table_value * cfactor * mask
        return carry

    lax.fori_loop(0, out_ref.shape[0] // rows, some_rows, 0)


def total_kernel(kept_ref, arrived_ref, grid_ref):
    grid_ref[...] = kept_ref[0] + arrived_ref[0].astype(jnp.float32)


def finish_kernel(count, *refs):
    grids, (low_ref, high_ref, factor_ref, out_ref) = refs[:count], refs[count:]
    start = 0
    for grid_ref in grids:
        grid = grid_ref[...]
        here = slice(start, start + grid.shape[1])
        before = jnp.concatenate([low_ref[:, here], grid[:-1]], axis=0)
        after = jnp.concatenate([grid[1:], high_ref[:, here]], axis=0)
        smoothed = 0.25 * before + 0.5 * grid + 0.25 * after
        out_ref[:, here] = (smoothed * factor_ref[:, here]).astype(jnp.bfloat16)
        start = here.stop


def on_device(
    swath_blocks,
    footprint,
    cell_row,
    tile_pick,
    sensor,
    bandpass_offset,
    weight_tiles,
    lookup_table,
    lookup_bin,
    lookup_frac,
    brdf_params,
    vol_kernel,
    geo_kernel,
    clear_mask,
):
    tiles, rows = lax.axis_size("tile"), lax.axis_size("row")
    devices = tiles * rows
    blocks, width = swath_blocks.shape[2], swath_blocks.shape[3]
    bands = bandpass_offset.shape[1]
    pixels = width // bands
    cells = lookup_bin.shape[1]
    capacity = max(2, 3 * blocks // (2 * devices))
    depth = tiles // 4
    peers = 2 * rows
    slots = 2 * depth * capacity
    bits = dict(z=4 * rows, x=2 * rows, core=rows, y=1)

    def exchange(array, flip, other=None):
        flips = (flip, flip if other is None else other)
        pairs = [(i, i ^ flips[i // rows % 2]) for i in range(devices)]
        return lax.ppermute(array, ("tile", "row"), pairs)

    def chip_flip(k):
        return (k // rows) * bits["x"] + k % rows

    me = lax.axis_index("tile") * rows + lax.axis_index("row")
    smem = pl.BlockSpec(memory_space=pltpu.SMEM)
    hbm = pl.BlockSpec(memory_space=pltpu.HBM)
    layout = ((0,), (1, 3), (2,)) if rows == 2 else tuple((k,) for k in range(peers))
    shape = (bands, pixels, rows, depth, slots, peers, layout)
    x = swath_blocks.reshape(blocks, width)
    table = jnp.pad(lookup_table, ((0, 0), (0, 128 - lookup_table.shape[1])))
    flips = [bits["core"]] + [bits["z"] << i for i in range(depth.bit_length() - 1)]
    shared = {}
    chunks = [dict(hops=0) for _ in CHUNKS]

    def struct(*dims, dtype=jnp.bfloat16):
        return jax.ShapeDtypeStruct(dims, dtype)

    def send(i, after):
        begin, end = CHUNKS[i]
        columns = (end - begin) * pixels
        height = slots + (0 if i else TAG_ROWS)
        payload = [struct(len(chips) * height, columns) for chips in layout]
        work = [
            pltpu.VMEM((end - begin, blocks, pixels), jnp.bfloat16),
            pltpu.VMEM((blocks, columns), jnp.bfloat16),
        ]
        if i == 0:
            *lists, shared["position"], shared["codes"] = call(
                functools.partial(lead_kernel, shape, CHUNKS[i]),
                "lead",
                63,
                payload
                + [struct(1, blocks, dtype=jnp.int32), struct(blocks, 128, dtype=jnp.float32)],
                (
                    me.reshape(1).astype(jnp.int32),
                    bandpass_offset,
                    x,
                    footprint.reshape(1, blocks),
                    cell_row.reshape(1, blocks),
                    tile_pick.reshape(1, blocks),
                    sensor.reshape(1, blocks),
                    weight_tiles,
                ),
                after,
                in_specs=[smem] + [hbm] * 7,
                scratch_shapes=[
                    pltpu.SMEM(bandpass_offset.shape, jnp.float32),
                    pltpu.VMEM((blocks, width), jnp.bfloat16),
                    *[pltpu.VMEM((1, blocks), jnp.int32)] * 4,
                    pltpu.VMEM(weight_tiles.shape, jnp.bfloat16),
                    *work,
                    pltpu.SemaphoreType.DMA((6 + blocks // (UNROLL * GROUP),)),
                ],
            )
        else:
            lists = call(
                functools.partial(follow_kernel, shape, CHUNKS[i]),
                "follow",
                28,
                payload,
                (bandpass_offset, x, shared["position"], shared["codes"], weight_tiles),
                after,
                scalars=1,
                scratch_shapes=work,
            )
        if rows == 2:
            own, first, chunks[i]["second"] = lists
            chunks[i]["lists"] = [own, exchange(first, bits["y"], bits["x"])]
        else:
            chunks[i]["lists"] = [
                array if k == 0 else exchange(array, chip_flip(k)) for k, array in enumerate(lists)
            ]
        chunks[i]["parts"] = [(k, 0) for k in range(len(lists))]
        return lists[0]

    def join(i, after):
        if rows != 2:
            return after
        chunk = chunks[i]
        arrived = chunk["lists"][1]
        height, columns = arrived.shape
        both = call(
            join_kernel, "join", 16, struct(height, columns), (chunk["second"], arrived), after
        )
        chunk["lists"].append(exchange(both, bits["x"], bits["y"]))
        chunk["parts"] = [(0, 0), (1, 0), (2, 0), (2, height // 2)]
        return both

    def forward(i, keep, sends):
        chunk = chunks[i]
        chunk["keep"] = keep
        chunk["arrived"] = [exchange(array, flips[chunk["hops"]]) for array in sends]
        chunk["hops"] += 1
        return sends[0]

    def pieces(hop, planes, columns):
        count = min(planes, SPLIT[min(hop, 2)])
        return [struct(planes // count, cells, columns)] * count

    def merge(i, after):
        arrays = chunks[i]["lists"]
        columns = arrays[0].shape[1]
        parts = chunks[i]["parts"]
        outs = [struct(depth, cells, columns, dtype=jnp.float32), *pieces(0, depth, columns)]
        if i == 0:
            outs.append(struct(2 * peers, 1, slots // 2, dtype=jnp.int32))
        outs = call(
            functools.partial(merge_kernel, i == 0, slots, cells, parts),
            "merge",
            24,
            outs,
            (*arrays, *(() if i == 0 else (shared["keys"],))),
            after,
        )
        if i == 0:
            (*outs, shared["keys"]) = outs
        return forward(i, outs[0], outs[1:])

    def halve(i, after):
        keep, arrived = chunks[i]["keep"], chunks[i]["arrived"]
        half, columns = keep.shape[0] // 2, keep.shape[2]
        outs = call(
            functools.partial(halve_kernel, len(arrived)),
            "halve",
            16,
            [
                struct(half, cells, columns, dtype=jnp.float32),
                *pieces(chunks[i]["hops"], half, columns),
            ],
            (keep, *arrived),
            after,
        )
        return forward(i, outs[0], outs[1:])

    def total(i, after):
        chunk = chunks[i]
        while chunk["keep"].shape[0] > 1:
            after = halve(i, after)
        chunk["grid"] = call(
            total_kernel,
            "total",
            16,
            struct(*chunk["keep"].shape[1:], dtype=jnp.float32),
            (chunk["keep"], *chunk["arrived"]),
            after,
        )
        return chunk["grid"]

    def finish(i, after):
        first_row = jnp.concatenate([chunk["grid"][:1] for chunk in chunks], axis=1)
        last_row = jnp.concatenate([chunk["grid"][-1:] for chunk in chunks], axis=1)
        if rows == 2:
            upper_half = lax.axis_index("row") == 0
            edge = lax.ppermute(
                jnp.where(upper_half, last_row, first_row), "row", [(0, 1), (1, 0)]
            )
            low = jnp.where(upper_half, 0.0, edge)
            high = jnp.where(upper_half, edge, 0.0)
        else:
            low = lax.ppermute(last_row, "row", [(i, i + 1) for i in range(rows - 1)])
            high = lax.ppermute(first_row, "row", [(i + 1, i) for i in range(rows - 1)])
        return call(
            functools.partial(finish_kernel, len(chunks)),
            "finish",
            16,
            struct(cells, width),
            (
                *[chunk["grid"] for chunk in chunks],
                low,
                high,
                shared["factor"],
            ),
            after,
        )

    def factors(i, after):
        shared["factor"] = call(
            functools.partial(factor_kernel, bands, pixels),
            "factor",
            16,
            struct(cells, width, dtype=jnp.float32),
            (
                lookup_bin[0],
                lookup_frac[0],
                vol_kernel[0],
                geo_kernel[0],
                clear_mask[0],
                table,
                brdf_params,
            ),
            after,
            in_specs=[pl.BlockSpec(memory_space=pltpu.VMEM)] * 6 + [smem],
        )
        return shared["factor"]

    steps = dict(s=send, j=join, m=merge, h=halve, g=total, x=factors, f=finish)
    token = None
    for step in ORDER:
        token = steps[step[0]](int(step[1]), token)
    return token.reshape(1, cells, width)


def solution(mesh):
    in_specs = (
        P("tile", "row", None, None),
        P("tile", "row", None, None),
        P("tile", "row", None),
        P("tile", "row", None),
        P("tile", "row", None),
        P(),
        P(),
        P(),
        P("tile", "row", None),
        P("tile", "row", None),
        P(),
        P("tile", "row", None),
        P("tile", "row", None),
        P("tile", "row", None),
    )
    out_specs = P("tile", "row", None)
    return jax.shard_map(
        on_device, mesh=mesh, in_specs=in_specs, out_specs=out_specs, check_vma=False
    )
```

time: 151 us -> 108 us (0.72)
  starting transfers between devices: 53 us -> 33.2 us
  other arithmetic: 9.96 us -> 0.03 us
  local copies, waits for them, and re-layouts: 13.1 us -> 4.69 us
  waiting for transfers between devices: 47 us -> 43 us
    ppermute x6 -> x1, starting transfers between devices: 15.6 us -> 1.59 us  [finish(): lax.ppermute(jnp.where(upper_half, last_row, first_row), 'row', [(0, 1),...]
    ppermute x25 -> x24, starting transfers between devices: 37.4 us -> 31.6 us  [exchange(): return lax.ppermute(array, ('tile', 'row'), pairs)]
    mul x4 -> x0, local copies, waits for them, and re-layouts: 5.03 us -> none  [on_device(): mixing[:, :, None, :, None]]
    squeeze x9 -> x0, local copies, waits for them, and re-layouts: 4.4 us -> none  [the longest x6 4.29 us: on_device(): both = jnp.concatenate([own[k], arrived[k]], axis=0)]
    unnamed x27 -> x33, local copies, waits for them, and re-layouts: 0.82 us -> 4.67 us
    concatenate x16 -> x0, other arithmetic: 3.4 us -> none  [the longest x12 3.1 us: on_device(): both = jnp.concatenate([own[k], arrived[k]], axis=0)]
    ppermute x25 -> x24, waiting for transfers between devices: 43.3 us -> 40.9 us  [exchange(): return lax.ppermute(array, ('tile', 'row'), pairs)]
    ppermute x6 -> x1, waiting for transfers between devices: 3.68 us -> 2.13 us  [finish(): lax.ppermute(jnp.where(upper_half, last_row, first_row), 'row', [(0, 1),...]
  transfers between devices with their start and end apart: 31 -> 25, of which waited for: 12 -> 17; matrix products, arithmetic and copies ran while one was open for 13% -> 0% of each run, Pallas kernels for 18% -> 16%
where the time goes in v2:
time: 108 us
  waiting for transfers between devices  43 us (40%)
  starting transfers between devices  33.2 us (31%)
  Pallas kernels  26.9 us (25%)
  local copies, waits for them, and re-layouts  4.69 us (4%)
    ppermute x24, waiting for transfers between devices, exchange(): return lax.ppermute(array, ('tile', 'row'), pairs)  40.9 us
    ppermute x24, starting transfers between devices, exchange(): return lax.ppermute(array, ('tile', 'row'), pairs)  31.6 us
    pallas_call x26, Pallas kernels, call(): pl.pallas_call(body, out_shape=out_shape, in_specs=specs, out_specs=jax.t...  26.9 us
    unnamed x33, local copies, waits for them, and re-layouts  4.67 us
  transfers between devices with their start and end apart: 25, of which 17 were waited for; matrix products, arithmetic and copies ran while one was open for 0% of the time, Pallas kernels for 16%

profile of v2, /device:TPU:0, one launch (start us, length us, event | category | flops | bytes accessed | tf_op | source)
XLA Modules:
  0.0 108.0 jit_solution(17242395009606894900)
XLA Ops:
  0.0 6.7 %lead.1 = (bf16[304,512]{1,0:T(8,128)(2,1)}, bf16[608,512]{1,0:T(8,128)(2,1)}, bf16[304,512]{1,0:T(8,128)(2,1)}, s32[1,768]{1,0:T(1,128)}, f32[768,128]{1,0:T(8,128)}) custom-call(s32[1]{0:T(128)} %bitcast.refs_0_, f32[2,8,8]{2,1,0:T(8,128)} %refs_0_.5, bf16[768,2048]{1,0:T(8,128)(2,1)} %bitcast.12, s32[1,768]{1,0:T(1,128)} %bitcast.21, s32[1,768]{1,0:T(1,128)} %bitcast.22, ...), custom_call_target="tpu_custom_call" | custom-call | tf_op jit(solution)/shard_map/lead/pallas_call | solution.py:36
  6.7 3.0 %collective-permute-start = (bf16[608,512]{1,0:T(8,128)(2,1)}, bf16[608,512]{1,0:T(8,128)(2,1)S(1)}, u32[]{:S(2)}, u32[]{:S(2)}) collective-permute-start(bf16[608,512]{1,0:T(8,128)(2,1)} %get-tuple-element.53), channel_id=1, source_target_pairs={{0,1},{1,0},{2,6},{3,7},{4,5},{5,4},{6,2},{7,3},{8,9},{9,8},{10,14... | collective-permute-start | bytes 1867784 | tf_op jit(solution)/shard_map/ppermute | solution.py:357
  9.8 1.9 %copy-done = bf16[1,1,768,2048]{3,2,1,0:T(8,128)(2,1)S(1)} copy-done((bf16[1,1,768,2048]{3,2,1,0:T(8,128)(2,1)S(1)}, bf16[1,1,768,2048]{3,2,1,0:T(8,128)(2,1)}, u32[]{:S(2)}) %copy-start) | copy-done | bytes 3145752
  11.7 1.0 copy-done.2
  12.7 1.0 copy-done.4
  13.6 0.7 copy-done.13
  14.3 3.4 %follow.3 = (bf16[288,512]{1,0:T(8,128)(2,1)S(1)}, bf16[576,512]{1,0:T(8,128)(2,1)S(1)}, bf16[288,512]{1,0:T(8,128)(2,1)S(1)}) custom-call(bf16[304,512]{1,0:T(8,128)(2,1)S(1)} %copy-done.4, f32[2,8,8]{2,1,0:T(8,128)S(1)} %copy-done.7, bf16[768,2048]{1,0:T(8,128)(2,1)S(1)} %bitcast.13, s32[1,768]{1,0:T(1,128)S(1)} %copy-done.13, f32[768,128]{1,0:T(8,128)S(1)} %copy-done.2, ...), custom_call_target="tpu_custom_call" | custom-call | tf_op jit(solution)/shard_map/follow/pallas_call | solution.py:36
  17.7 0.1 collective-permute-start.1
  17.8 0.4 collective-permute-done.refs_1_
  18.3 2.1 %collective-permute-start.2 = (bf16[608,512]{1,0:T(8,128)(2,1)S(1)}, bf16[608,512]{1,0:T(8,128)(2,1)S(1)}, u32[]{:S(2)}, u32[]{:S(2)}) collective-permute-start(bf16[608,512]{1,0:T(8,128)(2,1)S(1)} %join.4.unused), channel_id=1, source_target_pairs={{0,4},{1,5},{2,3},{3,2},{4,0},{5,1},{6,7},{7,6},{8,12},{9,13},{10,... | collective-permute-start | bytes 1867784 | tf_op jit(solution)/shard_map/ppermute | solution.py:357
  20.3 3.4 %follow.4 = (bf16[288,512]{1,0:T(8,128)(2,1)S(1)}, bf16[576,512]{1,0:T(8,128)(2,1)S(1)}, bf16[288,512]{1,0:T(8,128)(2,1)S(1)}) custom-call(bf16[608,512]{1,0:T(8,128)(2,1)S(1)} %join.4.unused, f32[2,8,8]{2,1,0:T(8,128)S(1)} %copy-done.7, bf16[768,2048]{1,0:T(8,128)(2,1)S(1)} %bitcast.14, s32[1,768]{1,0:T(1,128)S(1)} %copy-done.13, f32[768,128]{1,0:T(8,128)S(1)} %copy-done.3, ...), custom_call_target="tpu_custom_call" | custom-call | tf_op jit(solution)/shard_map/follow/pallas_call | solution.py:36
  23.7 1.6 %collective-permute-start.5 = (bf16[576,512]{1,0:T(8,128)(2,1)S(1)}, bf16[576,512]{1,0:T(8,128)(2,1)S(1)}, u32[]{:S(2)}, u32[]{:S(2)}) collective-permute-start(bf16[576,512]{1,0:T(8,128)(2,1)S(1)} %get-tuple-element.63), channel_id=1, source_target_pairs={{0,1},{1,0},{2,6},{3,7},{4,5},{5,4},{6,2},{7,3},{8,9},{9,8},{10,14... | collective-permute-start | bytes 1769480 | tf_op jit(solution)/shard_map/ppermute | solution.py:357
  25.3 7.8 %collective-permute-done.1.refs_1_ = bf16[576,512]{1,0:T(8,128)(2,1)S(1)} collective-permute-done((bf16[576,512]{1,0:T(8,128)(2,1)S(1)}, bf16[576,512]{1,0:T(8,128)(2,1)S(1)}, u32[]{:S(2)}, u32[]{:S(2)}) %collective-permute-start.1) | collective-permute-done | bytes 589856 | tf_op jit(solution)/shard_map/ppermute | solution.py:357
  33.2 2.4 %collective-permute-start.7 = (bf16[576,512]{1,0:T(8,128)(2,1)S(1)}, bf16[576,512]{1,0:T(8,128)(2,1)S(1)}, u32[]{:S(2)}, u32[]{:S(2)}) collective-permute-start(bf16[576,512]{1,0:T(8,128)(2,1)S(1)} %join.5.unused), channel_id=1, source_target_pairs={{0,4},{1,5},{2,3},{3,2},{4,0},{5,1},{6,7},{7,6},{8,12},{9,13},{10,... | collective-permute-start | bytes 1769480 | tf_op jit(solution)/shard_map/ppermute | solution.py:357
  35.6 1.3 %merge.4 = (f32[4,128,512]{2,1,0:T(8,128)S(1)}, bf16[2,128,512]{2,1,0:T(8,128)(2,1)S(1)}, bf16[2,128,512]{2,1,0:T(8,128)(2,1)S(1)}, s32[8,1,144]{2,1,0:T(1,128)S(1)}) custom-call(bf16[576,512]{1,0:T(8,128)(2,1)S(1)} %join.5.unused, bf16[304,512]{1,0:T(8,128)(2,1)S(1)} %copy-done.5, bf16[608,512]{1,0:T(8,128)(2,1)S(1)} %collective-permute-done.refs_1_, ...), custom_call_target="tpu_custom_call" | custom-call | tf_op jit(solution)/shard_map/merge/pallas_call | solution.py:36
  36.9 0.1 collective-permute-start.3
  37.0 0.5 collective-permute-start.4
  37.5 1.0 collective-permute-done.3.refs_1_
  38.5 0.4 collective-permute-done.4.refs_2_
  38.9 0.1 halve.8
  39.0 1.8 %collective-permute-start.6 = (bf16[2,128,512]{2,1,0:T(8,128)(2,1)S(1)}, bf16[2,128,512]{2,1,0:T(8,128)(2,1)S(1)}, u32[]{:S(2)}, u32[]{:S(2)}) collective-permute-start(bf16[2,128,512]{2,1,0:T(8,128)(2,1)S(1)} %get-tuple-element.60.unused), channel_id=1, source_target_pairs={{0,8},{1,9},{2,10},{3,11},{4,12},{5,13},{6,14},{7,15},{8,0},{9,1},... | collective-permute-start | bytes 786440 | tf_op jit(solution)/shard_map/ppermute | solution.py:357
  40.8 3.4 %follow.5 = (bf16[288,512]{1,0:T(8,128)(2,1)S(1)}, bf16[576,512]{1,0:T(8,128)(2,1)S(1)}, bf16[288,512]{1,0:T(8,128)(2,1)S(1)}) custom-call(bf16[2,128,512]{2,1,0:T(8,128)(2,1)S(1)} %get-tuple-element.60.unused, f32[2,8,8]{2,1,0:T(8,128)S(1)} %copy-done.7, bf16[768,2048]{1,0:T(8,128)(2,1)S(1)} %bitcast.15, s32[1,768]{1,0:T(1,128)S(1)} %copy-done.13, ...), custom_call_target="tpu_custom_call" | custom-call | tf_op jit(solution)/shard_map/follow/pallas_call | solution.py:36
  44.2 1.6 %collective-permute-start.11 = (bf16[576,512]{1,0:T(8,128)(2,1)S(1)}, bf16[576,512]{1,0:T(8,128)(2,1)S(1)}, u32[]{:S(2)}, u32[]{:S(2)}) collective-permute-start(bf16[576,512]{1,0:T(8,128)(2,1)S(1)} %get-tuple-element.73), channel_id=1, source_target_pairs={{0,1},{1,0},{2,6},{3,7},{4,5},{5,4},{6,2},{7,3},{8,9},{9,8},{10,14... | collective-permute-start | bytes 1769480 | tf_op jit(solution)/shard_map/ppermute | solution.py:357
  45.9 2.0 %collective-permute-start.13 = (bf16[576,512]{1,0:T(8,128)(2,1)S(1)}, bf16[576,512]{1,0:T(8,128)(2,1)S(1)}, u32[]{:S(2)}, u32[]{:S(2)}) collective-permute-start(bf16[576,512]{1,0:T(8,128)(2,1)S(1)} %join.6.unused), channel_id=1, source_target_pairs={{0,4},{1,5},{2,3},{3,2},{4,0},{5,1},{6,7},{7,6},{8,12},{9,13},{10,... | collective-permute-start | bytes 1769480 | tf_op jit(solution)/shard_map/ppermute | solution.py:357
  47.8 0.1 halve.9
  47.9 1.2 %merge.5 = (f32[4,128,512]{2,1,0:T(8,128)S(1)}, bf16[2,128,512]{2,1,0:T(8,128)(2,1)S(1)}, bf16[2,128,512]{2,1,0:T(8,128)(2,1)S(1)}) custom-call(bf16[1,128,512]{2,1,0:T(8,128)(2,1)S(1)} %get-tuple-element.65.unused, bf16[288,512]{1,0:T(8,128)(2,1)S(1)} %get-tuple-element.51.unused.refs_0_, bf16[576,512]{1,0:T(8,128)(2,1)S(1)} %collective-permute-done.1.refs_1_, ...), custom_call_target="tpu_custom_call" | custom-call | tf_op jit(solution)/shard_map/merge/pallas_call | solution.py:36
  49.1 0.1 collective-permute-start.8
  49.2 0.5 collective-permute-start.9
  49.7 1.0 collective-permute-done.8.refs_1_
  50.7 0.4 collective-permute-done.9.refs_2_
  51.1 0.1 halve.10
  51.2 1.6 %collective-permute-start.12 = (bf16[2,128,512]{2,1,0:T(8,128)(2,1)S(1)}, bf16[2,128,512]{2,1,0:T(8,128)(2,1)S(1)}, u32[]{:S(2)}, u32[]{:S(2)}) collective-permute-start(bf16[2,128,512]{2,1,0:T(8,128)(2,1)S(1)} %get-tuple-element.70.unused), channel_id=1, source_target_pairs={{0,8},{1,9},{2,10},{3,11},{4,12},{5,13},{6,14},{7,15},{8,0},{9,1},... | collective-permute-start | bytes 786440 | tf_op jit(solution)/shard_map/ppermute | solution.py:357
  52.8 2.6 %collective-permute-start.10 = (bf16[1,128,512]{2,1,0:T(8,128)(2,1)S(1)}, bf16[1,128,512]{2,1,0:T(8,128)(2,1)S(1)}, u32[]{:S(2)}, u32[]{:S(2)}) collective-permute-start(bf16[1,128,512]{2,1,0:T(8,128)(2,1)S(1)} %get-tuple-element.65.unused), channel_id=1, source_target_pairs={{0,16},{1,17},{2,18},{3,19},{4,20},{5,21},{6,22},{7,23},{8,24},{9,... | collective-permute-start | bytes 393224 | tf_op jit(solution)/shard_map/ppermute | solution.py:357
  55.4 6.1 %collective-permute-done.10.refs_1_ = bf16[1,128,512]{2,1,0:T(8,128)(2,1)S(1)} collective-permute-done((bf16[1,128,512]{2,1,0:T(8,128)(2,1)S(1)}, bf16[1,128,512]{2,1,0:T(8,128)(2,1)S(1)}, u32[]{:S(2)}, u32[]{:S(2)}) %collective-permute-start.10) | collective-permute-done | bytes 131104 | tf_op jit(solution)/shard_map/ppermute | solution.py:357
  61.6 1.3 %collective-permute-start.18 = (bf16[576,512]{1,0:T(8,128)(2,1)S(1)}, bf16[576,512]{1,0:T(8,128)(2,1)S(1)}, u32[]{:S(2)}, u32[]{:S(2)}) collective-permute-start(bf16[576,512]{1,0:T(8,128)(2,1)S(1)} %join.7.unused), channel_id=1, source_target_pairs={{0,4},{1,5},{2,3},{3,2},{4,0},{5,1},{6,7},{7,6},{8,12},{9,13},{10,... | collective-permute-start | bytes 1769480 | tf_op jit(solution)/shard_map/ppermute | solution.py:357
  63.0 0.0 copy-start.15
  63.0 0.0 copy-start.14
  63.0 1.2 %merge.6 = (f32[4,128,512]{2,1,0:T(8,128)S(1)}, bf16[2,128,512]{2,1,0:T(8,128)(2,1)S(1)}, bf16[2,128,512]{2,1,0:T(8,128)(2,1)S(1)}) custom-call(bf16[1,128,512]{2,1,0:T(8,128)(2,1)S(1)} %get-tuple-element.75.unused, bf16[288,512]{1,0:T(8,128)(2,1)S(1)} %get-tuple-element.54.unused.refs_0_, bf16[576,512]{1,0:T(8,128)(2,1)S(1)} %collective-permute-done.5.refs_1_, ...), custom_call_target="tpu_custom_call" | custom-call | tf_op jit(solution)/shard_map/merge/pallas_call | solution.py:36
  64.3 0.1 collective-permute-start.14
  64.3 0.5 collective-permute-start.15
  64.8 1.0 collective-permute-done.14.refs_1_
  65.9 0.4 collective-permute-done.15.refs_2_
  66.2 0.1 halve.12
  66.3 3.6 %collective-permute-start.17 = (bf16[2,128,512]{2,1,0:T(8,128)(2,1)S(1)}, bf16[2,128,512]{2,1,0:T(8,128)(2,1)S(1)}, u32[]{:S(2)}, u32[]{:S(2)}) collective-permute-start(bf16[2,128,512]{2,1,0:T(8,128)(2,1)S(1)} %get-tuple-element.79.unused), channel_id=1, source_target_pairs={{0,8},{1,9},{2,10},{3,11},{4,12},{5,13},{6,14},{7,15},{8,0},{9,1},... | collective-permute-start | bytes 786440 | tf_op jit(solution)/shard_map/ppermute | solution.py:357
  69.9 0.1 collective-permute-start.16
  70.0 8.5 %collective-permute-done.16.refs_1_ = bf16[1,128,512]{2,1,0:T(8,128)(2,1)S(1)} collective-permute-done((bf16[1,128,512]{2,1,0:T(8,128)(2,1)S(1)}, bf16[1,128,512]{2,1,0:T(8,128)(2,1)S(1)}, u32[]{:S(2)}, u32[]{:S(2)}) %collective-permute-start.16) | collective-permute-done | bytes 131104 | tf_op jit(solution)/shard_map/ppermute | solution.py:357
  78.6 0.7 collective-permute-done.17.refs_1_
  79.3 0.0 copy-start.12
  79.4 1.4 %merge.7 = (f32[4,128,512]{2,1,0:T(8,128)S(1)}, bf16[2,128,512]{2,1,0:T(8,128)(2,1)S(1)}, bf16[2,128,512]{2,1,0:T(8,128)(2,1)}) custom-call(bf16[1,128,512]{2,1,0:T(8,128)(2,1)S(1)} %get-tuple-element.82.unused, bf16[288,512]{1,0:T(8,128)(2,1)S(1)} %get-tuple-element.61.unused.refs_0_, bf16[576,512]{1,0:T(8,128)(2,1)S(1)} %collective-permute-done.11.refs_1_, ...), custom_call_target="tpu_custom_call" | custom-call | tf_op jit(solution)/shard_map/merge/pallas_call | solution.py:36
  80.8 0.5 collective-permute-start.20
  81.3 0.1 copy.15.refs_6_
  81.4 1.3 %collective-permute-done.19.refs_1_ = bf16[2,128,512]{2,1,0:T(8,128)(2,1)S(1)} collective-permute-done((bf16[2,128,512]{2,1,0:T(8,128)(2,1)S(1)}, bf16[2,128,512]{2,1,0:T(8,128)(2,1)S(1)}, u32[]{:S(2)}, u32[]{:S(2)}) %collective-permute-start.19) | collective-permute-done | bytes 262176 | tf_op jit(solution)/shard_map/ppermute | solution.py:357
  82.7 0.2 collective-permute-done.20.refs_2_
  82.9 0.1 halve.14
  83.0 1.8 %collective-permute-start.22 = (bf16[2,128,512]{2,1,0:T(8,128)(2,1)S(1)}, bf16[2,128,512]{2,1,0:T(8,128)(2,1)S(1)}, u32[]{:S(2)}, u32[]{:S(2)}) collective-permute-start(bf16[2,128,512]{2,1,0:T(8,128)(2,1)S(1)} %get-tuple-element.86.unused), channel_id=1, source_target_pairs={{0,8},{1,9},{2,10},{3,11},{4,12},{5,13},{6,14},{7,15},{8,0},{9,1},... | collective-permute-start | bytes 786440 | tf_op jit(solution)/shard_map/ppermute | solution.py:357
  84.8 1.1 %collective-permute-start.21 = (bf16[1,128,512]{2,1,0:T(8,128)(2,1)S(1)}, bf16[1,128,512]{2,1,0:T(8,128)(2,1)S(1)}, u32[]{:S(2)}, u32[]{:S(2)}) collective-permute-start(bf16[1,128,512]{2,1,0:T(8,128)(2,1)S(1)} %get-tuple-element.82.unused), channel_id=1, source_target_pairs={{0,16},{1,17},{2,18},{3,19},{4,20},{5,21},{6,22},{7,23},{8,24},{9,... | collective-permute-start | bytes 393224 | tf_op jit(solution)/shard_map/ppermute | solution.py:357
  85.9 7.6 %collective-permute-done.21.refs_1_ = bf16[1,128,512]{2,1,0:T(8,128)(2,1)S(1)} collective-permute-done((bf16[1,128,512]{2,1,0:T(8,128)(2,1)S(1)}, bf16[1,128,512]{2,1,0:T(8,128)(2,1)S(1)}, u32[]{:S(2)}, u32[]{:S(2)}) %collective-permute-start.21) | collective-permute-done | bytes 131104 | tf_op jit(solution)/shard_map/ppermute | solution.py:357
  93.5 0.7 collective-permute-done.22.refs_1_
  94.3 2.7 %collective-permute-start.23 = (bf16[1,128,512]{2,1,0:T(8,128)(2,1)S(1)}, bf16[1,128,512]{2,1,0:T(8,128)(2,1)S(1)}, u32[]{:S(2)}, u32[]{:S(2)}) collective-permute-start(bf16[1,128,512]{2,1,0:T(8,128)(2,1)S(1)} %get-tuple-element.89.unused), channel_id=1, source_target_pairs={{0,16},{1,17},{2,18},{3,19},{4,20},{5,21},{6,22},{7,23},{8,24},{9,... | collective-permute-start | bytes 393224 | tf_op jit(solution)/shard_map/ppermute | solution.py:357
  97.1 2.7 %factor.1.unused.refs_6_ = f32[128,2048]{1,0:T(8,128)S(1)} custom-call(bf16[1,128,512]{2,1,0:T(8,128)(2,1)S(1)} %get-tuple-element.89.unused, s32[128,256]{1,0:T(8,128)S(1)} %bitcast.16, f32[128,256]{1,0:T(8,128)S(1)} %bitcast.17, f32[128,256]{1,0:T(8,128)S(1)} %bitcast.18, f32[128,256]{1,0:T(8,128)S(1)} %bitcast.19, s32[128,256]{1,0:T(8,128)S(1)} %bitcast.20, ...), custom_call_target="tpu_custom_call" | custom-call | tf_op jit(solution)/shard_map/factor/pallas_call | solution.py:36
  99.8 3.3 %collective-permute-done.23.refs_1_ = bf16[1,128,512]{2,1,0:T(8,128)(2,1)S(1)} collective-permute-done((bf16[1,128,512]{2,1,0:T(8,128)(2,1)S(1)}, bf16[1,128,512]{2,1,0:T(8,128)(2,1)S(1)}, u32[]{:S(2)}, u32[]{:S(2)}) %collective-permute-start.23) | collective-permute-done | bytes 131104 | tf_op jit(solution)/shard_map/ppermute | solution.py:357
  103.1 1.6 %collective-permute-start.24 = (f32[1,2048]{1,0:T(1,128)S(1)}, f32[1,2048]{1,0:T(1,128)S(1)}, u32[]{:S(2)}, u32[]{:S(2)}) collective-permute-start(f32[1,2048]{1,0:T(1,128)S(1)} %broadcast_select_fusion.2), channel_id=1, source_target_pairs={{0,1},{1,0},{2,3},{3,2},{4,5},{5,4},{6,7},{7,6},{8,9},{9,8},{10,11... | collective-permute-start | bytes 24584 | tf_op jit(solution)/shard_map/ppermute | solution.py:512
  104.7 2.1 %collective-permute-done.24 = f32[1,2048]{1,0:T(1,128)S(1)} collective-permute-done((f32[1,2048]{1,0:T(1,128)S(1)}, f32[1,2048]{1,0:T(1,128)S(1)}, u32[]{:S(2)}, u32[]{:S(2)}) %collective-permute-start.24) | collective-permute-done | bytes 8224 | tf_op jit(solution)/shard_map/ppermute | solution.py:512
  106.8 1.2 %finish.1 = bf16[128,2048]{1,0:T(8,128)(2,1)} custom-call(f32[128,512]{1,0:T(8,128)S(1)} %total.7.unused.refs_3_, f32[128,512]{1,0:T(8,128)S(1)} %total.4.unused.refs_0_, f32[128,512]{1,0:T(8,128)S(1)} %total.5.unused.refs_1_, f32[128,512]{1,0:T(8,128)S(1)} %total.6.unused.refs_2_, f32[128,512]{1,0:T(8,128)S(1)} %total.7.unused.refs_3_, ...), custom_call_target="tpu_custom_call" | custom-call | tf_op jit(solution)/shard_map/finish/pallas_call | solution.py:36
  (52 shorter events, 0.6 us)
Async XLA Ops:
  0.0 9.8 %copy-start.7 = (f32[2,8,8]{2,1,0:T(8,128)S(1)}, f32[2,8,8]{2,1,0:T(8,128)}, u32[]{:S(2)}) copy-start(f32[2,8,8]{2,1,0:T(8,128)} %refs_0_.5) | copy-start | bytes 1540
  0.0 9.8 %copy-start.1 = (bf16[4,256,256]{2,1,0:T(8,128)(2,1)S(1)}, bf16[4,256,256]{2,1,0:T(8,128)(2,1)}, u32[]{:S(2)}) copy-start(bf16[4,256,256]{2,1,0:T(8,128)(2,1)} %refs_4_.5) | copy-start | bytes 1572868
  6.7 11.5 %collective-permute-start = (bf16[608,512]{1,0:T(8,128)(2,1)}, bf16[608,512]{1,0:T(8,128)(2,1)S(1)}, u32[]{:S(2)}, u32[]{:S(2)}) collective-permute-start(bf16[608,512]{1,0:T(8,128)(2,1)} %get-tuple-element.53), channel_id=1, source_target_pairs={{0,1},{1,0},{2,6},{3,7},{4,5},{5,4},{6,2},{7,3},{8,9},{9,8},{10,14... | collective-permute-start | bytes 1867784 | tf_op jit(solution)/shard_map/ppermute | solution.py:357
  9.8 1.9 %copy-start = (bf16[1,1,768,2048]{3,2,1,0:T(8,128)(2,1)S(1)}, bf16[1,1,768,2048]{3,2,1,0:T(8,128)(2,1)}, u32[]{:S(2)}) copy-start(bf16[1,1,768,2048]{3,2,1,0:T(8,128)(2,1)} %param.14) | copy-start | bytes 9437188
  11.7 1.0 copy-start.2
  12.7 1.0 copy-start.4
  13.6 0.7 copy-start.13
  14.3 3.9 %copy-start.6 = (bf16[304,512]{1,0:T(8,128)(2,1)S(1)}, bf16[304,512]{1,0:T(8,128)(2,1)}, u32[]{:S(2)}) copy-start(bf16[304,512]{1,0:T(8,128)(2,1)} %get-tuple-element.52.refs_0_) | copy-start | bytes 933892
  14.3 6.0 %copy-start.3 = (f32[768,128]{1,0:T(8,128)S(1)}, f32[768,128]{1,0:T(8,128)}, u32[]{:S(2)}) copy-start(f32[768,128]{1,0:T(8,128)} %get-tuple-element.50.refs_3_) | copy-start | bytes 1179652
  17.7 15.4 %collective-permute-start.1 = (bf16[576,512]{1,0:T(8,128)(2,1)S(1)}, bf16[576,512]{1,0:T(8,128)(2,1)S(1)}, u32[]{:S(2)}, u32[]{:S(2)}) collective-permute-start(bf16[576,512]{1,0:T(8,128)(2,1)S(1)} %get-tuple-element.56), channel_id=1, source_target_pairs={{0,1},{1,0},{2,6},{3,7},{4,5},{5,4},{6,2},{7,3},{8,9},{9,8},{10,14... | collective-permute-start | bytes 1769480 | tf_op jit(solution)/shard_map/ppermute | solution.py:357
  18.2 17.4 %copy-start.5 = (bf16[304,512]{1,0:T(8,128)(2,1)S(1)}, bf16[304,512]{1,0:T(8,128)(2,1)}, u32[]{:S(2)}) copy-start(bf16[304,512]{1,0:T(8,128)(2,1)} %get-tuple-element.48.unused.refs_0_) | copy-start | bytes 933892
  18.3 17.3 %collective-permute-start.2 = (bf16[608,512]{1,0:T(8,128)(2,1)S(1)}, bf16[608,512]{1,0:T(8,128)(2,1)S(1)}, u32[]{:S(2)}, u32[]{:S(2)}) collective-permute-start(bf16[608,512]{1,0:T(8,128)(2,1)S(1)} %join.4.unused), channel_id=1, source_target_pairs={{0,4},{1,5},{2,3},{3,2},{4,0},{5,1},{6,7},{7,6},{8,12},{9,13},{10,... | collective-permute-start | bytes 1867784 | tf_op jit(solution)/shard_map/ppermute | solution.py:357
  23.7 22.1 %collective-permute-start.5 = (bf16[576,512]{1,0:T(8,128)(2,1)S(1)}, bf16[576,512]{1,0:T(8,128)(2,1)S(1)}, u32[]{:S(2)}, u32[]{:S(2)}) collective-permute-start(bf16[576,512]{1,0:T(8,128)(2,1)S(1)} %get-tuple-element.63), channel_id=1, source_target_pairs={{0,1},{1,0},{2,6},{3,7},{4,5},{5,4},{6,2},{7,3},{8,9},{9,8},{10,14... | collective-permute-start | bytes 1769480 | tf_op jit(solution)/shard_map/ppermute | solution.py:357
  33.2 14.7 %collective-permute-start.7 = (bf16[576,512]{1,0:T(8,128)(2,1)S(1)}, bf16[576,512]{1,0:T(8,128)(2,1)S(1)}, u32[]{:S(2)}, u32[]{:S(2)}) collective-permute-start(bf16[576,512]{1,0:T(8,128)(2,1)S(1)} %join.5.unused), channel_id=1, source_target_pairs={{0,4},{1,5},{2,3},{3,2},{4,0},{5,1},{6,7},{7,6},{8,12},{9,13},{10,... | collective-permute-start | bytes 1769480 | tf_op jit(solution)/shard_map/ppermute | solution.py:357
  36.9 1.6 %collective-permute-start.3 = (bf16[2,128,512]{2,1,0:T(8,128)(2,1)S(1)}, bf16[2,128,512]{2,1,0:T(8,128)(2,1)S(1)}, u32[]{:S(2)}, u32[]{:S(2)}) collective-permute-start(bf16[2,128,512]{2,1,0:T(8,128)(2,1)S(1)} %get-tuple-element.57.unused), channel_id=1, source_target_pairs={{0,2},{1,3},{2,0},{3,1},{4,6},{5,7},{6,4},{7,5},{8,10},{9,11},{10,... | collective-permute-start | bytes 786440 | tf_op jit(solution)/shard_map/ppermute | solution.py:357
  37.0 1.9 %collective-permute-start.4 = (bf16[2,128,512]{2,1,0:T(8,128)(2,1)S(1)}, bf16[2,128,512]{2,1,0:T(8,128)(2,1)S(1)}, u32[]{:S(2)}, u32[]{:S(2)}) collective-permute-start(bf16[2,128,512]{2,1,0:T(8,128)(2,1)S(1)} %get-tuple-element.59), channel_id=1, source_target_pairs={{0,2},{1,3},{2,0},{3,1},{4,6},{5,7},{6,4},{7,5},{8,10},{9,11},{10,... | collective-permute-start | bytes 786440 | tf_op jit(solution)/shard_map/ppermute | solution.py:357
  39.0 8.8 %collective-permute-start.6 = (bf16[2,128,512]{2,1,0:T(8,128)(2,1)S(1)}, bf16[2,128,512]{2,1,0:T(8,128)(2,1)S(1)}, u32[]{:S(2)}, u32[]{:S(2)}) collective-permute-start(bf16[2,128,512]{2,1,0:T(8,128)(2,1)S(1)} %get-tuple-element.60.unused), channel_id=1, source_target_pairs={{0,8},{1,9},{2,10},{3,11},{4,12},{5,13},{6,14},{7,15},{8,0},{9,1},... | collective-permute-start | bytes 786440 | tf_op jit(solution)/shard_map/ppermute | solution.py:357
  44.2 17.3 %collective-permute-start.11 = (bf16[576,512]{1,0:T(8,128)(2,1)S(1)}, bf16[576,512]{1,0:T(8,128)(2,1)S(1)}, u32[]{:S(2)}, u32[]{:S(2)}) collective-permute-start(bf16[576,512]{1,0:T(8,128)(2,1)S(1)} %get-tuple-element.73), channel_id=1, source_target_pairs={{0,1},{1,0},{2,6},{3,7},{4,5},{5,4},{6,2},{7,3},{8,9},{9,8},{10,14... | collective-permute-start | bytes 1769480 | tf_op jit(solution)/shard_map/ppermute | solution.py:357
  45.9 17.1 %collective-permute-start.13 = (bf16[576,512]{1,0:T(8,128)(2,1)S(1)}, bf16[576,512]{1,0:T(8,128)(2,1)S(1)}, u32[]{:S(2)}, u32[]{:S(2)}) collective-permute-start(bf16[576,512]{1,0:T(8,128)(2,1)S(1)} %join.6.unused), channel_id=1, source_target_pairs={{0,4},{1,5},{2,3},{3,2},{4,0},{5,1},{6,7},{7,6},{8,12},{9,13},{10,... | collective-permute-start | bytes 1769480 | tf_op jit(solution)/shard_map/ppermute | solution.py:357
  49.1 1.6 %collective-permute-start.8 = (bf16[2,128,512]{2,1,0:T(8,128)(2,1)S(1)}, bf16[2,128,512]{2,1,0:T(8,128)(2,1)S(1)}, u32[]{:S(2)}, u32[]{:S(2)}) collective-permute-start(bf16[2,128,512]{2,1,0:T(8,128)(2,1)S(1)} %get-tuple-element.67.unused), channel_id=1, source_target_pairs={{0,2},{1,3},{2,0},{3,1},{4,6},{5,7},{6,4},{7,5},{8,10},{9,11},{10,... | collective-permute-start | bytes 786440 | tf_op jit(solution)/shard_map/ppermute | solution.py:357
  49.2 1.9 %collective-permute-start.9 = (bf16[2,128,512]{2,1,0:T(8,128)(2,1)S(1)}, bf16[2,128,512]{2,1,0:T(8,128)(2,1)S(1)}, u32[]{:S(2)}, u32[]{:S(2)}) collective-permute-start(bf16[2,128,512]{2,1,0:T(8,128)(2,1)S(1)} %get-tuple-element.69), channel_id=1, source_target_pairs={{0,2},{1,3},{2,0},{3,1},{4,6},{5,7},{6,4},{7,5},{8,10},{9,11},{10,... | collective-permute-start | bytes 786440 | tf_op jit(solution)/shard_map/ppermute | solution.py:357
  51.2 11.7 %collective-permute-start.12 = (bf16[2,128,512]{2,1,0:T(8,128)(2,1)S(1)}, bf16[2,128,512]{2,1,0:T(8,128)(2,1)S(1)}, u32[]{:S(2)}, u32[]{:S(2)}) collective-permute-start(bf16[2,128,512]{2,1,0:T(8,128)(2,1)S(1)} %get-tuple-element.70.unused), channel_id=1, source_target_pairs={{0,8},{1,9},{2,10},{3,11},{4,12},{5,13},{6,14},{7,15},{8,0},{9,1},... | collective-permute-start | bytes 786440 | tf_op jit(solution)/shard_map/ppermute | solution.py:357
  52.8 8.7 %collective-permute-start.10 = (bf16[1,128,512]{2,1,0:T(8,128)(2,1)S(1)}, bf16[1,128,512]{2,1,0:T(8,128)(2,1)S(1)}, u32[]{:S(2)}, u32[]{:S(2)}) collective-permute-start(bf16[1,128,512]{2,1,0:T(8,128)(2,1)S(1)} %get-tuple-element.65.unused), channel_id=1, source_target_pairs={{0,16},{1,17},{2,18},{3,19},{4,20},{5,21},{6,22},{7,23},{8,24},{9,... | collective-permute-start | bytes 393224 | tf_op jit(solution)/shard_map/ppermute | solution.py:357
  61.6 17.8 %collective-permute-start.18 = (bf16[576,512]{1,0:T(8,128)(2,1)S(1)}, bf16[576,512]{1,0:T(8,128)(2,1)S(1)}, u32[]{:S(2)}, u32[]{:S(2)}) collective-permute-start(bf16[576,512]{1,0:T(8,128)(2,1)S(1)} %join.7.unused), channel_id=1, source_target_pairs={{0,4},{1,5},{2,3},{3,2},{4,0},{5,1},{6,7},{7,6},{8,12},{9,13},{10,... | collective-permute-start | bytes 1769480 | tf_op jit(solution)/shard_map/ppermute | solution.py:357
  63.0 18.3 %copy-start.15 = (f32[8,3]{0,1:T(4,128)S(1)}, f32[8,3]{0,1:T(4,128)}, u32[]{:S(2)}) copy-start(f32[8,3]{0,1:T(4,128)} %param.24) | copy-start | bytes 292
  63.0 18.4 %copy-start.14 = (f32[8,33]{1,0:T(8,128)S(1)}, f32[8,33]{1,0:T(8,128)}, u32[]{:S(2)}) copy-start(f32[8,33]{1,0:T(8,128)} %param.21) | copy-start | bytes 3172
  64.3 1.6 %collective-permute-start.14 = (bf16[2,128,512]{2,1,0:T(8,128)(2,1)S(1)}, bf16[2,128,512]{2,1,0:T(8,128)(2,1)S(1)}, u32[]{:S(2)}, u32[]{:S(2)}) collective-permute-start(bf16[2,128,512]{2,1,0:T(8,128)(2,1)S(1)} %get-tuple-element.76.unused), channel_id=1, source_target_pairs={{0,2},{1,3},{2,0},{3,1},{4,6},{5,7},{6,4},{7,5},{8,10},{9,11},{10,... | collective-permute-start | bytes 786440 | tf_op jit(solution)/shard_map/ppermute | solution.py:357
  64.3 1.9 %collective-permute-start.15 = (bf16[2,128,512]{2,1,0:T(8,128)(2,1)S(1)}, bf16[2,128,512]{2,1,0:T(8,128)(2,1)S(1)}, u32[]{:S(2)}, u32[]{:S(2)}) collective-permute-start(bf16[2,128,512]{2,1,0:T(8,128)(2,1)S(1)} %get-tuple-element.78), channel_id=1, source_target_pairs={{0,2},{1,3},{2,0},{3,1},{4,6},{5,7},{6,4},{7,5},{8,10},{9,11},{10,... | collective-permute-start | bytes 786440 | tf_op jit(solution)/shard_map/ppermute | solution.py:357
  66.3 13.0 %collective-permute-start.17 = (bf16[2,128,512]{2,1,0:T(8,128)(2,1)S(1)}, bf16[2,128,512]{2,1,0:T(8,128)(2,1)S(1)}, u32[]{:S(2)}, u32[]{:S(2)}) collective-permute-start(bf16[2,128,512]{2,1,0:T(8,128)(2,1)S(1)} %get-tuple-element.79.unused), channel_id=1, source_target_pairs={{0,8},{1,9},{2,10},{3,11},{4,12},{5,13},{6,14},{7,15},{8,0},{9,1},... | collective-permute-start | bytes 786440 | tf_op jit(solution)/shard_map/ppermute | solution.py:357
  69.9 8.7 %collective-permute-start.16 = (bf16[1,128,512]{2,1,0:T(8,128)(2,1)S(1)}, bf16[1,128,512]{2,1,0:T(8,128)(2,1)S(1)}, u32[]{:S(2)}, u32[]{:S(2)}) collective-permute-start(bf16[1,128,512]{2,1,0:T(8,128)(2,1)S(1)} %get-tuple-element.75.unused), channel_id=1, source_target_pairs={{0,16},{1,17},{2,18},{3,19},{4,20},{5,21},{6,22},{7,23},{8,24},{9,... | collective-permute-start | bytes 393224 | tf_op jit(solution)/shard_map/ppermute | solution.py:357
  79.3 17.7 %copy-start.8 = (s32[1,128,256]{2,1,0:T(8,128)S(1)}, s32[1,128,256]{2,1,0:T(8,128)}, u32[]{:S(2)}) copy-start(s32[1,128,256]{2,1,0:T(8,128)} %param.22) | copy-start | bytes 393220
  79.3 17.7 %copy-start.9 = (f32[1,128,256]{2,1,0:T(8,128)S(1)}, f32[1,128,256]{2,1,0:T(8,128)}, u32[]{:S(2)}) copy-start(f32[1,128,256]{2,1,0:T(8,128)} %param.23) | copy-start | bytes 393220
  79.3 17.7 %copy-start.10 = (f32[1,128,256]{2,1,0:T(8,128)S(1)}, f32[1,128,256]{2,1,0:T(8,128)}, u32[]{:S(2)}) copy-start(f32[1,128,256]{2,1,0:T(8,128)} %param.25) | copy-start | bytes 393220
  79.3 17.7 %copy-start.11 = (f32[1,128,256]{2,1,0:T(8,128)S(1)}, f32[1,128,256]{2,1,0:T(8,128)}, u32[]{:S(2)}) copy-start(f32[1,128,256]{2,1,0:T(8,128)} %param.26) | copy-start | bytes 393220
  79.3 17.7 %copy-start.12 = (s32[1,128,256]{2,1,0:T(8,128)S(1)}, s32[1,128,256]{2,1,0:T(8,128)}, u32[]{:S(2)}) copy-start(s32[1,128,256]{2,1,0:T(8,128)} %param.27) | copy-start | bytes 393220
  80.8 1.9 %collective-permute-start.19 = (bf16[2,128,512]{2,1,0:T(8,128)(2,1)S(1)}, bf16[2,128,512]{2,1,0:T(8,128)(2,1)S(1)}, u32[]{:S(2)}, u32[]{:S(2)}) collective-permute-start(bf16[2,128,512]{2,1,0:T(8,128)(2,1)S(1)} %get-tuple-element.83.unused), channel_id=1, source_target_pairs={{0,2},{1,3},{2,0},{3,1},{4,6},{5,7},{6,4},{7,5},{8,10},{9,11},{10,... | collective-permute-start | bytes 786440 | tf_op jit(solution)/shard_map/ppermute | solution.py:357
  80.8 2.1 %collective-permute-start.20 = (bf16[2,128,512]{2,1,0:T(8,128)(2,1)}, bf16[2,128,512]{2,1,0:T(8,128)(2,1)S(1)}, u32[]{:S(2)}, u32[]{:S(2)}) collective-permute-start(bf16[2,128,512]{2,1,0:T(8,128)(2,1)} %get-tuple-element.85), channel_id=1, source_target_pairs={{0,2},{1,3},{2,0},{3,1},{4,6},{5,7},{6,4},{7,5},{8,10},{9,11},{10,... | collective-permute-start | bytes 786440 | tf_op jit(solution)/shard_map/ppermute | solution.py:357
  83.0 11.2 %collective-permute-start.22 = (bf16[2,128,512]{2,1,0:T(8,128)(2,1)S(1)}, bf16[2,128,512]{2,1,0:T(8,128)(2,1)S(1)}, u32[]{:S(2)}, u32[]{:S(2)}) collective-permute-start(bf16[2,128,512]{2,1,0:T(8,128)(2,1)S(1)} %get-tuple-element.86.unused), channel_id=1, source_target_pairs={{0,8},{1,9},{2,10},{3,11},{4,12},{5,13},{6,14},{7,15},{8,0},{9,1},... | collective-permute-start | bytes 786440 | tf_op jit(solution)/shard_map/ppermute | solution.py:357
  84.8 8.7 %collective-permute-start.21 = (bf16[1,128,512]{2,1,0:T(8,128)(2,1)S(1)}, bf16[1,128,512]{2,1,0:T(8,128)(2,1)S(1)}, u32[]{:S(2)}, u32[]{:S(2)}) collective-permute-start(bf16[1,128,512]{2,1,0:T(8,128)(2,1)S(1)} %get-tuple-element.82.unused), channel_id=1, source_target_pairs={{0,16},{1,17},{2,18},{3,19},{4,20},{5,21},{6,22},{7,23},{8,24},{9,... | collective-permute-start | bytes 393224 | tf_op jit(solution)/shard_map/ppermute | solution.py:357
  94.3 8.7 %collective-permute-start.23 = (bf16[1,128,512]{2,1,0:T(8,128)(2,1)S(1)}, bf16[1,128,512]{2,1,0:T(8,128)(2,1)S(1)}, u32[]{:S(2)}, u32[]{:S(2)}) collective-permute-start(bf16[1,128,512]{2,1,0:T(8,128)(2,1)S(1)} %get-tuple-element.89.unused), channel_id=1, source_target_pairs={{0,16},{1,17},{2,18},{3,19},{4,20},{5,21},{6,22},{7,23},{8,24},{9,... | collective-permute-start | bytes 393224 | tf_op jit(solution)/shard_map/ppermute | solution.py:357
  103.1 3.7 %collective-permute-start.24 = (f32[1,2048]{1,0:T(1,128)S(1)}, f32[1,2048]{1,0:T(1,128)S(1)}, u32[]{:S(2)}, u32[]{:S(2)}) collective-permute-start(f32[1,2048]{1,0:T(1,128)S(1)} %broadcast_select_fusion.2), channel_id=1, source_target_pairs={{0,1},{1,0},{2,3},{3,2},{4,5},{5,4},{6,7},{7,6},{8,9},{9,8},{10,11... | collective-permute-start | bytes 24584 | tf_op jit(solution)/shard_map/ppermute | solution.py:512

commit v3 on v2

--- a/solution.py
+++ b/solution.py
@@ -13,9 +13,35 @@
 GROUP = 32
 TAG_ROWS = 16
 CHUNKS = ((0, 2), (2, 4), (4, 6), (6, 8))
-ORDER = ("s0", "s1", "j0", "s2", "j1", "m0", "h0", "s3", "j2", "h0", "m1", "h1", "g0", "j3", "h1", "m2", "h2", "g1", "h2", "m3", "h3", "g2", "h3", "x0", "g3", "f0")
+ORDER = (
+    "s0",
+    "k0",
+    "s1",
+    "k1",
+    "j0",
+    "s2",
+    "s3",
+    "k2",
+    "j1",
+    "m0",
+    "h0",
+    "k3",
+    "j2",
+    "m1",
+    "h1",
+    "g0",
+    "j3",
+    "m2",
+    "g1",
+    "h2",
+    "m3",
+    "g2",
+    "h3",
+    "x0",
+    "f0",
+)
 UNROLL = 6
-SPLIT = (2, 1, 1)
+SPLIT = (1, 1)
 MIB = 1024 * 1024
 
 
@@ -71,10 +97,11 @@
     rel_z = lax.shift_right_logical(relative, shift + 2)
     chip = rel_x * rows + rel_y
     if rows == 2:
-        core = lax.shift_right_logical(me, shift) & 1
+        core = lax.shift_right_logical(footprint, shift) & 1
         swap = jnp.logical_and(core == 1, jnp.logical_or(chip == 1, chip == 2))
         chip = jnp.where(swap, 3 - chip, chip)
-    return rel_z, chip * 2 + rel_core
+        chip = jnp.bitwise_xor(chip, lax.shift_right_logical(chip, 1))
+    return rel_z, rel_core * 2 * rows + chip
 
 
 def resample(shape, chunk, offset_ref, x_ref, wait, code_cols, weights_ref, banded_ref, result_ref):
@@ -127,14 +154,14 @@
         result_ref[:, b * pixels : (b + 1) * pixels] = total.astype(jnp.bfloat16)
 
 
-def pack(position, slots, layout, result_ref, out_refs, tags=None):
+def pack(position, slots, peers, result_ref, out_refs, tags=None):
     blocks = result_ref.shape[0]
-    for chips, ref in zip(layout, out_refs):
-        height = ref.shape[0] // len(chips)
-        for i, k in enumerate(chips):
-            ids = lax.broadcasted_iota(jnp.int32, (slots, blocks), 0) + k * slots
+    height = out_refs[0].shape[0] // peers
+    for core, ref in enumerate(out_refs):
+        for k in range(peers):
+            ids = lax.broadcasted_iota(jnp.int32, (slots, blocks), 0) + (core * peers + k) * slots
             chosen = one_hot(ids == position)
-            start = i * height
+            start = k * height
             ref[start : start + slots, :] = dot(chosen, result_ref[...]).astype(jnp.bfloat16)
             if tags is not None:
                 start, stop = start + slots, start + height
@@ -145,11 +172,10 @@
 
 
 def lead_kernel(shape, chunk, *refs):
-    bands, pixels, rows, depth, slots, peers, layout = shape
-    count = len(layout)
-    ins, outs, scratch = refs[:8], refs[8 : 10 + count], refs[10 + count :]
+    bands, pixels, rows, depth, slots, peers = shape
+    ins, outs, scratch = refs[:8], refs[8:12], refs[12:]
     me_ref = ins[0]
-    position_ref, code_cols = outs[count:]
+    position_ref, code_cols = outs[2:]
     offset, x, foot, cell, pick, sensor, weights, banded_ref, result_ref, sems = scratch
     blocks = x.shape[0]
     tiles = weights.shape[0]
@@ -183,7 +209,7 @@
     )
     before = dot(member.astype(jnp.bfloat16), one_hot(earlier))
     rank = jnp.sum(member * before, axis=0, keepdims=True).astype(jnp.int32)
-    position = group * (slots // 2) + rank
+    position = group * slots + rank
     position_ref[...] = position
     line = lax.broadcasted_iota(jnp.int32, (TAG_ROWS, blocks), 0)
     tags = jnp.where(line == 0, cell[...] + 1, jnp.where(line == 1, place, 0))
@@ -195,14 +221,13 @@
             matrices.wait()
 
     resample(shape, chunk, offset, x, wait, code_cols, weights, banded_ref, result_ref)
-    pack(position, slots, layout, result_ref, outs[:count], tags)
+    pack(position, slots, peers, result_ref, outs[:2], tags)
 
 
 def follow_kernel(shape, chunk, *refs):
-    slots, layout = shape[4], shape[6]
-    count = len(layout)
+    slots, peers = shape[4:]
     offset_ref, x_ref, position_ref, code_cols, weights_ref = refs[:5]
-    outs, (banded_ref, result_ref) = refs[5 : 5 + count], refs[5 + count :]
+    outs, (banded_ref, result_ref) = refs[5:7], refs[7:]
     resample(
         shape,
         chunk,
@@ -214,13 +239,24 @@
         banded_ref,
         result_ref,
     )
-    pack(position_ref[...], slots, layout, result_ref, outs)
-
-
-def join_kernel(own_ref, arrived_ref, out_ref):
-    height = own_ref.shape[0]
-    out_ref[:height, :] = own_ref[...]
-    out_ref[height:, :] = arrived_ref[height:, :]
+    pack(position_ref[...], slots, peers, result_ref, outs)
+
+
+def fold_kernel(picks, peers, mine_ref, crossed_ref, *outs):
+    height = mine_ref.shape[0] // peers
+    for parts, ref in zip(picks, outs):
+        start = 0
+        for k in parts:
+            for source in (mine_ref, crossed_ref):
+                ref[start : start + height, :] = source[k * height : (k + 1) * height, :]
+                start += height
+
+
+def join_kernel(peers, mine_ref, crossed_ref, arrived_ref, out_ref):
+    height = mine_ref.shape[0] // peers
+    out_ref[:height, :] = mine_ref[-height:, :]
+    out_ref[height : 2 * height, :] = crossed_ref[-height:, :]
+    out_ref[2 * height :, :] = arrived_ref[2 * height :, :]
 
 
 def put(refs, planes):
@@ -237,28 +273,23 @@
         keep_ref, *sends, keys_ref = refs[count:]
     else:
         keys_ref, keep_ref, *sends = refs[count:]
-    depth, columns = keep_ref.shape[0], keep_ref.shape[2]
-    half = slots // 2
-    ids = lax.broadcasted_iota(jnp.int32, (depth * cells, half), 0)
-    for h in (1, 0):
-        total = None
-        for i, (j, start) in enumerate(parts):
-            if lead:
-                tag = rows[j][start + slots : start + slots + TAG_ROWS, h * half : (h + 1) * half]
-                tag = tag.astype(jnp.float32)
-                cell, place = tag[0:1].astype(jnp.int32), tag[1:2].astype(jnp.int32)
-                key = place * cells + cell - 1
-                keys_ref[2 * i + h] = key
-            else:
-                key = keys_ref[2 * i + h]
-            first = start + h * half
-            part = dot(one_hot(ids == key), rows[j][first : first + half, :])
-            total = part if total is None else total + part
-        total = total.reshape(depth, cells, columns)
-        if h == 0:
-            keep_ref[...] = total
+    depth, columns = 2 * keep_ref.shape[0], keep_ref.shape[2]
+    ids = lax.broadcasted_iota(jnp.int32, (depth * cells, slots), 0)
+    total = None
+    for i, (j, start) in enumerate(parts):
+        stop = start + slots
+        if lead:
+            tag = rows[j][stop : stop + TAG_ROWS, :slots].astype(jnp.float32)
+            cell, place = tag[0:1].astype(jnp.int32), tag[1:2].astype(jnp.int32)
+            key = place * cells + cell - 1
+            keys_ref[i] = key
         else:
-            put(sends, total.astype(jnp.bfloat16))
+            key = keys_ref[i]
+        part = dot(one_hot(ids == key), rows[j][start:stop, :])
+        total = part if total is None else total + part
+    total = total.reshape(depth // 2, 2, cells, columns)
+    keep_ref[...] = total[:, 0]
+    put(sends, total[:, 1].astype(jnp.bfloat16))
 
 
 def halve_kernel(count, *refs):
@@ -311,10 +342,16 @@
 
 
 def finish_kernel(count, *refs):
-    grids, (low_ref, high_ref, factor_ref, out_ref) = refs[:count], refs[count:]
+    grids, arrived_ref, (low_ref, high_ref, factor_ref, out_ref) = (
+        refs[:count],
+        refs[count],
+        refs[count + 1 :],
+    )
     start = 0
-    for grid_ref in grids:
+    for i, grid_ref in enumerate(grids):
         grid = grid_ref[...]
+        if i == count - 1:
+            grid = grid[0] + arrived_ref[...].astype(jnp.float32).reshape(grid.shape[1:])
         here = slice(start, start + grid.shape[1])
         before = jnp.concatenate([low_ref[:, here], grid[:-1]], axis=0)
         after = jnp.concatenate([grid[1:], high_ref[:, here]], axis=0)
@@ -348,7 +385,7 @@
     capacity = max(2, 3 * blocks // (2 * devices))
     depth = tiles // 4
     peers = 2 * rows
-    slots = 2 * depth * capacity
+    slots = depth * capacity
     bits = dict(z=4 * rows, x=2 * rows, core=rows, y=1)
 
     def exchange(array, flip, other=None):
@@ -362,11 +399,10 @@
     me = lax.axis_index("tile") * rows + lax.axis_index("row")
     smem = pl.BlockSpec(memory_space=pltpu.SMEM)
     hbm = pl.BlockSpec(memory_space=pltpu.HBM)
-    layout = ((0,), (1, 3), (2,)) if rows == 2 else tuple((k,) for k in range(peers))
-    shape = (bands, pixels, rows, depth, slots, peers, layout)
+    shape = (bands, pixels, rows, depth, slots, peers)
     x = swath_blocks.reshape(blocks, width)
     table = jnp.pad(lookup_table, ((0, 0), (0, 128 - lookup_table.shape[1])))
-    flips = [bits["core"]] + [bits["z"] << i for i in range(depth.bit_length() - 1)]
+    picks = ((1, 2),) if rows == 2 else tuple((k,) for k in range(1, peers))
     shared = {}
     chunks = [dict(hops=0) for _ in CHUNKS]
 
@@ -377,13 +413,13 @@
         begin, end = CHUNKS[i]
         columns = (end - begin) * pixels
         height = slots + (0 if i else TAG_ROWS)
-        payload = [struct(len(chips) * height, columns) for chips in layout]
+        payload = [struct(peers * height, columns)] * 2
         work = [
             pltpu.VMEM((end - begin, blocks, pixels), jnp.bfloat16),
             pltpu.VMEM((blocks, columns), jnp.bfloat16),
         ]
         if i == 0:
-            *lists, shared["position"], shared["codes"] = call(
+            mine, cross, shared["position"], shared["codes"] = call(
                 functools.partial(lead_kernel, shape, CHUNKS[i]),
                 "lead",
                 63,
@@ -411,7 +447,7 @@
                 ],
             )
         else:
-            lists = call(
+            mine, cross = call(
                 functools.partial(follow_kernel, shape, CHUNKS[i]),
                 "follow",
                 28,
@@ -421,47 +457,68 @@
                 scalars=1,
                 scratch_shapes=work,
             )
+        chunks[i]["mine"], chunks[i]["crossed"] = mine, exchange(cross, bits["core"])
+        return mine
+
+    def fold(i, after):
+        chunk = chunks[i]
+        mine, crossed = chunk["mine"], chunk["crossed"]
+        height, columns = mine.shape[0] // peers, mine.shape[1]
+        outs = call(
+            functools.partial(fold_kernel, picks, peers),
+            "fold",
+            16,
+            [struct(2 * len(parts) * height, columns) for parts in picks],
+            (mine, crossed),
+            after,
+        )
         if rows == 2:
-            own, first, chunks[i]["second"] = lists
-            chunks[i]["lists"] = [own, exchange(first, bits["y"], bits["x"])]
+            arrived = [exchange(outs[0], bits["y"], bits["x"])]
         else:
-            chunks[i]["lists"] = [
-                array if k == 0 else exchange(array, chip_flip(k)) for k, array in enumerate(lists)
-            ]
-        chunks[i]["parts"] = [(k, 0) for k in range(len(lists))]
-        return lists[0]
+            arrived = [exchange(array, chip_flip(k + 1)) for k, array in enumerate(outs)]
+        chunk["lists"] = [mine, crossed, *arrived]
+        chunk["parts"] = [(0, 0), (1, 0)]
+        for k in range(len(arrived)):
+            chunk["parts"] += [(k + 2, 0), (k + 2, height)]
+        return outs[0]
 
     def join(i, after):
         if rows != 2:
             return after
         chunk = chunks[i]
-        arrived = chunk["lists"][1]
-        height, columns = arrived.shape
+        arrived = chunk["lists"][2]
         both = call(
-            join_kernel, "join", 16, struct(height, columns), (chunk["second"], arrived), after
+            functools.partial(join_kernel, peers),
+            "join",
+            16,
+            struct(*arrived.shape),
+            chunk["lists"],
+            after,
         )
         chunk["lists"].append(exchange(both, bits["x"], bits["y"]))
-        chunk["parts"] = [(0, 0), (1, 0), (2, 0), (2, height // 2)]
+        chunk["parts"] += [(3, k * (arrived.shape[0] // 4)) for k in range(4)]
         return both
 
     def forward(i, keep, sends):
         chunk = chunks[i]
         chunk["keep"] = keep
-        chunk["arrived"] = [exchange(array, flips[chunk["hops"]]) for array in sends]
+        chunk["away"] = sends[-1]
+        chunk["arrived"] = [exchange(array, bits["z"] << chunk["hops"]) for array in sends]
         chunk["hops"] += 1
         return sends[0]
 
     def pieces(hop, planes, columns):
-        count = min(planes, SPLIT[min(hop, 2)])
+        count = min(planes, SPLIT[min(hop, 1)])
         return [struct(planes // count, cells, columns)] * count
 
     def merge(i, after):
         arrays = chunks[i]["lists"]
         columns = arrays[0].shape[1]
         parts = chunks[i]["parts"]
-        outs = [struct(depth, cells, columns, dtype=jnp.float32), *pieces(0, depth, columns)]
+        outs = [struct(depth // 2, cells, columns, dtype=jnp.float32)]
+        outs += pieces(0, depth // 2, columns)
         if i == 0:
-            outs.append(struct(2 * peers, 1, slots // 2, dtype=jnp.int32))
+            outs.append(struct(2 * peers, 1, slots, dtype=jnp.int32))
         outs = call(
             functools.partial(merge_kernel, i == 0, slots, cells, parts),
             "merge",
@@ -505,29 +562,54 @@
         return chunk["grid"]
 
     def finish(i, after):
-        first_row = jnp.concatenate([chunk["grid"][:1] for chunk in chunks], axis=1)
-        last_row = jnp.concatenate([chunk["grid"][-1:] for chunk in chunks], axis=1)
+        *early, final = chunks
+        for i in range(len(chunks)):
+            while chunks[i]["keep"].shape[0] > 1:
+                after = halve(i, after)
+            if i < len(early) and "grid" not in chunks[i]:
+                after = total(i, after)
+        keep, arrived = final["keep"], final["arrived"][0].reshape(cells, -1)
+        away = final["away"].reshape(cells, -1)
+
+        def ends(array):
+            return array[:1], array[-1:]
+
+        parts = []
+        for pick in (0, 1):
+            kept = [ends(chunk["grid"])[pick] for chunk in early] + [ends(keep[0])[pick]]
+            parts.append((jnp.concatenate(kept, axis=1), ends(away)[pick]))
+        width_early = width - arrived.shape[1]
+        hop = bits["z"] << (final["hops"] - 1)
+
+        def beside(kept, coming):
+            coming = jnp.pad(coming.astype(jnp.float32), ((0, 0), (width_early, 0)))
+            return kept + coming
+
         if rows == 2:
-            upper_half = lax.axis_index("row") == 0
-            edge = lax.ppermute(
-                jnp.where(upper_half, last_row, first_row), "row", [(0, 1), (1, 0)]
+            upper = lax.axis_index("row") == 0
+            kept = jnp.where(upper, parts[1][0], parts[0][0])
+            coming = jnp.where(upper, parts[1][1], parts[0][1])
+            row = beside(exchange(kept, 1), exchange(coming, hop ^ 1))
+            low, high = jnp.where(upper, 0.0, row), jnp.where(upper, row, 0.0)
+        else:
+            up = [(i, i + 1) for i in range(rows - 1)]
+            down = [(i + 1, i) for i in range(rows - 1)]
+            across = [(t * rows + r, (t * rows + r) ^ hop) for t in range(tiles) for r in range(rows)]
+            low_pairs = [(i, j + 1) for i, j in across if j % rows < rows - 1]
+            high_pairs = [(i, j - 1) for i, j in across if j % rows > 0]
+            axes = ("tile", "row")
+            low = beside(
+                lax.ppermute(parts[1][0], "row", up), lax.ppermute(parts[1][1], axes, low_pairs)
             )
-            low = jnp.where(upper_half, 0.0, edge)
-            high = jnp.where(upper_half, edge, 0.0)
-        else:
-            low = lax.ppermute(last_row, "row", [(i, i + 1) for i in range(rows - 1)])
-            high = lax.ppermute(first_row, "row", [(i + 1, i) for i in range(rows - 1)])
+            high = beside(
+                lax.ppermute(parts[0][0], "row", down), lax.ppermute(parts[0][1], axes, high_pairs)
+            )
         return call(
             functools.partial(finish_kernel, len(chunks)),
             "finish",
             16,
             struct(cells, width),
-            (
-                *[chunk["grid"] for chunk in chunks],
-                low,
-                high,
-                shared["factor"],
-            ),
+            (*[chunk["grid"] for chunk in early], keep, arrived, low, high, shared["factor"]),
             after,
         )
 
@@ -551,7 +633,7 @@
         )
         return shared["factor"]
 
-    steps = dict(s=send, j=join, m=merge, h=halve, g=total, x=factors, f=finish)
+    steps = dict(s=send, k=fold, j=join, m=merge, h=halve, g=total, x=factors, f=finish)
     token = None
     for step in ORDER:
         token = steps[step[0]](int(step[1]), token)

time: 108 us -> 108 us (level)
  waiting for transfers between devices: 43 us -> 37.8 us
  local copies, waits for them, and re-layouts: 4.69 us -> 8.44 us
  Pallas kernels: 26.9 us -> 29.4 us
  starting transfers between devices: 33.2 us -> 31.4 us
    unnamed x33, local copies, waits for them, and re-layouts: 4.67 us -> 8.41 us
    ppermute x24 -> x22, waiting for transfers between devices: 40.9 us -> 37.8 us  [exchange(): return lax.ppermute(array, ('tile', 'row'), pairs)]
    pallas_call x26 -> x25, Pallas kernels: 26.9 us -> 29.4 us  [call(): pl.pallas_call(body, out_shape=out_shape, in_specs=specs, out_specs=jax.t...]
    ppermute x1 -> x0, waiting for transfers between devices: 2.13 us -> none  [finish(): lax.ppermute(jnp.where(upper_half, last_row, first_row), 'row', [(0, 1),...]
    ppermute x1 -> x0, starting transfers between devices: 1.59 us -> none  [finish(): lax.ppermute(jnp.where(upper_half, last_row, first_row), 'row', [(0, 1),...]
    ppermute x24 -> x22, starting transfers between devices: 31.6 us -> 31.4 us  [exchange(): return lax.ppermute(array, ('tile', 'row'), pairs)]
  transfers between devices with their start and end apart: 25 -> 22, of which waited for: 17 -> 10; matrix products, arithmetic and copies ran while one was open for 0% -> 0% of each run, Pallas kernels for 16% -> 20%
where the time goes in v3:
time: 108 us; the launch traced here: 107 us
  waiting for transfers between devices  37.8 us (35%)
  starting transfers between devices  31.4 us (29%)
  Pallas kernels  29.4 us (27%)
  local copies, waits for them, and re-layouts  8.44 us (8%)
    ppermute x22, waiting for transfers between devices, exchange(): return lax.ppermute(array, ('tile', 'row'), pairs)  37.8 us
    ppermute x22, starting transfers between devices, exchange(): return lax.ppermute(array, ('tile', 'row'), pairs)  31.4 us
    pallas_call x25, Pallas kernels, call(): pl.pallas_call(body, out_shape=out_shape, in_specs=specs, out_specs=jax.t...  29.4 us
    unnamed x33, local copies, waits for them, and re-layouts  8.41 us
  transfers between devices with their start and end apart: 22, of which 10 were waited for; matrix products, arithmetic and copies ran while one was open for 0% of the time, Pallas kernels for 20%

profile of v3, /device:TPU:0, one launch (start us, length us, event | category | flops | bytes accessed | tf_op | source)
XLA Modules:
  0.0 107.4 jit_solution(11765904557326463843)
XLA Ops:
  0.0 6.9 %lead.1 = (bf16[640,512]{1,0:T(8,128)(2,1)}, bf16[640,512]{1,0:T(8,128)(2,1)}, s32[1,768]{1,0:T(1,128)}, f32[768,128]{1,0:T(8,128)}) custom-call(s32[1]{0:T(128)} %bitcast.refs_0_, f32[2,8,8]{2,1,0:T(8,128)} %refs_0_.5, bf16[768,2048]{1,0:T(8,128)(2,1)} %bitcast.19, s32[1,768]{1,0:T(1,128)} %bitcast.29, s32[1,768]{1,0:T(1,128)} %bitcast.30, ...), custom_call_target="tpu_custom_call" | custom-call | tf_op jit(solution)/shard_map/lead/pallas_call | solution.py:62
  6.9 0.5 collective-permute-start
  7.4 1.9 %collective-permute-done.refs_1_ = bf16[640,512]{1,0:T(8,128)(2,1)S(1)} collective-permute-done((bf16[640,512]{1,0:T(8,128)(2,1)}, bf16[640,512]{1,0:T(8,128)(2,1)S(1)}, u32[]{:S(2)}, u32[]{:S(2)}) %collective-permute-start) | collective-permute-done | bytes 655392 | tf_op jit(solution)/shard_map/ppermute | solution.py:394
  9.4 1.1 %copy-done.1 = bf16[640,512]{1,0:T(8,128)(2,1)S(1)} copy-done((bf16[640,512]{1,0:T(8,128)(2,1)S(1)}, bf16[640,512]{1,0:T(8,128)(2,1)}, u32[]{:S(2)}) %copy-start.1) | copy-done | bytes 655384
  10.5 2.9 %collective-permute-start.2 = (bf16[640,512]{1,0:T(8,128)(2,1)S(1)}, bf16[640,512]{1,0:T(8,128)(2,1)S(1)}, u32[]{:S(2)}, u32[]{:S(2)}) collective-permute-start(bf16[640,512]{1,0:T(8,128)(2,1)S(1)} %fold.4.unused), channel_id=1, source_target_pairs={{0,1},{1,0},{2,6},{3,7},{4,5},{5,4},{6,2},{7,3},{8,9},{9,8},{10,14... | collective-permute-start | bytes 1966088 | tf_op jit(solution)/shard_map/ppermute | solution.py:394
  13.4 1.9 %copy-done = bf16[1,1,768,2048]{3,2,1,0:T(8,128)(2,1)S(1)} copy-done((bf16[1,1,768,2048]{3,2,1,0:T(8,128)(2,1)S(1)}, bf16[1,1,768,2048]{3,2,1,0:T(8,128)(2,1)}, u32[]{:S(2)}) %copy-start) | copy-done | bytes 3145752
  15.3 1.0 copy-done.4
  16.3 0.7 copy-done.13
  17.0 3.5 %follow.3 = (bf16[576,512]{1,0:T(8,128)(2,1)S(1)}, bf16[576,512]{1,0:T(8,128)(2,1)S(1)}) custom-call(bf16[640,512]{1,0:T(8,128)(2,1)S(1)} %fold.4.unused, f32[2,8,8]{2,1,0:T(8,128)S(1)} %copy-done.7, bf16[768,2048]{1,0:T(8,128)(2,1)S(1)} %bitcast.20, s32[1,768]{1,0:T(1,128)S(1)} %copy-done.13, f32[768,128]{1,0:T(8,128)S(1)} %copy-done.4, ...), custom_call_target="tpu_custom_call" | custom-call | tf_op jit(solution)/shard_map/follow/pallas_call | solution.py:62
  20.5 0.1 collective-permute-start.1
  20.5 2.0 %collective-permute-done.1.refs_1_ = bf16[576,512]{1,0:T(8,128)(2,1)S(1)} collective-permute-done((bf16[576,512]{1,0:T(8,128)(2,1)S(1)}, bf16[576,512]{1,0:T(8,128)(2,1)S(1)}, u32[]{:S(2)}, u32[]{:S(2)}) %collective-permute-start.1) | collective-permute-done | bytes 589856 | tf_op jit(solution)/shard_map/ppermute | solution.py:394
  22.6 0.0 collective-permute-done.2.refs_2_
  22.7 1.6 %collective-permute-start.5 = (bf16[640,512]{1,0:T(8,128)(2,1)S(1)}, bf16[640,512]{1,0:T(8,128)(2,1)S(1)}, u32[]{:S(2)}, u32[]{:S(2)}) collective-permute-start(bf16[640,512]{1,0:T(8,128)(2,1)S(1)} %join.4.unused), channel_id=1, source_target_pairs={{0,4},{1,5},{2,3},{3,2},{4,0},{5,1},{6,7},{7,6},{8,12},{9,13},{10,... | collective-permute-start | bytes 1966088 | tf_op jit(solution)/shard_map/ppermute | solution.py:394
  24.2 3.5 %follow.4 = (bf16[576,512]{1,0:T(8,128)(2,1)S(1)}, bf16[576,512]{1,0:T(8,128)(2,1)S(1)}) custom-call(bf16[640,512]{1,0:T(8,128)(2,1)S(1)} %join.4.unused, f32[2,8,8]{2,1,0:T(8,128)S(1)} %copy-done.7, bf16[768,2048]{1,0:T(8,128)(2,1)S(1)} %bitcast.21, s32[1,768]{1,0:T(1,128)S(1)} %copy-done.13, f32[768,128]{1,0:T(8,128)S(1)} %copy-done.4, ...), custom_call_target="tpu_custom_call" | custom-call | tf_op jit(solution)/shard_map/follow/pallas_call | solution.py:62
  27.7 0.1 collective-permute-start.3
  27.8 1.5 %collective-permute-start.4 = (bf16[576,512]{1,0:T(8,128)(2,1)S(1)}, bf16[576,512]{1,0:T(8,128)(2,1)S(1)}, u32[]{:S(2)}, u32[]{:S(2)}) collective-permute-start(bf16[576,512]{1,0:T(8,128)(2,1)S(1)} %fold.5.unused), channel_id=1, source_target_pairs={{0,1},{1,0},{2,6},{3,7},{4,5},{5,4},{6,2},{7,3},{8,9},{9,8},{10,14... | collective-permute-start | bytes 1769480 | tf_op jit(solution)/shard_map/ppermute | solution.py:394
  29.2 3.5 %follow.5 = (bf16[576,512]{1,0:T(8,128)(2,1)S(1)}, bf16[576,512]{1,0:T(8,128)(2,1)S(1)}) custom-call(bf16[576,512]{1,0:T(8,128)(2,1)S(1)} %get-tuple-element.38.unused.refs_0_, f32[2,8,8]{2,1,0:T(8,128)S(1)} %copy-done.7, bf16[768,2048]{1,0:T(8,128)(2,1)S(1)} %bitcast.22, s32[1,768]{1,0:T(1,128)S(1)} %copy-done.13, f32[768,128]{1,0:T(8,128)S(1)} %copy-done.4, ...), custom_call_target="tpu_custom_call" | custom-call | tf_op jit(solution)/shard_map/follow/pallas_call | solution.py:62
  32.7 0.1 collective-permute-start.7
  32.8 0.0 collective-permute-done.3.refs_1_
  32.8 0.7 collective-permute-start.8
  33.6 5.2 %collective-permute-done.4.refs_2_ = bf16[576,512]{1,0:T(8,128)(2,1)S(1)} collective-permute-done((bf16[576,512]{1,0:T(8,128)(2,1)S(1)}, bf16[576,512]{1,0:T(8,128)(2,1)S(1)}, u32[]{:S(2)}, u32[]{:S(2)}) %collective-permute-start.4) | collective-permute-done | bytes 589856 | tf_op jit(solution)/shard_map/ppermute | solution.py:394
  38.8 1.6 %collective-permute-start.9 = (bf16[576,512]{1,0:T(8,128)(2,1)S(1)}, bf16[576,512]{1,0:T(8,128)(2,1)S(1)}, u32[]{:S(2)}, u32[]{:S(2)}) collective-permute-start(bf16[576,512]{1,0:T(8,128)(2,1)S(1)} %join.5.unused), channel_id=1, source_target_pairs={{0,4},{1,5},{2,3},{3,2},{4,0},{5,1},{6,7},{7,6},{8,12},{9,13},{10,... | collective-permute-start | bytes 1769480 | tf_op jit(solution)/shard_map/ppermute | solution.py:394
  40.4 0.0 collective-permute-done.5.refs_3_
  40.4 1.4 %merge.4 = (f32[2,128,512]{2,1,0:T(8,128)S(1)}, bf16[2,128,512]{2,1,0:T(8,128)(2,1)S(1)}, s32[8,1,144]{2,1,0:T(1,128)S(1)}) custom-call(bf16[576,512]{1,0:T(8,128)(2,1)S(1)} %join.5.unused, bf16[640,512]{1,0:T(8,128)(2,1)S(1)} %copy-done.2, bf16[640,512]{1,0:T(8,128)(2,1)S(1)} %collective-permute-done.refs_1_, ...), custom_call_target="tpu_custom_call" | custom-call | tf_op jit(solution)/shard_map/merge/pallas_call | solution.py:62
  41.8 1.6 %collective-permute-start.6 = (bf16[2,128,512]{2,1,0:T(8,128)(2,1)S(1)}, bf16[2,128,512]{2,1,0:T(8,128)(2,1)S(1)}, u32[]{:S(2)}, u32[]{:S(2)}) collective-permute-start(bf16[2,128,512]{2,1,0:T(8,128)(2,1)S(1)} %get-tuple-element.41.unused), channel_id=1, source_target_pairs={{0,8},{1,9},{2,10},{3,11},{4,12},{5,13},{6,14},{7,15},{8,0},{9,1},... | collective-permute-start | bytes 786440 | tf_op jit(solution)/shard_map/ppermute | solution.py:394
  43.5 7.2 %collective-permute-done.6.refs_1_ = bf16[2,128,512]{2,1,0:T(8,128)(2,1)S(1)} collective-permute-done((bf16[2,128,512]{2,1,0:T(8,128)(2,1)S(1)}, bf16[2,128,512]{2,1,0:T(8,128)(2,1)S(1)}, u32[]{:S(2)}, u32[]{:S(2)}) %collective-permute-start.6) | collective-permute-done | bytes 262176 | tf_op jit(solution)/shard_map/ppermute | solution.py:394
  50.7 0.0 collective-permute-done.7.refs_1_
  50.8 0.7 collective-permute-start.12
  51.5 0.0 collective-permute-done.8.refs_2_
  51.5 0.8 collective-permute-done.9.refs_3_
  52.3 1.2 %merge.5 = (f32[2,128,512]{2,1,0:T(8,128)S(1)}, bf16[2,128,512]{2,1,0:T(8,128)(2,1)S(1)}) custom-call(bf16[576,512]{1,0:T(8,128)(2,1)S(1)} %join.6.unused, bf16[576,512]{1,0:T(8,128)(2,1)S(1)} %get-tuple-element.36.unused.refs_0_, bf16[576,512]{1,0:T(8,128)(2,1)S(1)} %collective-permute-done.1.refs_1_, bf16[576,512]{1,0:T(8,128)(2,1)S(1)} %collective-permute-done.4.refs_2_, ...), custom_call_target="tpu_custom_call" | custom-call | tf_op jit(solution)/shard_map/merge/pallas_call | solution.py:62
  53.5 1.6 %collective-permute-start.10 = (bf16[2,128,512]{2,1,0:T(8,128)(2,1)S(1)}, bf16[2,128,512]{2,1,0:T(8,128)(2,1)S(1)}, u32[]{:S(2)}, u32[]{:S(2)}) collective-permute-start(bf16[2,128,512]{2,1,0:T(8,128)(2,1)S(1)} %get-tuple-element.46.unused), channel_id=1, source_target_pairs={{0,8},{1,9},{2,10},{3,11},{4,12},{5,13},{6,14},{7,15},{8,0},{9,1},... | collective-permute-start | bytes 786440 | tf_op jit(solution)/shard_map/ppermute | solution.py:394
  55.1 1.5 %collective-permute-start.13 = (bf16[576,512]{1,0:T(8,128)(2,1)S(1)}, bf16[576,512]{1,0:T(8,128)(2,1)S(1)}, u32[]{:S(2)}, u32[]{:S(2)}) collective-permute-start(bf16[576,512]{1,0:T(8,128)(2,1)S(1)} %join.6.unused), channel_id=1, source_target_pairs={{0,4},{1,5},{2,3},{3,2},{4,0},{5,1},{6,7},{7,6},{8,12},{9,13},{10,... | collective-permute-start | bytes 1769480 | tf_op jit(solution)/shard_map/ppermute | solution.py:394
  56.6 2.6 %collective-permute-start.11 = (bf16[1,128,512]{2,1,0:T(8,128)(2,1)S(1)}, bf16[1,128,512]{2,1,0:T(8,128)(2,1)S(1)}, u32[]{:S(2)}, u32[]{:S(2)}) collective-permute-start(bf16[1,128,512]{2,1,0:T(8,128)(2,1)S(1)} %get-tuple-element.43.unused), channel_id=1, source_target_pairs={{0,16},{1,17},{2,18},{3,19},{4,20},{5,21},{6,22},{7,23},{8,24},{9,... | collective-permute-start | bytes 393224 | tf_op jit(solution)/shard_map/ppermute | solution.py:394
  59.2 4.8 %collective-permute-done.10.refs_1_ = bf16[2,128,512]{2,1,0:T(8,128)(2,1)S(1)} collective-permute-done((bf16[2,128,512]{2,1,0:T(8,128)(2,1)S(1)}, bf16[2,128,512]{2,1,0:T(8,128)(2,1)S(1)}, u32[]{:S(2)}, u32[]{:S(2)}) %collective-permute-start.10) | collective-permute-done | bytes 262176 | tf_op jit(solution)/shard_map/ppermute | solution.py:394
  64.1 0.5 collective-permute-done.12.refs_2_
  64.6 0.9 join.7.unused
  65.4 0.9 collective-permute-start.16
  66.3 0.0 collective-permute-done.13.refs_3_
  66.3 1.9 %merge.6 = (f32[2,128,512]{2,1,0:T(8,128)S(1)}, bf16[2,128,512]{2,1,0:T(8,128)(2,1)}) custom-call(bf16[576,512]{1,0:T(8,128)(2,1)} %join.7.unused, bf16[576,512]{1,0:T(8,128)(2,1)S(1)} %get-tuple-element.38.unused.refs_0_, bf16[576,512]{1,0:T(8,128)(2,1)S(1)} %collective-permute-done.3.refs_1_, bf16[576,512]{1,0:T(8,128)(2,1)S(1)} %collective-permute-done.8.refs_2_, ...), custom_call_target="tpu_custom_call" | custom-call | tf_op jit(solution)/shard_map/merge/pallas_call | solution.py:62
  68.3 2.5 %collective-permute-start.15 = (bf16[2,128,512]{2,1,0:T(8,128)(2,1)}, bf16[2,128,512]{2,1,0:T(8,128)(2,1)S(1)}, u32[]{:S(2)}, u32[]{:S(2)}) collective-permute-start(bf16[2,128,512]{2,1,0:T(8,128)(2,1)} %get-tuple-element.50.unused), channel_id=1, source_target_pairs={{0,8},{1,9},{2,10},{3,11},{4,12},{5,13},{6,14},{7,15},{8,0},{9,1},... | collective-permute-start | bytes 786440 | tf_op jit(solution)/shard_map/ppermute | solution.py:394
  70.8 1.9 %collective-permute-start.14 = (bf16[1,128,512]{2,1,0:T(8,128)(2,1)S(1)}, bf16[1,128,512]{2,1,0:T(8,128)(2,1)S(1)}, u32[]{:S(2)}, u32[]{:S(2)}) collective-permute-start(bf16[1,128,512]{2,1,0:T(8,128)(2,1)S(1)} %get-tuple-element.48.unused), channel_id=1, source_target_pairs={{0,16},{1,17},{2,18},{3,19},{4,20},{5,21},{6,22},{7,23},{8,24},{9,... | collective-permute-start | bytes 393224 | tf_op jit(solution)/shard_map/ppermute | solution.py:394
  72.7 6.5 %collective-permute-done.14.refs_1_ = bf16[1,128,512]{2,1,0:T(8,128)(2,1)S(1)} collective-permute-done((bf16[1,128,512]{2,1,0:T(8,128)(2,1)S(1)}, bf16[1,128,512]{2,1,0:T(8,128)(2,1)S(1)}, u32[]{:S(2)}, u32[]{:S(2)}) %collective-permute-start.14) | collective-permute-done | bytes 131104 | tf_op jit(solution)/shard_map/ppermute | solution.py:394
  79.1 0.9 copy-done.6
  80.1 0.0 collective-permute-done.15.refs_1_
  80.2 3.4 %collective-permute-start.17 = (bf16[1,128,512]{2,1,0:T(8,128)(2,1)S(1)}, bf16[1,128,512]{2,1,0:T(8,128)(2,1)S(1)}, u32[]{:S(2)}, u32[]{:S(2)}) collective-permute-start(bf16[1,128,512]{2,1,0:T(8,128)(2,1)S(1)} %get-tuple-element.53.unused), channel_id=1, source_target_pairs={{0,16},{1,17},{2,18},{3,19},{4,20},{5,21},{6,22},{7,23},{8,24},{9,... | collective-permute-start | bytes 393224 | tf_op jit(solution)/shard_map/ppermute | solution.py:394
  83.7 0.0 collective-permute-done.16.refs_3_
  83.7 2.3 %merge.7 = (f32[2,128,512]{2,1,0:T(8,128)S(1)}, bf16[2,128,512]{2,1,0:T(8,128)(2,1)S(1)}) custom-call(bf16[1,128,512]{2,1,0:T(8,128)(2,1)S(1)} %get-tuple-element.53.unused, bf16[576,512]{1,0:T(8,128)(2,1)S(1)} %get-tuple-element.39.unused.refs_0_, bf16[576,512]{1,0:T(8,128)(2,1)S(1)} %collective-permute-done.7.refs_1_, ...), custom_call_target="tpu_custom_call" | custom-call | tf_op jit(solution)/shard_map/merge/pallas_call | solution.py:62
  86.0 0.7 collective-permute-start.18
  86.7 0.0 collective-permute-done.17.refs_1_
  86.7 5.8 %collective-permute-done.18.refs_1_ = bf16[2,128,512]{2,1,0:T(8,128)(2,1)S(1)} collective-permute-done((bf16[2,128,512]{2,1,0:T(8,128)(2,1)S(1)}, bf16[2,128,512]{2,1,0:T(8,128)(2,1)S(1)}, u32[]{:S(2)}, u32[]{:S(2)}) %collective-permute-start.18) | collective-permute-done | bytes 262176 | tf_op jit(solution)/shard_map/ppermute | solution.py:394
  92.5 0.1 halve.7
  92.6 1.1 %collective-permute-start.20 = (f32[1,2048]{1,0:T(1,128)S(1)}, f32[1,2048]{1,0:T(1,128)S(1)}, u32[]{:S(2)}, u32[]{:S(2)}) collective-permute-start(f32[1,2048]{1,0:T(1,128)S(1)} %broadcast_select_fusion.2), channel_id=1, source_target_pairs={{0,1},{1,0},{2,3},{3,2},{4,5},{5,4},{6,7},{7,6},{8,9},{9,8},{10,11... | collective-permute-start | bytes 24584 | tf_op jit(solution)/shard_map/ppermute | solution.py:394
  93.8 3.7 %collective-permute-start.21 = (bf16[1,512]{1,0:T(2,128)(2,1)S(1)}, bf16[1,512]{1,0:T(2,128)(2,1)S(1)}, u32[]{:S(2)}, u32[]{:S(2)}) collective-permute-start(bf16[1,512]{1,0:T(2,128)(2,1)S(1)} %fusion), channel_id=1, source_target_pairs={{0,17},{1,16},{2,19},{3,18},{4,21},{5,20},{6,23},{7,22},{8,25},{9,... | collective-permute-start | bytes 3080 | tf_op jit(solution)/shard_map/ppermute | solution.py:394
  97.5 0.1 copy.15.refs_6_
  97.6 0.0 collective-permute-start.19
  97.6 0.0 copy-start.10
  97.6 0.9 copy-done.10
  98.5 0.9 copy-done.11
  99.4 0.9 copy-done.12
  100.3 2.7 %factor.1.unused.refs_7_ = f32[128,2048]{1,0:T(8,128)S(1)} custom-call(bf16[1,128,512]{2,1,0:T(8,128)(2,1)S(1)} %get-tuple-element.57.unused, s32[128,256]{1,0:T(8,128)S(1)} %bitcast.23, f32[128,256]{1,0:T(8,128)S(1)} %bitcast.24, f32[128,256]{1,0:T(8,128)S(1)} %bitcast.25, f32[128,256]{1,0:T(8,128)S(1)} %bitcast.26, s32[128,256]{1,0:T(8,128)S(1)} %bitcast.27, ...), custom_call_target="tpu_custom_call" | custom-call | tf_op jit(solution)/shard_map/factor/pallas_call | solution.py:62
  103.0 0.0 collective-permute-done.20
  103.1 3.2 %collective-permute-done.19 = bf16[1,128,512]{2,1,0:T(8,128)(2,1)S(1)} collective-permute-done((bf16[1,128,512]{2,1,0:T(8,128)(2,1)S(1)}, bf16[1,128,512]{2,1,0:T(8,128)(2,1)S(1)}, u32[]{:S(2)}, u32[]{:S(2)}) %collective-permute-start.19) | collective-permute-done | bytes 131104 | tf_op jit(solution)/shard_map/ppermute | solution.py:394
  106.3 1.2 %finish.1 = bf16[128,2048]{1,0:T(8,128)(2,1)} custom-call(f32[128,2048]{1,0:T(8,128)S(1)} %factor.1.unused.refs_7_, f32[128,512]{1,0:T(8,128)S(1)} %total.3.unused.refs_0_, f32[128,512]{1,0:T(8,128)S(1)} %total.4.unused.refs_1_, f32[128,512]{1,0:T(8,128)S(1)} %total.5.unused.refs_2_, f32[1,128,512]{2,1,0:T(8,128)S(1)} %get-tuple-element.58.refs_3_, ...), custom_call_target="tpu_custom_call" | custom-call | tf_op jit(solution)/shard_map/finish/pallas_call | solution.py:62
  (46 shorter events, 0.6 us)
Async XLA Ops:
  0.0 13.4 %copy-start.3 = (bf16[4,256,256]{2,1,0:T(8,128)(2,1)S(1)}, bf16[4,256,256]{2,1,0:T(8,128)(2,1)}, u32[]{:S(2)}) copy-start(bf16[4,256,256]{2,1,0:T(8,128)(2,1)} %refs_4_.5) | copy-start | bytes 1572868
  0.0 13.4 %copy-start.7 = (f32[2,8,8]{2,1,0:T(8,128)S(1)}, f32[2,8,8]{2,1,0:T(8,128)}, u32[]{:S(2)}) copy-start(f32[2,8,8]{2,1,0:T(8,128)} %refs_0_.5) | copy-start | bytes 1540
  6.9 2.5 %collective-permute-start = (bf16[640,512]{1,0:T(8,128)(2,1)}, bf16[640,512]{1,0:T(8,128)(2,1)S(1)}, u32[]{:S(2)}, u32[]{:S(2)}) collective-permute-start(bf16[640,512]{1,0:T(8,128)(2,1)} %get-tuple-element.33), channel_id=1, source_target_pairs={{0,2},{1,3},{2,0},{3,1},{4,6},{5,7},{6,4},{7,5},{8,10},{9,11},{10,... | collective-permute-start | bytes 1966088 | tf_op jit(solution)/shard_map/ppermute | solution.py:394
  9.4 1.1 %copy-start.1 = (bf16[640,512]{1,0:T(8,128)(2,1)S(1)}, bf16[640,512]{1,0:T(8,128)(2,1)}, u32[]{:S(2)}) copy-start(bf16[640,512]{1,0:T(8,128)(2,1)} %get-tuple-element.32.unused.refs_0_) | copy-start | bytes 1966084
  10.5 12.1 %collective-permute-start.2 = (bf16[640,512]{1,0:T(8,128)(2,1)S(1)}, bf16[640,512]{1,0:T(8,128)(2,1)S(1)}, u32[]{:S(2)}, u32[]{:S(2)}) collective-permute-start(bf16[640,512]{1,0:T(8,128)(2,1)S(1)} %fold.4.unused), channel_id=1, source_target_pairs={{0,1},{1,0},{2,6},{3,7},{4,5},{5,4},{6,2},{7,3},{8,9},{9,8},{10,14... | collective-permute-start | bytes 1966088 | tf_op jit(solution)/shard_map/ppermute | solution.py:394
  13.4 1.9 %copy-start = (bf16[1,1,768,2048]{3,2,1,0:T(8,128)(2,1)S(1)}, bf16[1,1,768,2048]{3,2,1,0:T(8,128)(2,1)}, u32[]{:S(2)}) copy-start(bf16[1,1,768,2048]{3,2,1,0:T(8,128)(2,1)} %param.14) | copy-start | bytes 9437188
  15.3 1.0 copy-start.4
  16.3 0.7 copy-start.13
  17.0 5.6 %copy-start.2 = (bf16[640,512]{1,0:T(8,128)(2,1)S(1)}, bf16[640,512]{1,0:T(8,128)(2,1)}, u32[]{:S(2)}) copy-start(bf16[640,512]{1,0:T(8,128)(2,1)} %get-tuple-element.32.unused.refs_0_) | copy-start | bytes 1966084
  20.5 2.1 %collective-permute-start.1 = (bf16[576,512]{1,0:T(8,128)(2,1)S(1)}, bf16[576,512]{1,0:T(8,128)(2,1)S(1)}, u32[]{:S(2)}, u32[]{:S(2)}) collective-permute-start(bf16[576,512]{1,0:T(8,128)(2,1)S(1)} %get-tuple-element.37), channel_id=1, source_target_pairs={{0,2},{1,3},{2,0},{3,1},{4,6},{5,7},{6,4},{7,5},{8,10},{9,11},{10,... | collective-permute-start | bytes 1769480 | tf_op jit(solution)/shard_map/ppermute | solution.py:394
  22.7 17.7 %collective-permute-start.5 = (bf16[640,512]{1,0:T(8,128)(2,1)S(1)}, bf16[640,512]{1,0:T(8,128)(2,1)S(1)}, u32[]{:S(2)}, u32[]{:S(2)}) collective-permute-start(bf16[640,512]{1,0:T(8,128)(2,1)S(1)} %join.4.unused), channel_id=1, source_target_pairs={{0,4},{1,5},{2,3},{3,2},{4,0},{5,1},{6,7},{7,6},{8,12},{9,13},{10,... | collective-permute-start | bytes 1966088 | tf_op jit(solution)/shard_map/ppermute | solution.py:394
  27.7 5.1 %collective-permute-start.3 = (bf16[576,512]{1,0:T(8,128)(2,1)S(1)}, bf16[576,512]{1,0:T(8,128)(2,1)S(1)}, u32[]{:S(2)}, u32[]{:S(2)}) collective-permute-start(bf16[576,512]{1,0:T(8,128)(2,1)S(1)} %get-tuple-element.40), channel_id=1, source_target_pairs={{0,2},{1,3},{2,0},{3,1},{4,6},{5,7},{6,4},{7,5},{8,10},{9,11},{10,... | collective-permute-start | bytes 1769480 | tf_op jit(solution)/shard_map/ppermute | solution.py:394
  27.8 11.0 %collective-permute-start.4 = (bf16[576,512]{1,0:T(8,128)(2,1)S(1)}, bf16[576,512]{1,0:T(8,128)(2,1)S(1)}, u32[]{:S(2)}, u32[]{:S(2)}) collective-permute-start(bf16[576,512]{1,0:T(8,128)(2,1)S(1)} %fold.5.unused), channel_id=1, source_target_pairs={{0,1},{1,0},{2,6},{3,7},{4,5},{5,4},{6,2},{7,3},{8,9},{9,8},{10,14... | collective-permute-start | bytes 1769480 | tf_op jit(solution)/shard_map/ppermute | solution.py:394
  32.7 18.0 %collective-permute-start.7 = (bf16[576,512]{1,0:T(8,128)(2,1)S(1)}, bf16[576,512]{1,0:T(8,128)(2,1)S(1)}, u32[]{:S(2)}, u32[]{:S(2)}) collective-permute-start(bf16[576,512]{1,0:T(8,128)(2,1)S(1)} %get-tuple-element.44), channel_id=1, source_target_pairs={{0,2},{1,3},{2,0},{3,1},{4,6},{5,7},{6,4},{7,5},{8,10},{9,11},{10,... | collective-permute-start | bytes 1769480 | tf_op jit(solution)/shard_map/ppermute | solution.py:394
  32.8 18.6 %collective-permute-start.8 = (bf16[576,512]{1,0:T(8,128)(2,1)S(1)}, bf16[576,512]{1,0:T(8,128)(2,1)S(1)}, u32[]{:S(2)}, u32[]{:S(2)}) collective-permute-start(bf16[576,512]{1,0:T(8,128)(2,1)S(1)} %fold.6.unused), channel_id=1, source_target_pairs={{0,1},{1,0},{2,6},{3,7},{4,5},{5,4},{6,2},{7,3},{8,9},{9,8},{10,14... | collective-permute-start | bytes 1769480 | tf_op jit(solution)/shard_map/ppermute | solution.py:394
  38.8 13.4 %collective-permute-start.9 = (bf16[576,512]{1,0:T(8,128)(2,1)S(1)}, bf16[576,512]{1,0:T(8,128)(2,1)S(1)}, u32[]{:S(2)}, u32[]{:S(2)}) collective-permute-start(bf16[576,512]{1,0:T(8,128)(2,1)S(1)} %join.5.unused), channel_id=1, source_target_pairs={{0,4},{1,5},{2,3},{3,2},{4,0},{5,1},{6,7},{7,6},{8,12},{9,13},{10,... | collective-permute-start | bytes 1769480 | tf_op jit(solution)/shard_map/ppermute | solution.py:394
  41.8 8.9 %collective-permute-start.6 = (bf16[2,128,512]{2,1,0:T(8,128)(2,1)S(1)}, bf16[2,128,512]{2,1,0:T(8,128)(2,1)S(1)}, u32[]{:S(2)}, u32[]{:S(2)}) collective-permute-start(bf16[2,128,512]{2,1,0:T(8,128)(2,1)S(1)} %get-tuple-element.41.unused), channel_id=1, source_target_pairs={{0,8},{1,9},{2,10},{3,11},{4,12},{5,13},{6,14},{7,15},{8,0},{9,1},... | collective-permute-start | bytes 786440 | tf_op jit(solution)/shard_map/ppermute | solution.py:394
  50.8 13.8 %collective-permute-start.12 = (bf16[576,512]{1,0:T(8,128)(2,1)S(1)}, bf16[576,512]{1,0:T(8,128)(2,1)S(1)}, u32[]{:S(2)}, u32[]{:S(2)}) collective-permute-start(bf16[576,512]{1,0:T(8,128)(2,1)S(1)} %fold.7.unused), channel_id=1, source_target_pairs={{0,1},{1,0},{2,6},{3,7},{4,5},{5,4},{6,2},{7,3},{8,9},{9,8},{10,14... | collective-permute-start | bytes 1769480 | tf_op jit(solution)/shard_map/ppermute | solution.py:394
  53.5 10.5 %collective-permute-start.10 = (bf16[2,128,512]{2,1,0:T(8,128)(2,1)S(1)}, bf16[2,128,512]{2,1,0:T(8,128)(2,1)S(1)}, u32[]{:S(2)}, u32[]{:S(2)}) collective-permute-start(bf16[2,128,512]{2,1,0:T(8,128)(2,1)S(1)} %get-tuple-element.46.unused), channel_id=1, source_target_pairs={{0,8},{1,9},{2,10},{3,11},{4,12},{5,13},{6,14},{7,15},{8,0},{9,1},... | collective-permute-start | bytes 786440 | tf_op jit(solution)/shard_map/ppermute | solution.py:394
  55.1 11.2 %collective-permute-start.13 = (bf16[576,512]{1,0:T(8,128)(2,1)S(1)}, bf16[576,512]{1,0:T(8,128)(2,1)S(1)}, u32[]{:S(2)}, u32[]{:S(2)}) collective-permute-start(bf16[576,512]{1,0:T(8,128)(2,1)S(1)} %join.6.unused), channel_id=1, source_target_pairs={{0,4},{1,5},{2,3},{3,2},{4,0},{5,1},{6,7},{7,6},{8,12},{9,13},{10,... | collective-permute-start | bytes 1769480 | tf_op jit(solution)/shard_map/ppermute | solution.py:394
  56.6 7.4 %collective-permute-start.11 = (bf16[1,128,512]{2,1,0:T(8,128)(2,1)S(1)}, bf16[1,128,512]{2,1,0:T(8,128)(2,1)S(1)}, u32[]{:S(2)}, u32[]{:S(2)}) collective-permute-start(bf16[1,128,512]{2,1,0:T(8,128)(2,1)S(1)} %get-tuple-element.43.unused), channel_id=1, source_target_pairs={{0,16},{1,17},{2,18},{3,19},{4,20},{5,21},{6,22},{7,23},{8,24},{9,... | collective-permute-start | bytes 393224 | tf_op jit(solution)/shard_map/ppermute | solution.py:394
  64.0 2.3 %copy-start.5 = (f32[1,128,512]{2,1,0:T(8,128)}, f32[1,128,512]{2,1,0:T(8,128)S(1)}, u32[]{:S(2)}) copy-start(f32[1,128,512]{2,1,0:T(8,128)S(1)} %get-tuple-element.51.refs_0_) | copy-start | bytes 786436
  65.4 18.2 %collective-permute-start.16 = (bf16[576,512]{1,0:T(8,128)(2,1)}, bf16[576,512]{1,0:T(8,128)(2,1)}, u32[]{:S(2)}, u32[]{:S(2)}) collective-permute-start(bf16[576,512]{1,0:T(8,128)(2,1)} %join.7.unused), channel_id=1, source_target_pairs={{0,4},{1,5},{2,3},{3,2},{4,0},{5,1},{6,7},{7,6},{8,12},{9,13},{10,... | collective-permute-start | bytes 1769480 | tf_op jit(solution)/shard_map/ppermute | solution.py:394
  68.3 11.9 %collective-permute-start.15 = (bf16[2,128,512]{2,1,0:T(8,128)(2,1)}, bf16[2,128,512]{2,1,0:T(8,128)(2,1)S(1)}, u32[]{:S(2)}, u32[]{:S(2)}) collective-permute-start(bf16[2,128,512]{2,1,0:T(8,128)(2,1)} %get-tuple-element.50.unused), channel_id=1, source_target_pairs={{0,8},{1,9},{2,10},{3,11},{4,12},{5,13},{6,14},{7,15},{8,0},{9,1},... | collective-permute-start | bytes 786440 | tf_op jit(solution)/shard_map/ppermute | solution.py:394
  70.8 8.4 %collective-permute-start.14 = (bf16[1,128,512]{2,1,0:T(8,128)(2,1)S(1)}, bf16[1,128,512]{2,1,0:T(8,128)(2,1)S(1)}, u32[]{:S(2)}, u32[]{:S(2)}) collective-permute-start(bf16[1,128,512]{2,1,0:T(8,128)(2,1)S(1)} %get-tuple-element.48.unused), channel_id=1, source_target_pairs={{0,16},{1,17},{2,18},{3,19},{4,20},{5,21},{6,22},{7,23},{8,24},{9,... | collective-permute-start | bytes 393224 | tf_op jit(solution)/shard_map/ppermute | solution.py:394
  79.1 0.9 copy-start.6
  80.1 17.4 %copy-start.15 = (f32[8,3]{0,1:T(4,128)S(1)}, f32[8,3]{0,1:T(4,128)}, u32[]{:S(2)}) copy-start(f32[8,3]{0,1:T(4,128)} %param.24) | copy-start | bytes 292
  80.1 17.5 %copy-start.14 = (f32[8,33]{1,0:T(8,128)S(1)}, f32[8,33]{1,0:T(8,128)}, u32[]{:S(2)}) copy-start(f32[8,33]{1,0:T(8,128)} %param.21) | copy-start | bytes 3172
  80.1 17.5 %copy-start.8 = (s32[1,128,256]{2,1,0:T(8,128)S(1)}, s32[1,128,256]{2,1,0:T(8,128)}, u32[]{:S(2)}) copy-start(s32[1,128,256]{2,1,0:T(8,128)} %param.22) | copy-start | bytes 393220
  80.1 17.5 %copy-start.9 = (f32[1,128,256]{2,1,0:T(8,128)S(1)}, f32[1,128,256]{2,1,0:T(8,128)}, u32[]{:S(2)}) copy-start(f32[1,128,256]{2,1,0:T(8,128)} %param.23) | copy-start | bytes 393220
  80.2 6.5 %collective-permute-start.17 = (bf16[1,128,512]{2,1,0:T(8,128)(2,1)S(1)}, bf16[1,128,512]{2,1,0:T(8,128)(2,1)S(1)}, u32[]{:S(2)}, u32[]{:S(2)}) collective-permute-start(bf16[1,128,512]{2,1,0:T(8,128)(2,1)S(1)} %get-tuple-element.53.unused), channel_id=1, source_target_pairs={{0,16},{1,17},{2,18},{3,19},{4,20},{5,21},{6,22},{7,23},{8,24},{9,... | collective-permute-start | bytes 393224 | tf_op jit(solution)/shard_map/ppermute | solution.py:394
  86.0 6.6 %collective-permute-start.18 = (bf16[2,128,512]{2,1,0:T(8,128)(2,1)S(1)}, bf16[2,128,512]{2,1,0:T(8,128)(2,1)S(1)}, u32[]{:S(2)}, u32[]{:S(2)}) collective-permute-start(bf16[2,128,512]{2,1,0:T(8,128)(2,1)S(1)} %get-tuple-element.54.unused), channel_id=1, source_target_pairs={{0,8},{1,9},{2,10},{3,11},{4,12},{5,13},{6,14},{7,15},{8,0},{9,1},... | collective-permute-start | bytes 786440 | tf_op jit(solution)/shard_map/ppermute | solution.py:394
  92.6 10.4 %collective-permute-start.20 = (f32[1,2048]{1,0:T(1,128)S(1)}, f32[1,2048]{1,0:T(1,128)S(1)}, u32[]{:S(2)}, u32[]{:S(2)}) collective-permute-start(f32[1,2048]{1,0:T(1,128)S(1)} %broadcast_select_fusion.2), channel_id=1, source_target_pairs={{0,1},{1,0},{2,3},{3,2},{4,5},{5,4},{6,7},{7,6},{8,9},{9,8},{10,11... | collective-permute-start | bytes 24584 | tf_op jit(solution)/shard_map/ppermute | solution.py:394
  93.8 9.3 %collective-permute-start.21 = (bf16[1,512]{1,0:T(2,128)(2,1)S(1)}, bf16[1,512]{1,0:T(2,128)(2,1)S(1)}, u32[]{:S(2)}, u32[]{:S(2)}) collective-permute-start(bf16[1,512]{1,0:T(2,128)(2,1)S(1)} %fusion), channel_id=1, source_target_pairs={{0,17},{1,16},{2,19},{3,18},{4,21},{5,20},{6,23},{7,22},{8,25},{9,... | collective-permute-start | bytes 3080 | tf_op jit(solution)/shard_map/ppermute | solution.py:394
  97.6 8.7 %collective-permute-start.19 = (bf16[1,128,512]{2,1,0:T(8,128)(2,1)S(1)}, bf16[1,128,512]{2,1,0:T(8,128)(2,1)S(1)}, u32[]{:S(2)}, u32[]{:S(2)}) collective-permute-start(bf16[1,128,512]{2,1,0:T(8,128)(2,1)S(1)} %get-tuple-element.57.unused), channel_id=1, source_target_pairs={{0,16},{1,17},{2,18},{3,19},{4,20},{5,21},{6,22},{7,23},{8,24},{9,... | collective-permute-start | bytes 393224 | tf_op jit(solution)/shard_map/ppermute | solution.py:394
  97.6 0.9 copy-start.10
  98.5 0.9 copy-start.11
  99.4 0.9 copy-start.12

commit v4 on v3

--- a/solution.py
+++ b/solution.py
@@ -38,6 +38,7 @@
     "g2",
     "h3",
     "x0",
+    "g3",
     "f0",
 )
 UNROLL = 6
@@ -45,7 +46,7 @@
 MIB = 1024 * 1024
 
 
-def call(kernel, name, limit, out_shape, operands, after, scalars=0, **more):
+def call(kernel, name, weight, limit, out_shape, operands, after, scalars=0, **more):
     vmem = pl.BlockSpec(memory_space=pltpu.VMEM)
     smem = pl.BlockSpec(memory_space=pltpu.SMEM)
     specs = more.pop("in_specs", None)
@@ -65,9 +66,16 @@
         in_specs=specs,
         out_specs=jax.tree.map(lambda _: vmem, out_shape),
         compiler_params=pltpu.CompilerParams(vmem_limit_bytes=limit * MIB),
+        cost_estimate=cost(weight),
         name=name,
         **more,
     )(*operands)
+
+
+def cost(weight):
+    return pl.CostEstimate(
+        flops=int(weight * 1.1e6), bytes_accessed=int(weight * 3.6e3), transcendentals=0
+    )
 
 
 def dot(a, b):
@@ -342,16 +350,10 @@
 
 
 def finish_kernel(count, *refs):
-    grids, arrived_ref, (low_ref, high_ref, factor_ref, out_ref) = (
-        refs[:count],
-        refs[count],
-        refs[count + 1 :],
-    )
+    grids, (low_ref, high_ref, factor_ref, out_ref) = refs[:count], refs[count:]
     start = 0
-    for i, grid_ref in enumerate(grids):
+    for grid_ref in grids:
         grid = grid_ref[...]
-        if i == count - 1:
-            grid = grid[0] + arrived_ref[...].astype(jnp.float32).reshape(grid.shape[1:])
         here = slice(start, start + grid.shape[1])
         before = jnp.concatenate([low_ref[:, here], grid[:-1]], axis=0)
         after = jnp.concatenate([grid[1:], high_ref[:, here]], axis=0)
@@ -422,6 +424,7 @@
             mine, cross, shared["position"], shared["codes"] = call(
                 functools.partial(lead_kernel, shape, CHUNKS[i]),
                 "lead",
+                6,
                 63,
                 payload
                 + [struct(1, blocks, dtype=jnp.int32), struct(blocks, 128, dtype=jnp.float32)],
@@ -450,6 +453,7 @@
             mine, cross = call(
                 functools.partial(follow_kernel, shape, CHUNKS[i]),
                 "follow",
+                2 + (end - begin),
                 28,
                 payload,
                 (bandpass_offset, x, shared["position"], shared["codes"], weight_tiles),
@@ -467,6 +471,7 @@
         outs = call(
             functools.partial(fold_kernel, picks, peers),
             "fold",
+            0.3,
             16,
             [struct(2 * len(parts) * height, columns) for parts in picks],
             (mine, crossed),
@@ -490,6 +495,7 @@
         both = call(
             functools.partial(join_kernel, peers),
             "join",
+            0.3,
             16,
             struct(*arrived.shape),
             chunk["lists"],
@@ -522,6 +528,7 @@
         outs = call(
             functools.partial(merge_kernel, i == 0, slots, cells, parts),
             "merge",
+            0.5 + 0.7 * columns / pixels,
             24,
             outs,
             (*arrays, *(() if i == 0 else (shared["keys"],))),
@@ -537,6 +544,7 @@
         outs = call(
             functools.partial(halve_kernel, len(arrived)),
             "halve",
+            0.5,
             16,
             [
                 struct(half, cells, columns, dtype=jnp.float32),
@@ -545,6 +553,8 @@
             (keep, *arrived),
             after,
         )
+        if i == len(chunks) - 1 and half == 1:
+            chunks[i]["edges"] = edges(outs[0], outs[-1].reshape(cells, -1))
         return forward(i, outs[0], outs[1:])
 
     def total(i, after):
@@ -554,6 +564,7 @@
         chunk["grid"] = call(
             total_kernel,
             "total",
+            0.3,
             16,
             struct(*chunk["keep"].shape[1:], dtype=jnp.float32),
             (chunk["keep"], *chunk["arrived"]),
@@ -561,16 +572,8 @@
         )
         return chunk["grid"]
 
-    def finish(i, after):
-        *early, final = chunks
-        for i in range(len(chunks)):
-            while chunks[i]["keep"].shape[0] > 1:
-                after = halve(i, after)
-            if i < len(early) and "grid" not in chunks[i]:
-                after = total(i, after)
-        keep, arrived = final["keep"], final["arrived"][0].reshape(cells, -1)
-        away = final["away"].reshape(cells, -1)
-
+    def edges(keep, away):
+        early = chunks[:-1]
         def ends(array):
             return array[:1], array[-1:]
 
@@ -578,8 +581,8 @@
         for pick in (0, 1):
             kept = [ends(chunk["grid"])[pick] for chunk in early] + [ends(keep[0])[pick]]
             parts.append((jnp.concatenate(kept, axis=1), ends(away)[pick]))
-        width_early = width - arrived.shape[1]
-        hop = bits["z"] << (final["hops"] - 1)
+        width_early = width - away.shape[1]
+        hop = bits["z"] << (depth.bit_length() - 2)
 
         def beside(kept, coming):
             coming = jnp.pad(coming.astype(jnp.float32), ((0, 0), (width_early, 0)))
@@ -604,12 +607,17 @@
             high = beside(
                 lax.ppermute(parts[0][0], "row", down), lax.ppermute(parts[0][1], axes, high_pairs)
             )
+        return low, high
+
+    def finish(i, after):
+        low, high = chunks[-1]["edges"]
         return call(
             functools.partial(finish_kernel, len(chunks)),
             "finish",
+            1,
             16,
             struct(cells, width),
-            (*[chunk["grid"] for chunk in early], keep, arrived, low, high, shared["factor"]),
+            (*[chunk["grid"] for chunk in chunks], low, high, shared["factor"]),
             after,
         )
 
@@ -617,6 +625,7 @@
         shared["factor"] = call(
             functools.partial(factor_kernel, bands, pixels),
             "factor",
+            3,
             16,
             struct(cells, width, dtype=jnp.float32),
             (

time: 108 us -> 104 us (0.963)
  local copies, waits for them, and re-layouts: 8.44 us -> 5.75 us
  starting transfers between devices: 31.4 us -> 30.1 us
    unnamed x33, local copies, waits for them, and re-layouts: 8.41 us -> 5.72 us
    ppermute x22, starting transfers between devices: 31.4 us -> 30.1 us  [exchange(): return lax.ppermute(array, ('tile', 'row'), pairs)]
    pallas_call x25 -> x26, Pallas kernels: 29.4 us -> 29.4 us  [call(): pl.pallas_call(body, out_shape=out_shape, in_specs=specs, out_specs=jax.t...]
  transfers between devices with their start and end apart: 22 -> 22, of which waited for: 10 -> 10; matrix products, arithmetic and copies ran while one was open for 0% -> 0% of each run, Pallas kernels for 20% -> 21%
where the time goes in v4:
time: 104 us; the launch traced here: 103 us
  waiting for transfers between devices  37.5 us (36%)
  starting transfers between devices  30.1 us (29%)
  Pallas kernels  29.4 us (28%)
  local copies, waits for them, and re-layouts  5.75 us (6%)
    ppermute x22, waiting for transfers between devices, exchange(): return lax.ppermute(array, ('tile', 'row'), pairs)  37.5 us
    ppermute x22, starting transfers between devices, exchange(): return lax.ppermute(array, ('tile', 'row'), pairs)  30.1 us
    pallas_call x26, Pallas kernels, call(): pl.pallas_call(body, out_shape=out_shape, in_specs=specs, out_specs=jax.t...  29.4 us
    unnamed x33, local copies, waits for them, and re-layouts  5.72 us
  transfers between devices with their start and end apart: 22, of which 10 were waited for; matrix products, arithmetic and copies ran while one was open for 0% of the time, Pallas kernels for 21%

profile of v4, /device:TPU:0, one launch (start us, length us, event | category | flops | bytes accessed | tf_op | source)
XLA Modules:
  0.0 103.2 jit_solution(13150616220051026532)
XLA Ops:
  0.0 6.9 %lead.1 = (bf16[640,512]{1,0:T(8,128)(2,1)}, bf16[640,512]{1,0:T(8,128)(2,1)}, s32[1,768]{1,0:T(1,128)}, f32[768,128]{1,0:T(8,128)}) custom-call(s32[1]{0:T(128)} %bitcast.refs_0_, f32[2,8,8]{2,1,0:T(8,128)} %refs_0_.5, bf16[768,2048]{1,0:T(8,128)(2,1)} %bitcast.18, s32[1,768]{1,0:T(1,128)} %bitcast.27, s32[1,768]{1,0:T(1,128)} %bitcast.28, ...), custom_call_target="tpu_custom_call" | custom-call | flops 6600000 | bytes 21600 | tf_op jit(solution)/shard_map/lead/pallas_call | solution.py:63
  6.9 0.5 collective-permute-start
  7.4 1.9 %collective-permute-done.refs_1_ = bf16[640,512]{1,0:T(8,128)(2,1)S(1)} collective-permute-done((bf16[640,512]{1,0:T(8,128)(2,1)}, bf16[640,512]{1,0:T(8,128)(2,1)S(1)}, u32[]{:S(2)}, u32[]{:S(2)}) %collective-permute-start) | collective-permute-done | bytes 655392 | tf_op jit(solution)/shard_map/ppermute | solution.py:396
  9.4 1.1 %copy-done.1 = bf16[640,512]{1,0:T(8,128)(2,1)S(1)} copy-done((bf16[640,512]{1,0:T(8,128)(2,1)S(1)}, bf16[640,512]{1,0:T(8,128)(2,1)}, u32[]{:S(2)}) %copy-start.1) | copy-done | bytes 655384
  10.5 2.9 %collective-permute-start.2 = (bf16[640,512]{1,0:T(8,128)(2,1)S(1)}, bf16[640,512]{1,0:T(8,128)(2,1)S(1)}, u32[]{:S(2)}, u32[]{:S(2)}) collective-permute-start(bf16[640,512]{1,0:T(8,128)(2,1)S(1)} %fold.4.unused), channel_id=1, source_target_pairs={{0,1},{1,0},{2,6},{3,7},{4,5},{5,4},{6,2},{7,3},{8,9},{9,8},{10,14... | collective-permute-start | bytes 1966088 | tf_op jit(solution)/shard_map/ppermute | solution.py:396
  13.4 1.9 %copy-done = bf16[1,1,768,2048]{3,2,1,0:T(8,128)(2,1)S(1)} copy-done((bf16[1,1,768,2048]{3,2,1,0:T(8,128)(2,1)S(1)}, bf16[1,1,768,2048]{3,2,1,0:T(8,128)(2,1)}, u32[]{:S(2)}) %copy-start) | copy-done | bytes 3145752
  15.3 1.0 copy-done.4
  16.3 0.7 copy-done.13
  17.0 3.5 %follow.3 = (bf16[576,512]{1,0:T(8,128)(2,1)S(1)}, bf16[576,512]{1,0:T(8,128)(2,1)S(1)}) custom-call(bf16[640,512]{1,0:T(8,128)(2,1)S(1)} %fold.4.unused, f32[2,8,8]{2,1,0:T(8,128)S(1)} %copy-done.7, bf16[768,2048]{1,0:T(8,128)(2,1)S(1)} %bitcast.19, s32[1,768]{1,0:T(1,128)S(1)} %copy-done.13, f32[768,128]{1,0:T(8,128)S(1)} %copy-done.4, ...), custom_call_target="tpu_custom_call" | custom-call | flops 4400000 | bytes 14400 | tf_op jit(solution)/shard_map/follow/pallas_call | solution.py:63
  20.5 0.1 collective-permute-start.1
  20.5 2.0 %collective-permute-done.1.refs_1_ = bf16[576,512]{1,0:T(8,128)(2,1)S(1)} collective-permute-done((bf16[576,512]{1,0:T(8,128)(2,1)S(1)}, bf16[576,512]{1,0:T(8,128)(2,1)S(1)}, u32[]{:S(2)}, u32[]{:S(2)}) %collective-permute-start.1) | collective-permute-done | bytes 589856 | tf_op jit(solution)/shard_map/ppermute | solution.py:396
  22.6 0.0 collective-permute-done.2.refs_2_
  22.7 1.6 %collective-permute-start.5 = (bf16[640,512]{1,0:T(8,128)(2,1)S(1)}, bf16[640,512]{1,0:T(8,128)(2,1)S(1)}, u32[]{:S(2)}, u32[]{:S(2)}) collective-permute-start(bf16[640,512]{1,0:T(8,128)(2,1)S(1)} %join.4.unused), channel_id=1, source_target_pairs={{0,4},{1,5},{2,3},{3,2},{4,0},{5,1},{6,7},{7,6},{8,12},{9,13},{10,... | collective-permute-start | bytes 1966088 | tf_op jit(solution)/shard_map/ppermute | solution.py:396
  24.2 3.5 %follow.4 = (bf16[576,512]{1,0:T(8,128)(2,1)S(1)}, bf16[576,512]{1,0:T(8,128)(2,1)S(1)}) custom-call(bf16[640,512]{1,0:T(8,128)(2,1)S(1)} %join.4.unused, f32[2,8,8]{2,1,0:T(8,128)S(1)} %copy-done.7, bf16[768,2048]{1,0:T(8,128)(2,1)S(1)} %bitcast.20, s32[1,768]{1,0:T(1,128)S(1)} %copy-done.13, f32[768,128]{1,0:T(8,128)S(1)} %copy-done.4, ...), custom_call_target="tpu_custom_call" | custom-call | flops 4400000 | bytes 14400 | tf_op jit(solution)/shard_map/follow/pallas_call | solution.py:63
  27.7 0.1 collective-permute-start.3
  27.8 1.5 %collective-permute-start.4 = (bf16[576,512]{1,0:T(8,128)(2,1)S(1)}, bf16[576,512]{1,0:T(8,128)(2,1)S(1)}, u32[]{:S(2)}, u32[]{:S(2)}) collective-permute-start(bf16[576,512]{1,0:T(8,128)(2,1)S(1)} %fold.5.unused), channel_id=1, source_target_pairs={{0,1},{1,0},{2,6},{3,7},{4,5},{5,4},{6,2},{7,3},{8,9},{9,8},{10,14... | collective-permute-start | bytes 1769480 | tf_op jit(solution)/shard_map/ppermute | solution.py:396
  29.2 3.5 %follow.5 = (bf16[576,512]{1,0:T(8,128)(2,1)S(1)}, bf16[576,512]{1,0:T(8,128)(2,1)S(1)}) custom-call(bf16[576,512]{1,0:T(8,128)(2,1)S(1)} %get-tuple-element.38.unused.refs_0_, f32[2,8,8]{2,1,0:T(8,128)S(1)} %copy-done.7, bf16[768,2048]{1,0:T(8,128)(2,1)S(1)} %bitcast.21, s32[1,768]{1,0:T(1,128)S(1)} %copy-done.13, f32[768,128]{1,0:T(8,128)S(1)} %copy-done.4, ...), custom_call_target="tpu_custom_call" | custom-call | flops 4400000 | bytes 14400 | tf_op jit(solution)/shard_map/follow/pallas_call | solution.py:63
  32.7 0.1 collective-permute-start.7
  32.8 0.0 collective-permute-done.3.refs_1_
  32.8 0.7 collective-permute-start.8
  33.6 5.2 %collective-permute-done.4.refs_2_ = bf16[576,512]{1,0:T(8,128)(2,1)S(1)} collective-permute-done((bf16[576,512]{1,0:T(8,128)(2,1)S(1)}, bf16[576,512]{1,0:T(8,128)(2,1)S(1)}, u32[]{:S(2)}, u32[]{:S(2)}) %collective-permute-start.4) | collective-permute-done | bytes 589856 | tf_op jit(solution)/shard_map/ppermute | solution.py:396
  38.8 1.6 %collective-permute-start.9 = (bf16[576,512]{1,0:T(8,128)(2,1)S(1)}, bf16[576,512]{1,0:T(8,128)(2,1)S(1)}, u32[]{:S(2)}, u32[]{:S(2)}) collective-permute-start(bf16[576,512]{1,0:T(8,128)(2,1)S(1)} %join.5.unused), channel_id=1, source_target_pairs={{0,4},{1,5},{2,3},{3,2},{4,0},{5,1},{6,7},{7,6},{8,12},{9,13},{10,... | collective-permute-start | bytes 1769480 | tf_op jit(solution)/shard_map/ppermute | solution.py:396
  40.4 0.0 collective-permute-done.5.refs_3_
  40.4 1.4 %merge.4 = (f32[2,128,512]{2,1,0:T(8,128)S(1)}, bf16[2,128,512]{2,1,0:T(8,128)(2,1)S(1)}, s32[8,1,144]{2,1,0:T(1,128)S(1)}) custom-call(bf16[576,512]{1,0:T(8,128)(2,1)S(1)} %join.5.unused, bf16[640,512]{1,0:T(8,128)(2,1)S(1)} %copy-done.2, bf16[640,512]{1,0:T(8,128)(2,1)S(1)} %collective-permute-done.refs_1_, ...), custom_call_target="tpu_custom_call" | custom-call | flops 2090000 | bytes 6840 | tf_op jit(solution)/shard_map/merge/pallas_call | solution.py:63
  41.8 1.6 %collective-permute-start.6 = (bf16[2,128,512]{2,1,0:T(8,128)(2,1)S(1)}, bf16[2,128,512]{2,1,0:T(8,128)(2,1)S(1)}, u32[]{:S(2)}, u32[]{:S(2)}) collective-permute-start(bf16[2,128,512]{2,1,0:T(8,128)(2,1)S(1)} %get-tuple-element.41.unused), channel_id=1, source_target_pairs={{0,8},{1,9},{2,10},{3,11},{4,12},{5,13},{6,14},{7,15},{8,0},{9,1},... | collective-permute-start | bytes 786440 | tf_op jit(solution)/shard_map/ppermute | solution.py:396
  43.5 7.2 %collective-permute-done.6.refs_1_ = bf16[2,128,512]{2,1,0:T(8,128)(2,1)S(1)} collective-permute-done((bf16[2,128,512]{2,1,0:T(8,128)(2,1)S(1)}, bf16[2,128,512]{2,1,0:T(8,128)(2,1)S(1)}, u32[]{:S(2)}, u32[]{:S(2)}) %collective-permute-start.6) | collective-permute-done | bytes 262176 | tf_op jit(solution)/shard_map/ppermute | solution.py:396
  50.7 0.0 collective-permute-done.7.refs_1_
  50.8 0.7 collective-permute-start.12
  51.5 0.0 collective-permute-done.8.refs_2_
  51.5 1.6 %collective-permute-start.13 = (bf16[576,512]{1,0:T(8,128)(2,1)S(1)}, bf16[576,512]{1,0:T(8,128)(2,1)S(1)}, u32[]{:S(2)}, u32[]{:S(2)}) collective-permute-start(bf16[576,512]{1,0:T(8,128)(2,1)S(1)} %join.6.unused), channel_id=1, source_target_pairs={{0,4},{1,5},{2,3},{3,2},{4,0},{5,1},{6,7},{7,6},{8,12},{9,13},{10,... | collective-permute-start | bytes 1769480 | tf_op jit(solution)/shard_map/ppermute | solution.py:396
  53.1 0.0 collective-permute-done.9.refs_3_
  53.1 1.2 %merge.5 = (f32[2,128,512]{2,1,0:T(8,128)S(1)}, bf16[2,128,512]{2,1,0:T(8,128)(2,1)S(1)}) custom-call(bf16[576,512]{1,0:T(8,128)(2,1)S(1)} %join.6.unused, bf16[576,512]{1,0:T(8,128)(2,1)S(1)} %get-tuple-element.36.unused.refs_0_, bf16[576,512]{1,0:T(8,128)(2,1)S(1)} %collective-permute-done.1.refs_1_, bf16[576,512]{1,0:T(8,128)(2,1)S(1)} %collective-permute-done.4.refs_2_, ...), custom_call_target="tpu_custom_call" | custom-call | flops 2090000 | bytes 6840 | tf_op jit(solution)/shard_map/merge/pallas_call | solution.py:63
  54.3 1.6 %collective-permute-start.10 = (bf16[2,128,512]{2,1,0:T(8,128)(2,1)S(1)}, bf16[2,128,512]{2,1,0:T(8,128)(2,1)S(1)}, u32[]{:S(2)}, u32[]{:S(2)}) collective-permute-start(bf16[2,128,512]{2,1,0:T(8,128)(2,1)S(1)} %get-tuple-element.46.unused), channel_id=1, source_target_pairs={{0,8},{1,9},{2,10},{3,11},{4,12},{5,13},{6,14},{7,15},{8,0},{9,1},... | collective-permute-start | bytes 786440 | tf_op jit(solution)/shard_map/ppermute | solution.py:396
  56.0 2.6 %collective-permute-start.11 = (bf16[1,128,512]{2,1,0:T(8,128)(2,1)S(1)}, bf16[1,128,512]{2,1,0:T(8,128)(2,1)S(1)}, u32[]{:S(2)}, u32[]{:S(2)}) collective-permute-start(bf16[1,128,512]{2,1,0:T(8,128)(2,1)S(1)} %get-tuple-element.43.unused), channel_id=1, source_target_pairs={{0,16},{1,17},{2,18},{3,19},{4,20},{5,21},{6,22},{7,23},{8,24},{9,... | collective-permute-start | bytes 393224 | tf_op jit(solution)/shard_map/ppermute | solution.py:396
  58.6 6.4 %collective-permute-done.10.refs_1_ = bf16[2,128,512]{2,1,0:T(8,128)(2,1)S(1)} collective-permute-done((bf16[2,128,512]{2,1,0:T(8,128)(2,1)S(1)}, bf16[2,128,512]{2,1,0:T(8,128)(2,1)S(1)}, u32[]{:S(2)}, u32[]{:S(2)}) %collective-permute-start.10) | collective-permute-done | bytes 262176 | tf_op jit(solution)/shard_map/ppermute | solution.py:396
  65.0 0.0 collective-permute-done.11.refs_1_
  65.0 0.0 copy-start.15
  65.0 1.9 %collective-permute-done.12.refs_2_ = bf16[576,512]{1,0:T(8,128)(2,1)S(1)} collective-permute-done((bf16[576,512]{1,0:T(8,128)(2,1)S(1)}, bf16[576,512]{1,0:T(8,128)(2,1)S(1)}, u32[]{:S(2)}, u32[]{:S(2)}) %collective-permute-start.12) | collective-permute-done | bytes 589856 | tf_op jit(solution)/shard_map/ppermute | solution.py:396
  66.9 0.9 join.7.unused
  67.8 0.2 collective-permute-start.16
  68.0 0.0 collective-permute-done.13.refs_3_
  68.0 1.9 %merge.6 = (f32[2,128,512]{2,1,0:T(8,128)S(1)}, bf16[2,128,512]{2,1,0:T(8,128)(2,1)}) custom-call(bf16[576,512]{1,0:T(8,128)(2,1)} %join.7.unused, bf16[576,512]{1,0:T(8,128)(2,1)S(1)} %get-tuple-element.38.unused.refs_0_, bf16[576,512]{1,0:T(8,128)(2,1)S(1)} %collective-permute-done.3.refs_1_, bf16[576,512]{1,0:T(8,128)(2,1)S(1)} %collective-permute-done.8.refs_2_, ...), custom_call_target="tpu_custom_call" | custom-call | flops 2090000 | bytes 6840 | tf_op jit(solution)/shard_map/merge/pallas_call | solution.py:63
  69.9 1.6 %collective-permute-start.15 = (bf16[2,128,512]{2,1,0:T(8,128)(2,1)}, bf16[2,128,512]{2,1,0:T(8,128)(2,1)S(1)}, u32[]{:S(2)}, u32[]{:S(2)}) collective-permute-start(bf16[2,128,512]{2,1,0:T(8,128)(2,1)} %get-tuple-element.50.unused), channel_id=1, source_target_pairs={{0,8},{1,9},{2,10},{3,11},{4,12},{5,13},{6,14},{7,15},{8,0},{9,1},... | collective-permute-start | bytes 786440 | tf_op jit(solution)/shard_map/ppermute | solution.py:396
  71.5 0.1 copy.15.refs_6_
  71.6 2.6 %collective-permute-start.14 = (bf16[1,128,512]{2,1,0:T(8,128)(2,1)S(1)}, bf16[1,128,512]{2,1,0:T(8,128)(2,1)S(1)}, u32[]{:S(2)}, u32[]{:S(2)}) collective-permute-start(bf16[1,128,512]{2,1,0:T(8,128)(2,1)S(1)} %get-tuple-element.48.unused), channel_id=1, source_target_pairs={{0,16},{1,17},{2,18},{3,19},{4,20},{5,21},{6,22},{7,23},{8,24},{9,... | collective-permute-start | bytes 393224 | tf_op jit(solution)/shard_map/ppermute | solution.py:396
  74.2 5.0 %collective-permute-done.14.refs_1_ = bf16[1,128,512]{2,1,0:T(8,128)(2,1)S(1)} collective-permute-done((bf16[1,128,512]{2,1,0:T(8,128)(2,1)S(1)}, bf16[1,128,512]{2,1,0:T(8,128)(2,1)S(1)}, u32[]{:S(2)}, u32[]{:S(2)}) %collective-permute-start.14) | collective-permute-done | bytes 131104 | tf_op jit(solution)/shard_map/ppermute | solution.py:396
  79.2 0.9 copy-done.6
  80.2 0.0 copy-start.11
  80.2 0.0 copy-start.12
  80.2 0.0 collective-permute-done.15.refs_1_
  80.3 3.4 %collective-permute-start.17 = (bf16[1,128,512]{2,1,0:T(8,128)(2,1)S(1)}, bf16[1,128,512]{2,1,0:T(8,128)(2,1)S(1)}, u32[]{:S(2)}, u32[]{:S(2)}) collective-permute-start(bf16[1,128,512]{2,1,0:T(8,128)(2,1)S(1)} %get-tuple-element.53.unused), channel_id=1, source_target_pairs={{0,16},{1,17},{2,18},{3,19},{4,20},{5,21},{6,22},{7,23},{8,24},{9,... | collective-permute-start | bytes 393224 | tf_op jit(solution)/shard_map/ppermute | solution.py:396
  83.8 2.3 %merge.7 = (f32[2,128,512]{2,1,0:T(8,128)S(1)}, bf16[2,128,512]{2,1,0:T(8,128)(2,1)S(1)}) custom-call(bf16[1,128,512]{2,1,0:T(8,128)(2,1)S(1)} %get-tuple-element.53.unused, bf16[576,512]{1,0:T(8,128)(2,1)S(1)} %get-tuple-element.39.unused.refs_0_, bf16[576,512]{1,0:T(8,128)(2,1)S(1)} %collective-permute-done.7.refs_1_, ...), custom_call_target="tpu_custom_call" | custom-call | flops 2090000 | bytes 6840 | tf_op jit(solution)/shard_map/merge/pallas_call | solution.py:63
  86.0 0.7 collective-permute-start.18
  86.8 0.6 collective-permute-done.17.refs_1_
  87.4 5.5 %collective-permute-done.18.refs_1_ = bf16[2,128,512]{2,1,0:T(8,128)(2,1)S(1)} collective-permute-done((bf16[2,128,512]{2,1,0:T(8,128)(2,1)S(1)}, bf16[2,128,512]{2,1,0:T(8,128)(2,1)S(1)}, u32[]{:S(2)}, u32[]{:S(2)}) %collective-permute-start.18) | collective-permute-done | bytes 262176 | tf_op jit(solution)/shard_map/ppermute | solution.py:396
  92.9 0.1 halve.7
  93.0 0.2 collective-permute-start.20
  93.2 2.9 %collective-permute-start.21 = (bf16[1,512]{1,0:T(2,128)(2,1)S(1)}, bf16[1,512]{1,0:T(2,128)(2,1)S(1)}, u32[]{:S(2)}, u32[]{:S(2)}) collective-permute-start(bf16[1,512]{1,0:T(2,128)(2,1)S(1)} %fusion), channel_id=1, source_target_pairs={{0,17},{1,16},{2,19},{3,18},{4,21},{5,20},{6,23},{7,22},{8,25},{9,... | collective-permute-start | bytes 3080 | tf_op jit(solution)/shard_map/ppermute | solution.py:396
  96.1 1.4 %collective-permute-start.19 = (bf16[1,128,512]{2,1,0:T(8,128)(2,1)S(1)}, bf16[1,128,512]{2,1,0:T(8,128)(2,1)S(1)}, u32[]{:S(2)}, u32[]{:S(2)}) collective-permute-start(bf16[1,128,512]{2,1,0:T(8,128)(2,1)S(1)} %get-tuple-element.57.unused), channel_id=1, source_target_pairs={{0,16},{1,17},{2,18},{3,19},{4,20},{5,21},{6,22},{7,23},{8,24},{9,... | collective-permute-start | bytes 393224 | tf_op jit(solution)/shard_map/ppermute | solution.py:396
  97.5 2.7 %factor.1.unused.refs_6_ = f32[128,2048]{1,0:T(8,128)S(1)} custom-call(bf16[1,128,512]{2,1,0:T(8,128)(2,1)S(1)} %get-tuple-element.57.unused, s32[128,256]{1,0:T(8,128)S(1)} %bitcast.22, f32[128,256]{1,0:T(8,128)S(1)} %bitcast.23, f32[128,256]{1,0:T(8,128)S(1)} %bitcast.24, f32[128,256]{1,0:T(8,128)S(1)} %bitcast.25, s32[128,256]{1,0:T(8,128)S(1)} %bitcast.26, ...), custom_call_target="tpu_custom_call" | custom-call | flops 3300000 | bytes 10800 | tf_op jit(solution)/shard_map/factor/pallas_call | solution.py:63
  100.2 0.0 collective-permute-done.21
  100.2 0.0 collective-permute-done.20
  100.3 1.7 %collective-permute-done.19.refs_1_ = bf16[1,128,512]{2,1,0:T(8,128)(2,1)S(1)} collective-permute-done((bf16[1,128,512]{2,1,0:T(8,128)(2,1)S(1)}, bf16[1,128,512]{2,1,0:T(8,128)(2,1)S(1)}, u32[]{:S(2)}, u32[]{:S(2)}) %collective-permute-start.19) | collective-permute-done | bytes 131104 | tf_op jit(solution)/shard_map/ppermute | solution.py:396
  102.0 1.2 %finish.1 = bf16[128,2048]{1,0:T(8,128)(2,1)} custom-call(f32[128,512]{1,0:T(8,128)S(1)} %total.7.unused.refs_3_, f32[128,512]{1,0:T(8,128)S(1)} %total.4.unused.refs_0_, f32[128,512]{1,0:T(8,128)S(1)} %total.5.unused.refs_1_, f32[128,512]{1,0:T(8,128)S(1)} %total.6.unused.refs_2_, f32[128,512]{1,0:T(8,128)S(1)} %total.7.unused.refs_3_, ...), custom_call_target="tpu_custom_call" | custom-call | flops 1100000 | bytes 3600 | tf_op jit(solution)/shard_map/finish/pallas_call | solution.py:63
  (47 shorter events, 0.7 us)
Async XLA Ops:
  0.0 13.4 %copy-start.3 = (bf16[4,256,256]{2,1,0:T(8,128)(2,1)S(1)}, bf16[4,256,256]{2,1,0:T(8,128)(2,1)}, u32[]{:S(2)}) copy-start(bf16[4,256,256]{2,1,0:T(8,128)(2,1)} %refs_4_.5) | copy-start | bytes 1572868
  0.0 13.4 %copy-start.7 = (f32[2,8,8]{2,1,0:T(8,128)S(1)}, f32[2,8,8]{2,1,0:T(8,128)}, u32[]{:S(2)}) copy-start(f32[2,8,8]{2,1,0:T(8,128)} %refs_0_.5) | copy-start | bytes 1540
  6.9 2.5 %collective-permute-start = (bf16[640,512]{1,0:T(8,128)(2,1)}, bf16[640,512]{1,0:T(8,128)(2,1)S(1)}, u32[]{:S(2)}, u32[]{:S(2)}) collective-permute-start(bf16[640,512]{1,0:T(8,128)(2,1)} %get-tuple-element.33), channel_id=1, source_target_pairs={{0,2},{1,3},{2,0},{3,1},{4,6},{5,7},{6,4},{7,5},{8,10},{9,11},{10,... | collective-permute-start | bytes 1966088 | tf_op jit(solution)/shard_map/ppermute | solution.py:396
  9.4 1.1 %copy-start.1 = (bf16[640,512]{1,0:T(8,128)(2,1)S(1)}, bf16[640,512]{1,0:T(8,128)(2,1)}, u32[]{:S(2)}) copy-start(bf16[640,512]{1,0:T(8,128)(2,1)} %get-tuple-element.32.unused.refs_0_) | copy-start | bytes 1966084
  10.5 12.1 %collective-permute-start.2 = (bf16[640,512]{1,0:T(8,128)(2,1)S(1)}, bf16[640,512]{1,0:T(8,128)(2,1)S(1)}, u32[]{:S(2)}, u32[]{:S(2)}) collective-permute-start(bf16[640,512]{1,0:T(8,128)(2,1)S(1)} %fold.4.unused), channel_id=1, source_target_pairs={{0,1},{1,0},{2,6},{3,7},{4,5},{5,4},{6,2},{7,3},{8,9},{9,8},{10,14... | collective-permute-start | bytes 1966088 | tf_op jit(solution)/shard_map/ppermute | solution.py:396
  13.4 1.9 %copy-start = (bf16[1,1,768,2048]{3,2,1,0:T(8,128)(2,1)S(1)}, bf16[1,1,768,2048]{3,2,1,0:T(8,128)(2,1)}, u32[]{:S(2)}) copy-start(bf16[1,1,768,2048]{3,2,1,0:T(8,128)(2,1)} %param.14) | copy-start | bytes 9437188
  15.3 1.0 copy-start.4
  16.3 0.7 copy-start.13
  17.0 5.6 %copy-start.2 = (bf16[640,512]{1,0:T(8,128)(2,1)S(1)}, bf16[640,512]{1,0:T(8,128)(2,1)}, u32[]{:S(2)}) copy-start(bf16[640,512]{1,0:T(8,128)(2,1)} %get-tuple-element.32.unused.refs_0_) | copy-start | bytes 1966084
  20.5 2.1 %collective-permute-start.1 = (bf16[576,512]{1,0:T(8,128)(2,1)S(1)}, bf16[576,512]{1,0:T(8,128)(2,1)S(1)}, u32[]{:S(2)}, u32[]{:S(2)}) collective-permute-start(bf16[576,512]{1,0:T(8,128)(2,1)S(1)} %get-tuple-element.37), channel_id=1, source_target_pairs={{0,2},{1,3},{2,0},{3,1},{4,6},{5,7},{6,4},{7,5},{8,10},{9,11},{10,... | collective-permute-start | bytes 1769480 | tf_op jit(solution)/shard_map/ppermute | solution.py:396
  22.7 17.7 %collective-permute-start.5 = (bf16[640,512]{1,0:T(8,128)(2,1)S(1)}, bf16[640,512]{1,0:T(8,128)(2,1)S(1)}, u32[]{:S(2)}, u32[]{:S(2)}) collective-permute-start(bf16[640,512]{1,0:T(8,128)(2,1)S(1)} %join.4.unused), channel_id=1, source_target_pairs={{0,4},{1,5},{2,3},{3,2},{4,0},{5,1},{6,7},{7,6},{8,12},{9,13},{10,... | collective-permute-start | bytes 1966088 | tf_op jit(solution)/shard_map/ppermute | solution.py:396
  27.7 5.1 %collective-permute-start.3 = (bf16[576,512]{1,0:T(8,128)(2,1)S(1)}, bf16[576,512]{1,0:T(8,128)(2,1)S(1)}, u32[]{:S(2)}, u32[]{:S(2)}) collective-permute-start(bf16[576,512]{1,0:T(8,128)(2,1)S(1)} %get-tuple-element.40), channel_id=1, source_target_pairs={{0,2},{1,3},{2,0},{3,1},{4,6},{5,7},{6,4},{7,5},{8,10},{9,11},{10,... | collective-permute-start | bytes 1769480 | tf_op jit(solution)/shard_map/ppermute | solution.py:396
  27.8 11.0 %collective-permute-start.4 = (bf16[576,512]{1,0:T(8,128)(2,1)S(1)}, bf16[576,512]{1,0:T(8,128)(2,1)S(1)}, u32[]{:S(2)}, u32[]{:S(2)}) collective-permute-start(bf16[576,512]{1,0:T(8,128)(2,1)S(1)} %fold.5.unused), channel_id=1, source_target_pairs={{0,1},{1,0},{2,6},{3,7},{4,5},{5,4},{6,2},{7,3},{8,9},{9,8},{10,14... | collective-permute-start | bytes 1769480 | tf_op jit(solution)/shard_map/ppermute | solution.py:396
  32.7 18.0 %collective-permute-start.7 = (bf16[576,512]{1,0:T(8,128)(2,1)S(1)}, bf16[576,512]{1,0:T(8,128)(2,1)S(1)}, u32[]{:S(2)}, u32[]{:S(2)}) collective-permute-start(bf16[576,512]{1,0:T(8,128)(2,1)S(1)} %get-tuple-element.44), channel_id=1, source_target_pairs={{0,2},{1,3},{2,0},{3,1},{4,6},{5,7},{6,4},{7,5},{8,10},{9,11},{10,... | collective-permute-start | bytes 1769480 | tf_op jit(solution)/shard_map/ppermute | solution.py:396
  32.8 18.6 %collective-permute-start.8 = (bf16[576,512]{1,0:T(8,128)(2,1)S(1)}, bf16[576,512]{1,0:T(8,128)(2,1)S(1)}, u32[]{:S(2)}, u32[]{:S(2)}) collective-permute-start(bf16[576,512]{1,0:T(8,128)(2,1)S(1)} %fold.6.unused), channel_id=1, source_target_pairs={{0,1},{1,0},{2,6},{3,7},{4,5},{5,4},{6,2},{7,3},{8,9},{9,8},{10,14... | collective-permute-start | bytes 1769480 | tf_op jit(solution)/shard_map/ppermute | solution.py:396
  38.8 14.3 %collective-permute-start.9 = (bf16[576,512]{1,0:T(8,128)(2,1)S(1)}, bf16[576,512]{1,0:T(8,128)(2,1)S(1)}, u32[]{:S(2)}, u32[]{:S(2)}) collective-permute-start(bf16[576,512]{1,0:T(8,128)(2,1)S(1)} %join.5.unused), channel_id=1, source_target_pairs={{0,4},{1,5},{2,3},{3,2},{4,0},{5,1},{6,7},{7,6},{8,12},{9,13},{10,... | collective-permute-start | bytes 1769480 | tf_op jit(solution)/shard_map/ppermute | solution.py:396
  41.8 8.9 %collective-permute-start.6 = (bf16[2,128,512]{2,1,0:T(8,128)(2,1)S(1)}, bf16[2,128,512]{2,1,0:T(8,128)(2,1)S(1)}, u32[]{:S(2)}, u32[]{:S(2)}) collective-permute-start(bf16[2,128,512]{2,1,0:T(8,128)(2,1)S(1)} %get-tuple-element.41.unused), channel_id=1, source_target_pairs={{0,8},{1,9},{2,10},{3,11},{4,12},{5,13},{6,14},{7,15},{8,0},{9,1},... | collective-permute-start | bytes 786440 | tf_op jit(solution)/shard_map/ppermute | solution.py:396
  50.8 16.2 %collective-permute-start.12 = (bf16[576,512]{1,0:T(8,128)(2,1)S(1)}, bf16[576,512]{1,0:T(8,128)(2,1)S(1)}, u32[]{:S(2)}, u32[]{:S(2)}) collective-permute-start(bf16[576,512]{1,0:T(8,128)(2,1)S(1)} %fold.7.unused), channel_id=1, source_target_pairs={{0,1},{1,0},{2,6},{3,7},{4,5},{5,4},{6,2},{7,3},{8,9},{9,8},{10,14... | collective-permute-start | bytes 1769480 | tf_op jit(solution)/shard_map/ppermute | solution.py:396
  51.5 16.5 %collective-permute-start.13 = (bf16[576,512]{1,0:T(8,128)(2,1)S(1)}, bf16[576,512]{1,0:T(8,128)(2,1)S(1)}, u32[]{:S(2)}, u32[]{:S(2)}) collective-permute-start(bf16[576,512]{1,0:T(8,128)(2,1)S(1)} %join.6.unused), channel_id=1, source_target_pairs={{0,4},{1,5},{2,3},{3,2},{4,0},{5,1},{6,7},{7,6},{8,12},{9,13},{10,... | collective-permute-start | bytes 1769480 | tf_op jit(solution)/shard_map/ppermute | solution.py:396
  54.3 10.6 %collective-permute-start.10 = (bf16[2,128,512]{2,1,0:T(8,128)(2,1)S(1)}, bf16[2,128,512]{2,1,0:T(8,128)(2,1)S(1)}, u32[]{:S(2)}, u32[]{:S(2)}) collective-permute-start(bf16[2,128,512]{2,1,0:T(8,128)(2,1)S(1)} %get-tuple-element.46.unused), channel_id=1, source_target_pairs={{0,8},{1,9},{2,10},{3,11},{4,12},{5,13},{6,14},{7,15},{8,0},{9,1},... | collective-permute-start | bytes 786440 | tf_op jit(solution)/shard_map/ppermute | solution.py:396
  56.0 9.0 %collective-permute-start.11 = (bf16[1,128,512]{2,1,0:T(8,128)(2,1)S(1)}, bf16[1,128,512]{2,1,0:T(8,128)(2,1)S(1)}, u32[]{:S(2)}, u32[]{:S(2)}) collective-permute-start(bf16[1,128,512]{2,1,0:T(8,128)(2,1)S(1)} %get-tuple-element.43.unused), channel_id=1, source_target_pairs={{0,16},{1,17},{2,18},{3,19},{4,20},{5,21},{6,22},{7,23},{8,24},{9,... | collective-permute-start | bytes 393224 | tf_op jit(solution)/shard_map/ppermute | solution.py:396
  65.0 3.0 %copy-start.5 = (f32[1,128,512]{2,1,0:T(8,128)}, f32[1,128,512]{2,1,0:T(8,128)S(1)}, u32[]{:S(2)}) copy-start(f32[1,128,512]{2,1,0:T(8,128)S(1)} %get-tuple-element.51.refs_0_) | copy-start | bytes 786436
  65.0 6.5 %copy-start.15 = (f32[8,3]{0,1:T(4,128)S(1)}, f32[8,3]{0,1:T(4,128)}, u32[]{:S(2)}) copy-start(f32[8,3]{0,1:T(4,128)} %param.24) | copy-start | bytes 292
  67.8 15.9 %collective-permute-start.16 = (bf16[576,512]{1,0:T(8,128)(2,1)}, bf16[576,512]{1,0:T(8,128)(2,1)}, u32[]{:S(2)}, u32[]{:S(2)}) collective-permute-start(bf16[576,512]{1,0:T(8,128)(2,1)} %join.7.unused), channel_id=1, source_target_pairs={{0,4},{1,5},{2,3},{3,2},{4,0},{5,1},{6,7},{7,6},{8,12},{9,13},{10,... | collective-permute-start | bytes 1769480 | tf_op jit(solution)/shard_map/ppermute | solution.py:396
  69.9 10.3 %collective-permute-start.15 = (bf16[2,128,512]{2,1,0:T(8,128)(2,1)}, bf16[2,128,512]{2,1,0:T(8,128)(2,1)S(1)}, u32[]{:S(2)}, u32[]{:S(2)}) collective-permute-start(bf16[2,128,512]{2,1,0:T(8,128)(2,1)} %get-tuple-element.50.unused), channel_id=1, source_target_pairs={{0,8},{1,9},{2,10},{3,11},{4,12},{5,13},{6,14},{7,15},{8,0},{9,1},... | collective-permute-start | bytes 786440 | tf_op jit(solution)/shard_map/ppermute | solution.py:396
  71.6 7.7 %collective-permute-start.14 = (bf16[1,128,512]{2,1,0:T(8,128)(2,1)S(1)}, bf16[1,128,512]{2,1,0:T(8,128)(2,1)S(1)}, u32[]{:S(2)}, u32[]{:S(2)}) collective-permute-start(bf16[1,128,512]{2,1,0:T(8,128)(2,1)S(1)} %get-tuple-element.48.unused), channel_id=1, source_target_pairs={{0,16},{1,17},{2,18},{3,19},{4,20},{5,21},{6,22},{7,23},{8,24},{9,... | collective-permute-start | bytes 393224 | tf_op jit(solution)/shard_map/ppermute | solution.py:396
  79.2 0.9 copy-start.6
  80.2 15.9 %copy-start.14 = (f32[8,33]{1,0:T(8,128)S(1)}, f32[8,33]{1,0:T(8,128)}, u32[]{:S(2)}) copy-start(f32[8,33]{1,0:T(8,128)} %param.21) | copy-start | bytes 3172
  80.2 17.3 %copy-start.8 = (s32[1,128,256]{2,1,0:T(8,128)S(1)}, s32[1,128,256]{2,1,0:T(8,128)}, u32[]{:S(2)}) copy-start(s32[1,128,256]{2,1,0:T(8,128)} %param.22) | copy-start | bytes 393220
  80.2 17.3 %copy-start.9 = (f32[1,128,256]{2,1,0:T(8,128)S(1)}, f32[1,128,256]{2,1,0:T(8,128)}, u32[]{:S(2)}) copy-start(f32[1,128,256]{2,1,0:T(8,128)} %param.23) | copy-start | bytes 393220
  80.2 17.3 %copy-start.10 = (f32[1,128,256]{2,1,0:T(8,128)S(1)}, f32[1,128,256]{2,1,0:T(8,128)}, u32[]{:S(2)}) copy-start(f32[1,128,256]{2,1,0:T(8,128)} %param.25) | copy-start | bytes 393220
  80.2 17.3 %copy-start.11 = (f32[1,128,256]{2,1,0:T(8,128)S(1)}, f32[1,128,256]{2,1,0:T(8,128)}, u32[]{:S(2)}) copy-start(f32[1,128,256]{2,1,0:T(8,128)} %param.26) | copy-start | bytes 393220
  80.2 17.3 %copy-start.12 = (s32[1,128,256]{2,1,0:T(8,128)S(1)}, s32[1,128,256]{2,1,0:T(8,128)}, u32[]{:S(2)}) copy-start(s32[1,128,256]{2,1,0:T(8,128)} %param.27) | copy-start | bytes 393220
  80.3 7.0 %collective-permute-start.17 = (bf16[1,128,512]{2,1,0:T(8,128)(2,1)S(1)}, bf16[1,128,512]{2,1,0:T(8,128)(2,1)S(1)}, u32[]{:S(2)}, u32[]{:S(2)}) collective-permute-start(bf16[1,128,512]{2,1,0:T(8,128)(2,1)S(1)} %get-tuple-element.53.unused), channel_id=1, source_target_pairs={{0,16},{1,17},{2,18},{3,19},{4,20},{5,21},{6,22},{7,23},{8,24},{9,... | collective-permute-start | bytes 393224 | tf_op jit(solution)/shard_map/ppermute | solution.py:396
  86.0 6.8 %collective-permute-start.18 = (bf16[2,128,512]{2,1,0:T(8,128)(2,1)S(1)}, bf16[2,128,512]{2,1,0:T(8,128)(2,1)S(1)}, u32[]{:S(2)}, u32[]{:S(2)}) collective-permute-start(bf16[2,128,512]{2,1,0:T(8,128)(2,1)S(1)} %get-tuple-element.54.unused), channel_id=1, source_target_pairs={{0,8},{1,9},{2,10},{3,11},{4,12},{5,13},{6,14},{7,15},{8,0},{9,1},... | collective-permute-start | bytes 786440 | tf_op jit(solution)/shard_map/ppermute | solution.py:396
  93.0 7.3 %collective-permute-start.20 = (f32[1,2048]{1,0:T(1,128)S(1)}, f32[1,2048]{1,0:T(1,128)S(1)}, u32[]{:S(2)}, u32[]{:S(2)}) collective-permute-start(f32[1,2048]{1,0:T(1,128)S(1)} %broadcast_select_fusion.2), channel_id=1, source_target_pairs={{0,1},{1,0},{2,3},{3,2},{4,5},{5,4},{6,7},{7,6},{8,9},{9,8},{10,11... | collective-permute-start | bytes 24584 | tf_op jit(solution)/shard_map/ppermute | solution.py:396
  93.2 7.0 %collective-permute-start.21 = (bf16[1,512]{1,0:T(2,128)(2,1)S(1)}, bf16[1,512]{1,0:T(2,128)(2,1)S(1)}, u32[]{:S(2)}, u32[]{:S(2)}) collective-permute-start(bf16[1,512]{1,0:T(2,128)(2,1)S(1)} %fusion), channel_id=1, source_target_pairs={{0,17},{1,16},{2,19},{3,18},{4,21},{5,20},{6,23},{7,22},{8,25},{9,... | collective-permute-start | bytes 3080 | tf_op jit(solution)/shard_map/ppermute | solution.py:396
  96.1 5.9 %collective-permute-start.19 = (bf16[1,128,512]{2,1,0:T(8,128)(2,1)S(1)}, bf16[1,128,512]{2,1,0:T(8,128)(2,1)S(1)}, u32[]{:S(2)}, u32[]{:S(2)}) collective-permute-start(bf16[1,128,512]{2,1,0:T(8,128)(2,1)S(1)} %get-tuple-element.57.unused), channel_id=1, source_target_pairs={{0,16},{1,17},{2,18},{3,19},{4,20},{5,21},{6,22},{7,23},{8,24},{9,... | collective-permute-start | bytes 393224 | tf_op jit(solution)/shard_map/ppermute | solution.py:396

commit v5 on v4

--- a/solution.py
+++ b/solution.py
@@ -32,9 +32,9 @@
     "g0",
     "j3",
     "m2",
+    "m3",
     "g1",
     "h2",
-    "m3",
     "g2",
     "h3",
     "x0",
@@ -507,6 +507,8 @@
 
     def forward(i, keep, sends):
         chunk = chunks[i]
+        if i == len(chunks) - 1 and keep.shape[0] == 1:
+            chunk["edges"] = edges(keep, sends[-1].reshape(cells, -1))
         chunk["keep"] = keep
         chunk["away"] = sends[-1]
         chunk["arrived"] = [exchange(array, bits["z"] << chunk["hops"]) for array in sends]
@@ -539,6 +541,8 @@
         return forward(i, outs[0], outs[1:])
 
     def halve(i, after):
+        if chunks[i]["keep"].shape[0] == 1:
+            return after
         keep, arrived = chunks[i]["keep"], chunks[i]["arrived"]
         half, columns = keep.shape[0] // 2, keep.shape[2]
         outs = call(
@@ -553,8 +557,6 @@
             (keep, *arrived),
             after,
         )
-        if i == len(chunks) - 1 and half == 1:
-            chunks[i]["edges"] = edges(outs[0], outs[-1].reshape(cells, -1))
         return forward(i, outs[0], outs[1:])
 
     def total(i, after):

time: 104 us -> 102 us (0.981)
  waiting for transfers between devices: 37.5 us -> 33.4 us
  starting transfers between devices: 30.1 us -> 32.7 us
    ppermute x22, waiting for transfers between devices: 37.5 us -> 33.4 us  [exchange(): return lax.ppermute(array, ('tile', 'row'), pairs)]
    ppermute x22, starting transfers between devices: 30.1 us -> 32.7 us  [exchange(): return lax.ppermute(array, ('tile', 'row'), pairs)]
    unnamed x33 -> x29, local copies, waits for them, and re-layouts: 5.72 us -> 4.76 us
  transfers between devices with their start and end apart: 22 -> 22, of which waited for: 10 -> 10; matrix products, arithmetic and copies ran while one was open for 0% -> 0% of each run, Pallas kernels for 21% -> 22%
where the time goes in v5:
time: 102 us; the launch traced here: 101 us
  waiting for transfers between devices  33.4 us (33%)
  starting transfers between devices  32.7 us (32%)
  Pallas kernels  30.1 us (30%)
  local copies, waits for them, and re-layouts  4.79 us (5%)
    ppermute x22, waiting for transfers between devices, exchange(): return lax.ppermute(array, ('tile', 'row'), pairs)  33.4 us
    ppermute x22, starting transfers between devices, exchange(): return lax.ppermute(array, ('tile', 'row'), pairs)  32.7 us
    pallas_call x26, Pallas kernels, call(): pl.pallas_call(body, out_shape=out_shape, in_specs=specs, out_specs=jax.t...  30.1 us
    unnamed x29, local copies, waits for them, and re-layouts  4.76 us
  transfers between devices with their start and end apart: 22, of which 10 were waited for; matrix products, arithmetic and copies ran while one was open for 0% of the time, Pallas kernels for 22%

profile of v5, /device:TPU:0, one launch (start us, length us, event | category | flops | bytes accessed | tf_op | source)
XLA Modules:
  0.0 101.3 jit_solution(12965294841191597910)
XLA Ops:
  0.0 6.8 %lead.1 = (bf16[640,512]{1,0:T(8,128)(2,1)}, bf16[640,512]{1,0:T(8,128)(2,1)}, s32[1,768]{1,0:T(1,128)}, f32[768,128]{1,0:T(8,128)}) custom-call(s32[1]{0:T(128)} %bitcast.refs_0_, f32[2,8,8]{2,1,0:T(8,128)} %refs_0_.5, bf16[768,2048]{1,0:T(8,128)(2,1)} %bitcast.18, s32[1,768]{1,0:T(1,128)} %bitcast.27, s32[1,768]{1,0:T(1,128)} %bitcast.28, ...), custom_call_target="tpu_custom_call" | custom-call | flops 6600000 | bytes 21600 | tf_op jit(solution)/shard_map/lead/pallas_call | solution.py:63
  6.9 0.5 collective-permute-start
  7.4 1.9 %collective-permute-done.refs_1_ = bf16[640,512]{1,0:T(8,128)(2,1)S(1)} collective-permute-done((bf16[640,512]{1,0:T(8,128)(2,1)}, bf16[640,512]{1,0:T(8,128)(2,1)S(1)}, u32[]{:S(2)}, u32[]{:S(2)}) %collective-permute-start) | collective-permute-done | bytes 655392 | tf_op jit(solution)/shard_map/ppermute | solution.py:396
  9.3 1.1 %copy-done.1 = bf16[640,512]{1,0:T(8,128)(2,1)S(1)} copy-done((bf16[640,512]{1,0:T(8,128)(2,1)S(1)}, bf16[640,512]{1,0:T(8,128)(2,1)}, u32[]{:S(2)}) %copy-start.1) | copy-done | bytes 655384
  10.5 2.9 %collective-permute-start.2 = (bf16[640,512]{1,0:T(8,128)(2,1)S(1)}, bf16[640,512]{1,0:T(8,128)(2,1)S(1)}, u32[]{:S(2)}, u32[]{:S(2)}) collective-permute-start(bf16[640,512]{1,0:T(8,128)(2,1)S(1)} %fold.4.unused), channel_id=1, source_target_pairs={{0,1},{1,0},{2,6},{3,7},{4,5},{5,4},{6,2},{7,3},{8,9},{9,8},{10,14... | collective-permute-start | bytes 1966088 | tf_op jit(solution)/shard_map/ppermute | solution.py:396
  13.4 1.9 %copy-done = bf16[1,1,768,2048]{3,2,1,0:T(8,128)(2,1)S(1)} copy-done((bf16[1,1,768,2048]{3,2,1,0:T(8,128)(2,1)S(1)}, bf16[1,1,768,2048]{3,2,1,0:T(8,128)(2,1)}, u32[]{:S(2)}) %copy-start) | copy-done | bytes 3145752
  15.3 1.0 copy-done.4
  16.3 0.7 copy-done.11
  17.0 3.5 %follow.3 = (bf16[576,512]{1,0:T(8,128)(2,1)S(1)}, bf16[576,512]{1,0:T(8,128)(2,1)S(1)}) custom-call(bf16[640,512]{1,0:T(8,128)(2,1)S(1)} %fold.4.unused, f32[2,8,8]{2,1,0:T(8,128)S(1)} %copy-done.5, bf16[768,2048]{1,0:T(8,128)(2,1)S(1)} %bitcast.19, s32[1,768]{1,0:T(1,128)S(1)} %copy-done.11, f32[768,128]{1,0:T(8,128)S(1)} %copy-done.4, ...), custom_call_target="tpu_custom_call" | custom-call | flops 4400000 | bytes 14400 | tf_op jit(solution)/shard_map/follow/pallas_call | solution.py:63
  20.4 0.1 collective-permute-start.1
  20.5 2.0 %collective-permute-done.1.refs_1_ = bf16[576,512]{1,0:T(8,128)(2,1)S(1)} collective-permute-done((bf16[576,512]{1,0:T(8,128)(2,1)S(1)}, bf16[576,512]{1,0:T(8,128)(2,1)S(1)}, u32[]{:S(2)}, u32[]{:S(2)}) %collective-permute-start.1) | collective-permute-done | bytes 589856 | tf_op jit(solution)/shard_map/ppermute | solution.py:396
  22.5 0.0 collective-permute-done.2.refs_2_
  22.6 1.6 %collective-permute-start.5 = (bf16[640,512]{1,0:T(8,128)(2,1)S(1)}, bf16[640,512]{1,0:T(8,128)(2,1)S(1)}, u32[]{:S(2)}, u32[]{:S(2)}) collective-permute-start(bf16[640,512]{1,0:T(8,128)(2,1)S(1)} %join.4.unused), channel_id=1, source_target_pairs={{0,4},{1,5},{2,3},{3,2},{4,0},{5,1},{6,7},{7,6},{8,12},{9,13},{10,... | collective-permute-start | bytes 1966088 | tf_op jit(solution)/shard_map/ppermute | solution.py:396
  24.2 3.5 %follow.4 = (bf16[576,512]{1,0:T(8,128)(2,1)S(1)}, bf16[576,512]{1,0:T(8,128)(2,1)S(1)}) custom-call(bf16[640,512]{1,0:T(8,128)(2,1)S(1)} %join.4.unused, f32[2,8,8]{2,1,0:T(8,128)S(1)} %copy-done.5, bf16[768,2048]{1,0:T(8,128)(2,1)S(1)} %bitcast.20, s32[1,768]{1,0:T(1,128)S(1)} %copy-done.11, f32[768,128]{1,0:T(8,128)S(1)} %copy-done.4, ...), custom_call_target="tpu_custom_call" | custom-call | flops 4400000 | bytes 14400 | tf_op jit(solution)/shard_map/follow/pallas_call | solution.py:63
  27.7 0.1 collective-permute-start.3
  27.7 1.5 %collective-permute-start.4 = (bf16[576,512]{1,0:T(8,128)(2,1)S(1)}, bf16[576,512]{1,0:T(8,128)(2,1)S(1)}, u32[]{:S(2)}, u32[]{:S(2)}) collective-permute-start(bf16[576,512]{1,0:T(8,128)(2,1)S(1)} %fold.5.unused), channel_id=1, source_target_pairs={{0,1},{1,0},{2,6},{3,7},{4,5},{5,4},{6,2},{7,3},{8,9},{9,8},{10,14... | collective-permute-start | bytes 1769480 | tf_op jit(solution)/shard_map/ppermute | solution.py:396
  29.2 3.5 %follow.5 = (bf16[576,512]{1,0:T(8,128)(2,1)S(1)}, bf16[576,512]{1,0:T(8,128)(2,1)S(1)}) custom-call(bf16[576,512]{1,0:T(8,128)(2,1)S(1)} %get-tuple-element.38.unused.refs_0_, f32[2,8,8]{2,1,0:T(8,128)S(1)} %copy-done.5, bf16[768,2048]{1,0:T(8,128)(2,1)S(1)} %bitcast.21, s32[1,768]{1,0:T(1,128)S(1)} %copy-done.11, f32[768,128]{1,0:T(8,128)S(1)} %copy-done.4, ...), custom_call_target="tpu_custom_call" | custom-call | flops 4400000 | bytes 14400 | tf_op jit(solution)/shard_map/follow/pallas_call | solution.py:63
  32.7 0.1 collective-permute-start.7
  32.8 0.0 collective-permute-done.3.refs_1_
  32.8 0.7 collective-permute-start.8
  33.5 5.2 %collective-permute-done.4.refs_2_ = bf16[576,512]{1,0:T(8,128)(2,1)S(1)} collective-permute-done((bf16[576,512]{1,0:T(8,128)(2,1)S(1)}, bf16[576,512]{1,0:T(8,128)(2,1)S(1)}, u32[]{:S(2)}, u32[]{:S(2)}) %collective-permute-start.4) | collective-permute-done | bytes 589856 | tf_op jit(solution)/shard_map/ppermute | solution.py:396
  38.8 1.6 %collective-permute-start.9 = (bf16[576,512]{1,0:T(8,128)(2,1)S(1)}, bf16[576,512]{1,0:T(8,128)(2,1)S(1)}, u32[]{:S(2)}, u32[]{:S(2)}) collective-permute-start(bf16[576,512]{1,0:T(8,128)(2,1)S(1)} %join.5.unused), channel_id=1, source_target_pairs={{0,4},{1,5},{2,3},{3,2},{4,0},{5,1},{6,7},{7,6},{8,12},{9,13},{10,... | collective-permute-start | bytes 1769480 | tf_op jit(solution)/shard_map/ppermute | solution.py:396
  40.4 0.0 collective-permute-done.5.refs_3_
  40.4 1.4 %merge.4 = (f32[2,128,512]{2,1,0:T(8,128)S(1)}, bf16[2,128,512]{2,1,0:T(8,128)(2,1)S(1)}, s32[8,1,144]{2,1,0:T(1,128)S(1)}) custom-call(bf16[576,512]{1,0:T(8,128)(2,1)S(1)} %join.5.unused, bf16[640,512]{1,0:T(8,128)(2,1)S(1)} %copy-done.2, bf16[640,512]{1,0:T(8,128)(2,1)S(1)} %collective-permute-done.refs_1_, ...), custom_call_target="tpu_custom_call" | custom-call | flops 2090000 | bytes 6840 | tf_op jit(solution)/shard_map/merge/pallas_call | solution.py:63
  41.8 1.6 %collective-permute-start.6 = (bf16[2,128,512]{2,1,0:T(8,128)(2,1)S(1)}, bf16[2,128,512]{2,1,0:T(8,128)(2,1)S(1)}, u32[]{:S(2)}, u32[]{:S(2)}) collective-permute-start(bf16[2,128,512]{2,1,0:T(8,128)(2,1)S(1)} %get-tuple-element.41.unused), channel_id=1, source_target_pairs={{0,8},{1,9},{2,10},{3,11},{4,12},{5,13},{6,14},{7,15},{8,0},{9,1},... | collective-permute-start | bytes 786440 | tf_op jit(solution)/shard_map/ppermute | solution.py:396
  43.4 7.3 %collective-permute-done.6.refs_1_ = bf16[2,128,512]{2,1,0:T(8,128)(2,1)S(1)} collective-permute-done((bf16[2,128,512]{2,1,0:T(8,128)(2,1)S(1)}, bf16[2,128,512]{2,1,0:T(8,128)(2,1)S(1)}, u32[]{:S(2)}, u32[]{:S(2)}) %collective-permute-start.6) | collective-permute-done | bytes 262176 | tf_op jit(solution)/shard_map/ppermute | solution.py:396
  50.7 0.0 collective-permute-done.7.refs_1_
  50.8 0.6 collective-permute-start.12
  51.4 0.0 collective-permute-done.8.refs_2_
  51.5 0.8 collective-permute-done.9.refs_3_
  52.2 1.2 %merge.5 = (f32[2,128,512]{2,1,0:T(8,128)S(1)}, bf16[2,128,512]{2,1,0:T(8,128)(2,1)S(1)}) custom-call(bf16[576,512]{1,0:T(8,128)(2,1)S(1)} %join.6.unused, bf16[576,512]{1,0:T(8,128)(2,1)S(1)} %get-tuple-element.36.unused.refs_0_, bf16[576,512]{1,0:T(8,128)(2,1)S(1)} %collective-permute-done.1.refs_1_, bf16[576,512]{1,0:T(8,128)(2,1)S(1)} %collective-permute-done.4.refs_2_, ...), custom_call_target="tpu_custom_call" | custom-call | flops 2090000 | bytes 6840 | tf_op jit(solution)/shard_map/merge/pallas_call | solution.py:63
  53.5 1.6 %collective-permute-start.10 = (bf16[2,128,512]{2,1,0:T(8,128)(2,1)S(1)}, bf16[2,128,512]{2,1,0:T(8,128)(2,1)S(1)}, u32[]{:S(2)}, u32[]{:S(2)}) collective-permute-start(bf16[2,128,512]{2,1,0:T(8,128)(2,1)S(1)} %get-tuple-element.46.unused), channel_id=1, source_target_pairs={{0,8},{1,9},{2,10},{3,11},{4,12},{5,13},{6,14},{7,15},{8,0},{9,1},... | collective-permute-start | bytes 786440 | tf_op jit(solution)/shard_map/ppermute | solution.py:396
  55.1 1.5 %collective-permute-start.13 = (bf16[576,512]{1,0:T(8,128)(2,1)S(1)}, bf16[576,512]{1,0:T(8,128)(2,1)S(1)}, u32[]{:S(2)}, u32[]{:S(2)}) collective-permute-start(bf16[576,512]{1,0:T(8,128)(2,1)S(1)} %join.6.unused), channel_id=1, source_target_pairs={{0,4},{1,5},{2,3},{3,2},{4,0},{5,1},{6,7},{7,6},{8,12},{9,13},{10,... | collective-permute-start | bytes 1769480 | tf_op jit(solution)/shard_map/ppermute | solution.py:396
  56.6 2.6 %collective-permute-start.11 = (bf16[1,128,512]{2,1,0:T(8,128)(2,1)S(1)}, bf16[1,128,512]{2,1,0:T(8,128)(2,1)S(1)}, u32[]{:S(2)}, u32[]{:S(2)}) collective-permute-start(bf16[1,128,512]{2,1,0:T(8,128)(2,1)S(1)} %get-tuple-element.43.unused), channel_id=1, source_target_pairs={{0,16},{1,17},{2,18},{3,19},{4,20},{5,21},{6,22},{7,23},{8,24},{9,... | collective-permute-start | bytes 393224 | tf_op jit(solution)/shard_map/ppermute | solution.py:396
  59.2 4.8 %collective-permute-done.10.refs_1_ = bf16[2,128,512]{2,1,0:T(8,128)(2,1)S(1)} collective-permute-done((bf16[2,128,512]{2,1,0:T(8,128)(2,1)S(1)}, bf16[2,128,512]{2,1,0:T(8,128)(2,1)S(1)}, u32[]{:S(2)}, u32[]{:S(2)}) %collective-permute-start.10) | collective-permute-done | bytes 262176 | tf_op jit(solution)/shard_map/ppermute | solution.py:396
  63.9 0.7 halve.5
  64.6 0.0 collective-permute-done.11.refs_1_
  64.7 0.0 collective-permute-done.12.refs_2_
  64.7 0.9 join.7.unused
  65.6 1.4 %collective-permute-start.14 = (bf16[576,512]{1,0:T(8,128)(2,1)}, bf16[576,512]{1,0:T(8,128)(2,1)}, u32[]{:S(2)}, u32[]{:S(2)}) collective-permute-start(bf16[576,512]{1,0:T(8,128)(2,1)} %join.7.unused), channel_id=1, source_target_pairs={{0,4},{1,5},{2,3},{3,2},{4,0},{5,1},{6,7},{7,6},{8,12},{9,13},{10,... | collective-permute-start | bytes 1769480 | tf_op jit(solution)/shard_map/ppermute | solution.py:396
  66.9 0.0 collective-permute-done.13.refs_3_
  66.9 1.9 %merge.6 = (f32[2,128,512]{2,1,0:T(8,128)S(1)}, bf16[2,128,512]{2,1,0:T(8,128)(2,1)}) custom-call(bf16[576,512]{1,0:T(8,128)(2,1)} %join.7.unused, bf16[576,512]{1,0:T(8,128)(2,1)S(1)} %get-tuple-element.38.unused.refs_0_, bf16[576,512]{1,0:T(8,128)(2,1)S(1)} %collective-permute-done.3.refs_1_, bf16[576,512]{1,0:T(8,128)(2,1)S(1)} %collective-permute-done.8.refs_2_, ...), custom_call_target="tpu_custom_call" | custom-call | flops 2090000 | bytes 6840 | tf_op jit(solution)/shard_map/merge/pallas_call | solution.py:63
  68.9 1.9 %collective-permute-start.16 = (bf16[2,128,512]{2,1,0:T(8,128)(2,1)}, bf16[2,128,512]{2,1,0:T(8,128)(2,1)S(1)}, u32[]{:S(2)}, u32[]{:S(2)}) collective-permute-start(bf16[2,128,512]{2,1,0:T(8,128)(2,1)} %get-tuple-element.50.unused), channel_id=1, source_target_pairs={{0,8},{1,9},{2,10},{3,11},{4,12},{5,13},{6,14},{7,15},{8,0},{9,1},... | collective-permute-start | bytes 786440 | tf_op jit(solution)/shard_map/ppermute | solution.py:396
  70.8 0.1 copy.15.refs_6_
  70.8 2.3 %collective-permute-start.15 = (bf16[1,128,512]{2,1,0:T(8,128)(2,1)}, bf16[1,128,512]{2,1,0:T(8,128)(2,1)S(1)}, u32[]{:S(2)}, u32[]{:S(2)}) collective-permute-start(bf16[1,128,512]{2,1,0:T(8,128)(2,1)} %get-tuple-element.48.unused), channel_id=1, source_target_pairs={{0,16},{1,17},{2,18},{3,19},{4,20},{5,21},{6,22},{7,23},{8,24},{9,... | collective-permute-start | bytes 393224 | tf_op jit(solution)/shard_map/ppermute | solution.py:396
  73.1 0.0 copy-start.7
  73.1 0.0 copy-start.8
  73.2 0.0 copy-start.9
  73.2 0.0 copy-start.10
  73.2 2.6 %collective-permute-done.14.refs_3_ = bf16[576,512]{1,0:T(8,128)(2,1)} collective-permute-done((bf16[576,512]{1,0:T(8,128)(2,1)}, bf16[576,512]{1,0:T(8,128)(2,1)}, u32[]{:S(2)}, u32[]{:S(2)}) %collective-permute-start.14) | collective-permute-done | bytes 589856 | tf_op jit(solution)/shard_map/ppermute | solution.py:396
  75.8 2.3 %merge.7 = (f32[2,128,512]{2,1,0:T(8,128)S(1)}, bf16[2,128,512]{2,1,0:T(8,128)(2,1)S(1)}) custom-call(bf16[2,128,512]{2,1,0:T(8,128)(2,1)} %get-tuple-element.50.unused, bf16[576,512]{1,0:T(8,128)(2,1)S(1)} %get-tuple-element.39.unused.refs_0_, bf16[576,512]{1,0:T(8,128)(2,1)S(1)} %collective-permute-done.7.refs_1_, ...), custom_call_target="tpu_custom_call" | custom-call | flops 2090000 | bytes 6840 | tf_op jit(solution)/shard_map/merge/pallas_call | solution.py:63
  78.0 2.7 %collective-permute-start.18 = (bf16[2,128,512]{2,1,0:T(8,128)(2,1)S(1)}, bf16[2,128,512]{2,1,0:T(8,128)(2,1)S(1)}, u32[]{:S(2)}, u32[]{:S(2)}) collective-permute-start(bf16[2,128,512]{2,1,0:T(8,128)(2,1)S(1)} %get-tuple-element.51.unused), channel_id=1, source_target_pairs={{0,8},{1,9},{2,10},{3,11},{4,12},{5,13},{6,14},{7,15},{8,0},{9,1},... | collective-permute-start | bytes 786440 | tf_op jit(solution)/shard_map/ppermute | solution.py:396
  80.8 0.3 collective-permute-done.16.refs_1_
  81.1 2.9 %collective-permute-start.17 = (bf16[1,128,512]{2,1,0:T(8,128)(2,1)S(1)}, bf16[1,128,512]{2,1,0:T(8,128)(2,1)S(1)}, u32[]{:S(2)}, u32[]{:S(2)}) collective-permute-start(bf16[1,128,512]{2,1,0:T(8,128)(2,1)S(1)} %get-tuple-element.54.unused), channel_id=1, source_target_pairs={{0,16},{1,17},{2,18},{3,19},{4,20},{5,21},{6,22},{7,23},{8,24},{9,... | collective-permute-start | bytes 393224 | tf_op jit(solution)/shard_map/ppermute | solution.py:396
  84.1 4.3 %collective-permute-done.17.refs_1_ = bf16[1,128,512]{2,1,0:T(8,128)(2,1)S(1)} collective-permute-done((bf16[1,128,512]{2,1,0:T(8,128)(2,1)S(1)}, bf16[1,128,512]{2,1,0:T(8,128)(2,1)S(1)}, u32[]{:S(2)}, u32[]{:S(2)}) %collective-permute-start.17) | collective-permute-done | bytes 131104 | tf_op jit(solution)/shard_map/ppermute | solution.py:396
  88.4 0.0 collective-permute-done.18.refs_1_
  88.5 0.1 halve.7
  88.6 1.0 collective-permute-start.20
  89.5 3.3 %collective-permute-start.21 = (bf16[1,512]{1,0:T(2,128)(2,1)S(1)}, bf16[1,512]{1,0:T(2,128)(2,1)S(1)}, u32[]{:S(2)}, u32[]{:S(2)}) collective-permute-start(bf16[1,512]{1,0:T(2,128)(2,1)S(1)} %fusion), channel_id=1, source_target_pairs={{0,17},{1,16},{2,19},{3,18},{4,21},{5,20},{6,23},{7,22},{8,25},{9,... | collective-permute-start | bytes 3080 | tf_op jit(solution)/shard_map/ppermute | solution.py:396
  92.8 0.3 collective-permute-start.19
  93.1 2.7 %factor.1.unused.refs_6_ = f32[128,2048]{1,0:T(8,128)S(1)} custom-call(bf16[1,128,512]{2,1,0:T(8,128)(2,1)S(1)} %get-tuple-element.57.unused, s32[128,256]{1,0:T(8,128)S(1)} %bitcast.22, f32[128,256]{1,0:T(8,128)S(1)} %bitcast.23, f32[128,256]{1,0:T(8,128)S(1)} %bitcast.24, f32[128,256]{1,0:T(8,128)S(1)} %bitcast.25, s32[128,256]{1,0:T(8,128)S(1)} %bitcast.26, ...), custom_call_target="tpu_custom_call" | custom-call | flops 3300000 | bytes 10800 | tf_op jit(solution)/shard_map/factor/pallas_call | solution.py:63
  95.9 0.0 collective-permute-done.20
  95.9 4.2 %collective-permute-done.19.refs_1_ = bf16[1,128,512]{2,1,0:T(8,128)(2,1)S(1)} collective-permute-done((bf16[1,128,512]{2,1,0:T(8,128)(2,1)S(1)}, bf16[1,128,512]{2,1,0:T(8,128)(2,1)S(1)}, u32[]{:S(2)}, u32[]{:S(2)}) %collective-permute-start.19) | collective-permute-done | bytes 131104 | tf_op jit(solution)/shard_map/ppermute | solution.py:396
  100.1 1.2 %finish.1 = bf16[128,2048]{1,0:T(8,128)(2,1)} custom-call(f32[128,512]{1,0:T(8,128)S(1)} %total.7.unused.refs_3_, f32[128,512]{1,0:T(8,128)S(1)} %total.4.unused.refs_0_, f32[128,512]{1,0:T(8,128)S(1)} %total.5.unused.refs_1_, f32[128,512]{1,0:T(8,128)S(1)} %total.6.unused.refs_2_, f32[128,512]{1,0:T(8,128)S(1)} %total.7.unused.refs_3_, ...), custom_call_target="tpu_custom_call" | custom-call | flops 1100000 | bytes 3600 | tf_op jit(solution)/shard_map/finish/pallas_call | solution.py:63
  (43 shorter events, 0.6 us)
Async XLA Ops:
  0.0 13.4 %copy-start.3 = (bf16[4,256,256]{2,1,0:T(8,128)(2,1)S(1)}, bf16[4,256,256]{2,1,0:T(8,128)(2,1)}, u32[]{:S(2)}) copy-start(bf16[4,256,256]{2,1,0:T(8,128)(2,1)} %refs_4_.5) | copy-start | bytes 1572868
  0.0 13.4 %copy-start.5 = (f32[2,8,8]{2,1,0:T(8,128)S(1)}, f32[2,8,8]{2,1,0:T(8,128)}, u32[]{:S(2)}) copy-start(f32[2,8,8]{2,1,0:T(8,128)} %refs_0_.5) | copy-start | bytes 1540
  6.9 2.5 %collective-permute-start = (bf16[640,512]{1,0:T(8,128)(2,1)}, bf16[640,512]{1,0:T(8,128)(2,1)S(1)}, u32[]{:S(2)}, u32[]{:S(2)}) collective-permute-start(bf16[640,512]{1,0:T(8,128)(2,1)} %get-tuple-element.33), channel_id=1, source_target_pairs={{0,2},{1,3},{2,0},{3,1},{4,6},{5,7},{6,4},{7,5},{8,10},{9,11},{10,... | collective-permute-start | bytes 1966088 | tf_op jit(solution)/shard_map/ppermute | solution.py:396
  9.3 1.1 %copy-start.1 = (bf16[640,512]{1,0:T(8,128)(2,1)S(1)}, bf16[640,512]{1,0:T(8,128)(2,1)}, u32[]{:S(2)}) copy-start(bf16[640,512]{1,0:T(8,128)(2,1)} %get-tuple-element.32.unused.refs_0_) | copy-start | bytes 1966084
  10.5 12.1 %collective-permute-start.2 = (bf16[640,512]{1,0:T(8,128)(2,1)S(1)}, bf16[640,512]{1,0:T(8,128)(2,1)S(1)}, u32[]{:S(2)}, u32[]{:S(2)}) collective-permute-start(bf16[640,512]{1,0:T(8,128)(2,1)S(1)} %fold.4.unused), channel_id=1, source_target_pairs={{0,1},{1,0},{2,6},{3,7},{4,5},{5,4},{6,2},{7,3},{8,9},{9,8},{10,14... | collective-permute-start | bytes 1966088 | tf_op jit(solution)/shard_map/ppermute | solution.py:396
  13.4 1.9 %copy-start = (bf16[1,1,768,2048]{3,2,1,0:T(8,128)(2,1)S(1)}, bf16[1,1,768,2048]{3,2,1,0:T(8,128)(2,1)}, u32[]{:S(2)}) copy-start(bf16[1,1,768,2048]{3,2,1,0:T(8,128)(2,1)} %param.14) | copy-start | bytes 9437188
  15.3 1.0 copy-start.4
  16.3 0.7 copy-start.11
  17.0 5.6 %copy-start.2 = (bf16[640,512]{1,0:T(8,128)(2,1)S(1)}, bf16[640,512]{1,0:T(8,128)(2,1)}, u32[]{:S(2)}) copy-start(bf16[640,512]{1,0:T(8,128)(2,1)} %get-tuple-element.32.unused.refs_0_) | copy-start | bytes 1966084
  20.4 2.1 %collective-permute-start.1 = (bf16[576,512]{1,0:T(8,128)(2,1)S(1)}, bf16[576,512]{1,0:T(8,128)(2,1)S(1)}, u32[]{:S(2)}, u32[]{:S(2)}) collective-permute-start(bf16[576,512]{1,0:T(8,128)(2,1)S(1)} %get-tuple-element.37), channel_id=1, source_target_pairs={{0,2},{1,3},{2,0},{3,1},{4,6},{5,7},{6,4},{7,5},{8,10},{9,11},{10,... | collective-permute-start | bytes 1769480 | tf_op jit(solution)/shard_map/ppermute | solution.py:396
  22.6 17.8 %collective-permute-start.5 = (bf16[640,512]{1,0:T(8,128)(2,1)S(1)}, bf16[640,512]{1,0:T(8,128)(2,1)S(1)}, u32[]{:S(2)}, u32[]{:S(2)}) collective-permute-start(bf16[640,512]{1,0:T(8,128)(2,1)S(1)} %join.4.unused), channel_id=1, source_target_pairs={{0,4},{1,5},{2,3},{3,2},{4,0},{5,1},{6,7},{7,6},{8,12},{9,13},{10,... | collective-permute-start | bytes 1966088 | tf_op jit(solution)/shard_map/ppermute | solution.py:396
  27.7 5.1 %collective-permute-start.3 = (bf16[576,512]{1,0:T(8,128)(2,1)S(1)}, bf16[576,512]{1,0:T(8,128)(2,1)S(1)}, u32[]{:S(2)}, u32[]{:S(2)}) collective-permute-start(bf16[576,512]{1,0:T(8,128)(2,1)S(1)} %get-tuple-element.40), channel_id=1, source_target_pairs={{0,2},{1,3},{2,0},{3,1},{4,6},{5,7},{6,4},{7,5},{8,10},{9,11},{10,... | collective-permute-start | bytes 1769480 | tf_op jit(solution)/shard_map/ppermute | solution.py:396
  27.7 11.0 %collective-permute-start.4 = (bf16[576,512]{1,0:T(8,128)(2,1)S(1)}, bf16[576,512]{1,0:T(8,128)(2,1)S(1)}, u32[]{:S(2)}, u32[]{:S(2)}) collective-permute-start(bf16[576,512]{1,0:T(8,128)(2,1)S(1)} %fold.5.unused), channel_id=1, source_target_pairs={{0,1},{1,0},{2,6},{3,7},{4,5},{5,4},{6,2},{7,3},{8,9},{9,8},{10,14... | collective-permute-start | bytes 1769480 | tf_op jit(solution)/shard_map/ppermute | solution.py:396
  32.7 18.0 %collective-permute-start.7 = (bf16[576,512]{1,0:T(8,128)(2,1)S(1)}, bf16[576,512]{1,0:T(8,128)(2,1)S(1)}, u32[]{:S(2)}, u32[]{:S(2)}) collective-permute-start(bf16[576,512]{1,0:T(8,128)(2,1)S(1)} %get-tuple-element.44), channel_id=1, source_target_pairs={{0,2},{1,3},{2,0},{3,1},{4,6},{5,7},{6,4},{7,5},{8,10},{9,11},{10,... | collective-permute-start | bytes 1769480 | tf_op jit(solution)/shard_map/ppermute | solution.py:396
  32.8 18.6 %collective-permute-start.8 = (bf16[576,512]{1,0:T(8,128)(2,1)S(1)}, bf16[576,512]{1,0:T(8,128)(2,1)S(1)}, u32[]{:S(2)}, u32[]{:S(2)}) collective-permute-start(bf16[576,512]{1,0:T(8,128)(2,1)S(1)} %fold.6.unused), channel_id=1, source_target_pairs={{0,1},{1,0},{2,6},{3,7},{4,5},{5,4},{6,2},{7,3},{8,9},{9,8},{10,14... | collective-permute-start | bytes 1769480 | tf_op jit(solution)/shard_map/ppermute | solution.py:396
  38.8 13.4 %collective-permute-start.9 = (bf16[576,512]{1,0:T(8,128)(2,1)S(1)}, bf16[576,512]{1,0:T(8,128)(2,1)S(1)}, u32[]{:S(2)}, u32[]{:S(2)}) collective-permute-start(bf16[576,512]{1,0:T(8,128)(2,1)S(1)} %join.5.unused), channel_id=1, source_target_pairs={{0,4},{1,5},{2,3},{3,2},{4,0},{5,1},{6,7},{7,6},{8,12},{9,13},{10,... | collective-permute-start | bytes 1769480 | tf_op jit(solution)/shard_map/ppermute | solution.py:396
  41.8 8.9 %collective-permute-start.6 = (bf16[2,128,512]{2,1,0:T(8,128)(2,1)S(1)}, bf16[2,128,512]{2,1,0:T(8,128)(2,1)S(1)}, u32[]{:S(2)}, u32[]{:S(2)}) collective-permute-start(bf16[2,128,512]{2,1,0:T(8,128)(2,1)S(1)} %get-tuple-element.41.unused), channel_id=1, source_target_pairs={{0,8},{1,9},{2,10},{3,11},{4,12},{5,13},{6,14},{7,15},{8,0},{9,1},... | collective-permute-start | bytes 786440 | tf_op jit(solution)/shard_map/ppermute | solution.py:396
  50.8 13.9 %collective-permute-start.12 = (bf16[576,512]{1,0:T(8,128)(2,1)S(1)}, bf16[576,512]{1,0:T(8,128)(2,1)S(1)}, u32[]{:S(2)}, u32[]{:S(2)}) collective-permute-start(bf16[576,512]{1,0:T(8,128)(2,1)S(1)} %fold.7.unused), channel_id=1, source_target_pairs={{0,1},{1,0},{2,6},{3,7},{4,5},{5,4},{6,2},{7,3},{8,9},{9,8},{10,14... | collective-permute-start | bytes 1769480 | tf_op jit(solution)/shard_map/ppermute | solution.py:396
  53.5 10.5 %collective-permute-start.10 = (bf16[2,128,512]{2,1,0:T(8,128)(2,1)S(1)}, bf16[2,128,512]{2,1,0:T(8,128)(2,1)S(1)}, u32[]{:S(2)}, u32[]{:S(2)}) collective-permute-start(bf16[2,128,512]{2,1,0:T(8,128)(2,1)S(1)} %get-tuple-element.46.unused), channel_id=1, source_target_pairs={{0,8},{1,9},{2,10},{3,11},{4,12},{5,13},{6,14},{7,15},{8,0},{9,1},... | collective-permute-start | bytes 786440 | tf_op jit(solution)/shard_map/ppermute | solution.py:396
  55.1 11.8 %collective-permute-start.13 = (bf16[576,512]{1,0:T(8,128)(2,1)S(1)}, bf16[576,512]{1,0:T(8,128)(2,1)S(1)}, u32[]{:S(2)}, u32[]{:S(2)}) collective-permute-start(bf16[576,512]{1,0:T(8,128)(2,1)S(1)} %join.6.unused), channel_id=1, source_target_pairs={{0,4},{1,5},{2,3},{3,2},{4,0},{5,1},{6,7},{7,6},{8,12},{9,13},{10,... | collective-permute-start | bytes 1769480 | tf_op jit(solution)/shard_map/ppermute | solution.py:396
  56.6 8.1 %collective-permute-start.11 = (bf16[1,128,512]{2,1,0:T(8,128)(2,1)S(1)}, bf16[1,128,512]{2,1,0:T(8,128)(2,1)S(1)}, u32[]{:S(2)}, u32[]{:S(2)}) collective-permute-start(bf16[1,128,512]{2,1,0:T(8,128)(2,1)S(1)} %get-tuple-element.43.unused), channel_id=1, source_target_pairs={{0,16},{1,17},{2,18},{3,19},{4,20},{5,21},{6,22},{7,23},{8,24},{9,... | collective-permute-start | bytes 393224 | tf_op jit(solution)/shard_map/ppermute | solution.py:396
  64.6 6.1 %copy-start.13 = (f32[8,3]{0,1:T(4,128)S(1)}, f32[8,3]{0,1:T(4,128)}, u32[]{:S(2)}) copy-start(f32[8,3]{0,1:T(4,128)} %param.24) | copy-start | bytes 292
  65.6 10.2 %collective-permute-start.14 = (bf16[576,512]{1,0:T(8,128)(2,1)}, bf16[576,512]{1,0:T(8,128)(2,1)}, u32[]{:S(2)}, u32[]{:S(2)}) collective-permute-start(bf16[576,512]{1,0:T(8,128)(2,1)} %join.7.unused), channel_id=1, source_target_pairs={{0,4},{1,5},{2,3},{3,2},{4,0},{5,1},{6,7},{7,6},{8,12},{9,13},{10,... | collective-permute-start | bytes 1769480 | tf_op jit(solution)/shard_map/ppermute | solution.py:396
  68.9 12.2 %collective-permute-start.16 = (bf16[2,128,512]{2,1,0:T(8,128)(2,1)}, bf16[2,128,512]{2,1,0:T(8,128)(2,1)S(1)}, u32[]{:S(2)}, u32[]{:S(2)}) collective-permute-start(bf16[2,128,512]{2,1,0:T(8,128)(2,1)} %get-tuple-element.50.unused), channel_id=1, source_target_pairs={{0,8},{1,9},{2,10},{3,11},{4,12},{5,13},{6,14},{7,15},{8,0},{9,1},... | collective-permute-start | bytes 786440 | tf_op jit(solution)/shard_map/ppermute | solution.py:396
  70.8 9.9 %collective-permute-start.15 = (bf16[1,128,512]{2,1,0:T(8,128)(2,1)}, bf16[1,128,512]{2,1,0:T(8,128)(2,1)S(1)}, u32[]{:S(2)}, u32[]{:S(2)}) collective-permute-start(bf16[1,128,512]{2,1,0:T(8,128)(2,1)} %get-tuple-element.48.unused), channel_id=1, source_target_pairs={{0,16},{1,17},{2,18},{3,19},{4,20},{5,21},{6,22},{7,23},{8,24},{9,... | collective-permute-start | bytes 393224 | tf_op jit(solution)/shard_map/ppermute | solution.py:396
  73.1 19.7 %copy-start.12 = (f32[8,33]{1,0:T(8,128)S(1)}, f32[8,33]{1,0:T(8,128)}, u32[]{:S(2)}) copy-start(f32[8,33]{1,0:T(8,128)} %param.21) | copy-start | bytes 3172
  73.1 20.0 %copy-start.6 = (s32[1,128,256]{2,1,0:T(8,128)S(1)}, s32[1,128,256]{2,1,0:T(8,128)}, u32[]{:S(2)}) copy-start(s32[1,128,256]{2,1,0:T(8,128)} %param.22) | copy-start | bytes 393220
  73.1 20.0 %copy-start.7 = (f32[1,128,256]{2,1,0:T(8,128)S(1)}, f32[1,128,256]{2,1,0:T(8,128)}, u32[]{:S(2)}) copy-start(f32[1,128,256]{2,1,0:T(8,128)} %param.23) | copy-start | bytes 393220
  73.1 20.0 %copy-start.8 = (f32[1,128,256]{2,1,0:T(8,128)S(1)}, f32[1,128,256]{2,1,0:T(8,128)}, u32[]{:S(2)}) copy-start(f32[1,128,256]{2,1,0:T(8,128)} %param.25) | copy-start | bytes 393220
  73.2 20.0 %copy-start.9 = (f32[1,128,256]{2,1,0:T(8,128)S(1)}, f32[1,128,256]{2,1,0:T(8,128)}, u32[]{:S(2)}) copy-start(f32[1,128,256]{2,1,0:T(8,128)} %param.26) | copy-start | bytes 393220
  73.2 20.0 %copy-start.10 = (s32[1,128,256]{2,1,0:T(8,128)S(1)}, s32[1,128,256]{2,1,0:T(8,128)}, u32[]{:S(2)}) copy-start(s32[1,128,256]{2,1,0:T(8,128)} %param.27) | copy-start | bytes 393220
  78.0 10.4 %collective-permute-start.18 = (bf16[2,128,512]{2,1,0:T(8,128)(2,1)S(1)}, bf16[2,128,512]{2,1,0:T(8,128)(2,1)S(1)}, u32[]{:S(2)}, u32[]{:S(2)}) collective-permute-start(bf16[2,128,512]{2,1,0:T(8,128)(2,1)S(1)} %get-tuple-element.51.unused), channel_id=1, source_target_pairs={{0,8},{1,9},{2,10},{3,11},{4,12},{5,13},{6,14},{7,15},{8,0},{9,1},... | collective-permute-start | bytes 786440 | tf_op jit(solution)/shard_map/ppermute | solution.py:396
  81.1 7.3 %collective-permute-start.17 = (bf16[1,128,512]{2,1,0:T(8,128)(2,1)S(1)}, bf16[1,128,512]{2,1,0:T(8,128)(2,1)S(1)}, u32[]{:S(2)}, u32[]{:S(2)}) collective-permute-start(bf16[1,128,512]{2,1,0:T(8,128)(2,1)S(1)} %get-tuple-element.54.unused), channel_id=1, source_target_pairs={{0,16},{1,17},{2,18},{3,19},{4,20},{5,21},{6,22},{7,23},{8,24},{9,... | collective-permute-start | bytes 393224 | tf_op jit(solution)/shard_map/ppermute | solution.py:396
  88.6 7.3 %collective-permute-start.20 = (f32[1,2048]{1,0:T(1,128)S(1)}, f32[1,2048]{1,0:T(1,128)S(1)}, u32[]{:S(2)}, u32[]{:S(2)}) collective-permute-start(f32[1,2048]{1,0:T(1,128)S(1)} %broadcast_select_fusion.2), channel_id=1, source_target_pairs={{0,1},{1,0},{2,3},{3,2},{4,5},{5,4},{6,7},{7,6},{8,9},{9,8},{10,11... | collective-permute-start | bytes 24584 | tf_op jit(solution)/shard_map/ppermute | solution.py:396
  89.5 6.3 %collective-permute-start.21 = (bf16[1,512]{1,0:T(2,128)(2,1)S(1)}, bf16[1,512]{1,0:T(2,128)(2,1)S(1)}, u32[]{:S(2)}, u32[]{:S(2)}) collective-permute-start(bf16[1,512]{1,0:T(2,128)(2,1)S(1)} %fusion), channel_id=1, source_target_pairs={{0,17},{1,16},{2,19},{3,18},{4,21},{5,20},{6,23},{7,22},{8,25},{9,... | collective-permute-start | bytes 3080 | tf_op jit(solution)/shard_map/ppermute | solution.py:396
  92.8 7.3 %collective-permute-start.19 = (bf16[1,128,512]{2,1,0:T(8,128)(2,1)S(1)}, bf16[1,128,512]{2,1,0:T(8,128)(2,1)S(1)}, u32[]{:S(2)}, u32[]{:S(2)}) collective-permute-start(bf16[1,128,512]{2,1,0:T(8,128)(2,1)S(1)} %get-tuple-element.57.unused), channel_id=1, source_target_pairs={{0,16},{1,17},{2,18},{3,19},{4,20},{5,21},{6,22},{7,23},{8,24},{9,... | collective-permute-start | bytes 393224 | tf_op jit(solution)/shard_map/ppermute | solution.py:396
